TPU v7x, 256 devices: a whole 4x4x8 slice. The times are simulated.
256 devices in a mesh: half: 2 (over x_hi), gx: 16 (over z, x_lo), gy: 8 (over y, core).
Axes of the slice: x: 4 (x_hi: 2, x_lo: 2; x = x_hi * 2 + x_lo), y: 4, z: 8, core: 2. Of those that a mesh axis runs over, the one named last changes fastest.
Arguments:
- grid_state: float32 [2, 4, 8, 256, 2048], P('half', None, None, 'gx', 'gy'), may hold values from 0.1 to 1.5
- materials: int32 [2, 8, 256, 2048], P('half', None, 'gx', 'gy'), may hold values from 0 to 3
- contacts: int32 [256, 2048], P('gx', 'gy'), may hold values 0 or 1
- received_sheets: float32 [2, 256, 2048], P('half', 'gx', 'gy'), may hold values from 0 to 2
Outputs:
- final_state: float32 [2, 4, 8, 256, 2048], P('half', None, None, 'gx', 'gy')
- outgoing: float32 [2, 256, 2048], P('half', 'gx', 'gy')
All inputs are finite; a program needn't handle non-finite values. No bound on the sum of `contacts` on one device may be relied on, other than what follows from the above.
Results may differ from a plain program's by a relative error of at most 0.0001.
Values sent between devices are 32-bit elements; how exact they have to be, the bound alone decides.
No kernel may reach another device: no remote copies, remote signals or barrier semaphores. Data moves between devices by JAX's collectives and lax.ppermute only.
A program may use at most 64 MiB of HBM per device.

v0:
```python
import jax
import jax.numpy as jnp
from jax import lax
from jax.sharding import PartitionSpec as P

RELAX = 1
STEPS = 2


OVERSHOOT = 0.8
OMEGA_HEAT = 0.9
POISSON = 0.7
RATE = 0.3
HEATING = 0.05
WARMTH_DIFFUSE = 0.5
DECAY_TIME = 2.0
SPEED_DROP = 0.3
HEAT_GAIN = 0.5
DOPING = (1.5, -1.5, 0.6, -0.6)
MOB_ELEC = (1.0, 0.35, 0.7, 0.5)
MOB_HOLE = (0.4, 0.8, 0.3, 0.6)
CONDUCT = (1.0, 0.15, 2.5, 0.5)
CAPACITY = (0.6, 1.2, 0.4, 0.9)


def swapped(block, axis, bit):
    count = lax.axis_size(axis)
    route = []
    for low in range(count):
        high = low | 1 << bit
        if high != low and high < count:
            route += [(low, high), (high, low)]
    return lax.ppermute(block, axis, route)


def with_halo(cells, sides, width):
    for axis, dim in sides:
        count = lax.axis_size(axis)
        ends = count - 1
        head = lax.slice_in_dim(cells, 0, width, axis=dim)
        tail = lax.slice_in_dim(cells, cells.shape[dim] - width, cells.shape[dim], axis=dim)
        cells = jnp.concatenate(
            [
                lax.ppermute(tail, axis, [(i, (i + 1) % count) for i in range(ends)]),
                cells,
                lax.ppermute(head, axis, [((i + 1) % count, i) for i in range(ends)]),
            ],
            axis=dim,
        )
    return cells


def lookup(material, table):
    summed = jnp.zeros(material.shape, jnp.float32)
    for code_value in range(4):
        summed = summed + jnp.where(material == code_value, table[code_value], 0.0)
    return summed


def layer_faces(layers):
    layer_index = jnp.arange(layers)[:, None, None]
    has_above = (layer_index > 0).astype(jnp.float32)
    has_below = (layer_index < layers - 1).astype(jnp.float32)
    return (layer_index, has_above, has_below)


def semiconductor_pass(
    padded_mesh,
    linearized_pass,
    crystal_warmth,
    impurity_density,
    negative_drift_speed,
    positive_drift_speed,
    locked_flags,
    baseline_solution,
):
    layers = padded_mesh.shape[1]
    layer_index, has_above, has_below = layer_faces(layers)
    middle_cell = padded_mesh[:, :, 1:-1, 1:-1]
    electrostatic_field = middle_cell[0]
    negative_charges = middle_cell[1]
    positive_charge_density = middle_cell[2]
    charge_warmth = middle_cell[3]
    neighbours = [
        (padded_mesh[:, :, :-2, 1:-1], 1.0),
        (padded_mesh[:, :, 2:, 1:-1], 1.0),
        (padded_mesh[:, :, 1:-1, :-2], 1.0),
        (padded_mesh[:, :, 1:-1, 2:], 1.0),
        (jnp.concatenate([middle_cell[:, :1], middle_cell[:, :-1]], axis=1), has_above),
        (jnp.concatenate([middle_cell[:, 1:], middle_cell[:, -1:]], axis=1), has_below),
    ]
    summed_coefficient = 4.0 + has_above + has_below
    if linearized_pass:
        laplace = jnp.zeros_like(electrostatic_field)
        for adjacent_cells, interface_coefficient in neighbours:
            laplace = laplace + interface_coefficient * (adjacent_cells[0] - electrostatic_field)
        equation_mismatch = laplace + POISSON * (
            positive_charge_density - negative_charges + impurity_density
        )
        jacobian_diagonal = summed_coefficient + POISSON * (
            jnp.abs(negative_charges) + jnp.abs(positive_charge_density)
        )
        refreshed_state = jnp.stack(
            [
                electrostatic_field + OVERSHOOT * equation_mismatch / jacobian_diagonal,
                negative_charges,
                positive_charge_density,
                charge_warmth,
            ]
        )
        warming_sheet = jnp.zeros(crystal_warmth.shape, jnp.float32)
    else:
        warming_factor = jnp.exp(-SPEED_DROP * crystal_warmth)[None]
        mobility_elec = negative_drift_speed * warming_factor
        mobility_hole = positive_drift_speed * warming_factor
        flux_elec = jnp.zeros_like(electrostatic_field)
        flux_hole = jnp.zeros_like(electrostatic_field)
        diag_elec = jnp.zeros_like(electrostatic_field)
        diag_hole = jnp.zeros_like(electrostatic_field)
        warmth_curvature = jnp.zeros_like(electrostatic_field)
        dissipated_power = jnp.zeros_like(electrostatic_field)
        for adjacent_cells, interface_coefficient in neighbours:
            drift_term = jnp.tanh(adjacent_cells[0] - electrostatic_field)
            current_elec = (
                adjacent_cells[1]
                - negative_charges
                - 0.5 * (negative_charges + adjacent_cells[1]) * drift_term
            )
            current_hole = (
                adjacent_cells[2]
                - positive_charge_density
                + 0.5 * (positive_charge_density + adjacent_cells[2]) * drift_term
            )
            flux_elec = flux_elec + interface_coefficient * current_elec
            flux_hole = flux_hole + interface_coefficient * current_hole
            diag_elec = diag_elec + interface_coefficient * (1.0 + 0.5 * drift_term)
            diag_hole = diag_hole + interface_coefficient * (1.0 - 0.5 * drift_term)
            warmth_curvature = warmth_curvature + interface_coefficient * (
                adjacent_cells[3] - charge_warmth
            )
            moving_elec = mobility_elec * current_elec
            moving_hole = mobility_hole * current_hole
            dissipated_power = dissipated_power + interface_coefficient * (
                moving_elec * moving_elec + moving_hole * moving_hole
            )
        dissipated_power = HEATING * dissipated_power
        recombine = (
            RATE
            * (negative_charges * positive_charge_density - 1.0)
            / (
                negative_charges * negative_charges
                + positive_charge_density * positive_charge_density
                + 2.0
            )
        )
        next_elec = negative_charges + OVERSHOOT * (mobility_elec * flux_elec - recombine) / (
            mobility_elec * diag_elec
        )
        next_hole = positive_charge_density + OVERSHOOT * (
            mobility_hole * flux_hole - recombine
        ) / (mobility_hole * diag_hole)
        damping_enabled = (charge_warmth - crystal_warmth[None]) / DECAY_TIME
        upcoming_warmth = charge_warmth + OVERSHOOT * (
            WARMTH_DIFFUSE * warmth_curvature + dissipated_power - damping_enabled
        ) / (WARMTH_DIFFUSE * summed_coefficient + 1.0 / DECAY_TIME)
        refreshed_state = jnp.stack([electrostatic_field, next_elec, next_hole, upcoming_warmth])
        warming_sheet = jnp.sum(dissipated_power, axis=0)
    refreshed_state = jnp.where(locked_flags[None] > 0.5, baseline_solution, refreshed_state)
    return (refreshed_state, warming_sheet)


def warming_pass(
    padded_mesh, diffusive_coefficient, specific_warmth, resistive_sheet, baseline_solution
):
    layers = padded_mesh.shape[1]
    layer_index, has_above, has_below = layer_faces(layers)
    on_top = (layer_index == 0).astype(jnp.float32)
    source = HEAT_GAIN * resistive_sheet[None] * on_top
    planes = []
    for subcell in range(4):
        offset_x = subcell // 2
        offset_y = subcell % 2
        middle_cell = padded_mesh[subcell, :, 1:-1, 1:-1]
        across_x = 2 * (1 - offset_x) + offset_y
        across_y = 2 * offset_x + (1 - offset_y)
        if offset_x == 0:
            west_cell = padded_mesh[across_x, :, :-2, 1:-1]
            east_cell = padded_mesh[across_x, :, 1:-1, 1:-1]
        else:
            west_cell = padded_mesh[across_x, :, 1:-1, 1:-1]
            east_cell = padded_mesh[across_x, :, 2:, 1:-1]
        if offset_y == 0:
            south_cell = padded_mesh[across_y, :, 1:-1, :-2]
            north_cell = padded_mesh[across_y, :, 1:-1, 1:-1]
        else:
            south_cell = padded_mesh[across_y, :, 1:-1, 1:-1]
            north_cell = padded_mesh[across_y, :, 1:-1, 2:]
        above_cell = jnp.concatenate([middle_cell[:1], middle_cell[:-1]], axis=0)
        below_cell = jnp.concatenate([middle_cell[1:], jnp.zeros_like(middle_cell[:1])], axis=0)
        laplace = west_cell + east_cell + south_cell + north_cell - 4.0 * middle_cell
        laplace = laplace + has_above * (above_cell - middle_cell) + (below_cell - middle_cell)
        weights = 5.0 + has_above
        change = (
            diffusive_coefficient * laplace
            + source
            - specific_warmth * (middle_cell - baseline_solution[subcell])
        )
        planes.append(
            middle_cell + OMEGA_HEAT * change / (diffusive_coefficient * weights + specific_warmth)
        )
    refreshed_state = jnp.stack(planes)
    return (refreshed_state, 0.25 * jnp.sum(refreshed_state[:, 0], axis=0))


def device_tables(material):
    return (lookup(material, DOPING), lookup(material, MOB_ELEC), lookup(material, MOB_HOLE))


def heat_tables(material):
    return (
        lookup(material, CONDUCT),
        lookup(material, CAPACITY),
        jnp.zeros(material.shape, jnp.float32),
    )


def run_sweep(
    is_device, padded_mesh, linearized_pass, coeffs, sheet_in, locked_flags, baseline_solution
):

    def device_branch(operands):
        grid_part, tables, incoming_sheet, holding, anchor_part = operands
        return semiconductor_pass(
            grid_part,
            linearized_pass,
            incoming_sheet,
            tables[0],
            tables[1],
            tables[2],
            holding,
            anchor_part,
        )

    def heat_branch(operands):
        grid_part, tables, incoming_sheet, holding, anchor_part = operands
        return warming_pass(grid_part, tables[0], tables[1], incoming_sheet, anchor_part)

    return lax.cond(
        is_device,
        device_branch,
        heat_branch,
        (padded_mesh, coeffs, sheet_in, locked_flags, baseline_solution),
    )


def exchange_sheets(produced):
    return swapped(produced, "half", 0)


def per_device(grid_state, materials, contacts, received_sheets):
    fields = grid_state[0]
    own_codes = materials[0]
    sheet_in = received_sheets[0]
    layers = fields.shape[1]
    is_device = lax.axis_index("half") == 0
    layer_index = jnp.arange(layers)[:, None, None]
    locked_flags = jnp.where((layer_index == 0) & (contacts[None] == 1), 1.0, 0.0).astype(
        jnp.float32
    )
    coeffs = lax.cond(is_device, device_tables, heat_tables, own_codes)
    current = fields
    produced = jnp.zeros(sheet_in.shape, jnp.float32)
    for time_step in range(STEPS):
        step_anchor = jnp.where(is_device, fields, current)
        for sweep_counter in range(RELAX + 1):
            padded_mesh = with_halo(current, (("gx", 2), ("gy", 3)), 1)
            current, produced = run_sweep(
                is_device,
                padded_mesh,
                sweep_counter == 0,
                coeffs,
                sheet_in,
                locked_flags,
                step_anchor,
            )
        if time_step + 1 < STEPS:
            sheet_in = exchange_sheets(produced)
    return (current[None], produced[None])


def solution(mesh):
    placed = (
        P("half", None, None, "gx", "gy"),
        P("half", None, "gx", "gy"),
        P("gx", "gy"),
        P("half", "gx", "gy"),
    )
    return jax.shard_map(
        per_device,
        mesh=mesh,
        in_specs=placed,
        out_specs=(P("half", None, None, "gx", "gy"), P("half", "gx", "gy")),
        check_vma=False,
    )
```

profile of v0, /device:TPU:75, one launch (start us, length us, event | category | flops | bytes accessed | tf_op | source)
XLA Modules:
  0.0 102.5 jit_solution(11078652090506113117)
XLA Ops:
  0.6 1.1 %fusion.391 = (f32[4,8,1,256]{3,2,1,0:T(1,128)S(1)}, f32[4,8,1,256]{3,2,1,0:T(1,128)S(1)}) fusion(f32[4,8,16,256]{3,2,1,0:T(8,128)} %bitcast.1644), kind=kLoop, calls=%fused_computation.764 | loop fusion | bytes 131072 | tf_op jit(solution)/shard_map/slice | solution.py:41
  1.7 3.5 %collective-permute-start = (f32[4,8,1,256]{3,2,1,0:T(1,128)S(1)}, f32[4,8,1,256]{3,2,1,0:T(1,128)S(1)}, u32[]{:S(2)}, u32[]{:S(2)}) collective-permute-start(f32[4,8,1,256]{3,2,1,0:T(1,128)S(1)} %get-tuple-element.305), channel_id=1, source_target_pairs={{0,8},{8,16},{16,24},{24,32},{32,40},{40,48},{48,56},{56,64},{64,7... | collective-permute-start | bytes 98312 | tf_op jit(solution)/shard_map/ppermute | solution.py:44
  5.2 1.9 %collective-permute-start.1 = (f32[4,8,1,256]{3,2,1,0:T(1,128)S(1)}, f32[4,8,1,256]{3,2,1,0:T(1,128)S(1)}, u32[]{:S(2)}, u32[]{:S(2)}) collective-permute-start(f32[4,8,1,256]{3,2,1,0:T(1,128)S(1)} %get-tuple-element.306), channel_id=1, source_target_pairs={{8,0},{16,8},{24,16},{32,24},{40,32},{48,40},{56,48},{64,56},{72,6... | collective-permute-start | bytes 98312 | tf_op jit(solution)/shard_map/ppermute | solution.py:46
  7.9 2.9 %collective-permute-done.1 = f32[4,8,1,256]{3,2,1,0:T(1,128)S(1)} collective-permute-done((f32[4,8,1,256]{3,2,1,0:T(1,128)S(1)}, f32[4,8,1,256]{3,2,1,0:T(1,128)S(1)}, u32[]{:S(2)}, u32[]{:S(2)}) %collective-permute-start.1) | collective-permute-done | bytes 32800 | tf_op jit(solution)/shard_map/ppermute | solution.py:46
  10.8 1.2 %pad_maximum_fusion.16 = f32[4,8,18,256]{3,2,1,0:T(8,128)S(1)} fusion(f32[4,8,1,256]{3,2,1,0:T(1,128)S(1)} %collective-permute-done.1, f32[4,8,16,256]{3,2,1,0:T(8,128)} %bitcast.1645, f32[4,8,1,256]{3,2,1,0:T(1,128)S(1)} %collective-permute-done), kind=kLoop, calls=%fused_computation.739 | loop fusion | flops 294912 | bytes 1179648 | tf_op jit(solution)/shard_map/concatenate | solution.py:42
  13.0 5.3 %collective-permute-start.2 = (f32[4,8,18,1]{3,2,1,0:T(8,128)}, f32[4,8,18,1]{3,2,1,0:T(8,128)S(1)}, u32[]{:S(2)}, u32[]{:S(2)}) collective-permute-start(f32[4,8,18,1]{3,2,1,0:T(8,128)} %get-tuple-element.297), channel_id=1, source_target_pairs={{0,1},{1,2},{2,3},{3,4},{4,5},{5,6},{6,7},{8,9},{9,10},{10,11},{11... | collective-permute-start | bytes 6920 | tf_op jit(solution)/shard_map/ppermute | solution.py:44
  18.3 1.9 %collective-permute-start.3 = (f32[4,8,18,1]{3,2,1,0:T(8,128)}, f32[4,8,18,1]{3,2,1,0:T(8,128)S(1)}, u32[]{:S(2)}, u32[]{:S(2)}) collective-permute-start(f32[4,8,18,1]{3,2,1,0:T(8,128)} %get-tuple-element.298), channel_id=1, source_target_pairs={{1,0},{2,1},{3,2},{4,3},{5,4},{6,5},{7,6},{9,8},{10,9},{11,10},{12... | collective-permute-start | bytes 6920 | tf_op jit(solution)/shard_map/ppermute | solution.py:46
  20.6 2.7 %collective-permute-done.2 = f32[4,8,18,1]{3,2,1,0:T(8,128)S(1)} collective-permute-done((f32[4,8,18,1]{3,2,1,0:T(8,128)}, f32[4,8,18,1]{3,2,1,0:T(8,128)S(1)}, u32[]{:S(2)}, u32[]{:S(2)}) %collective-permute-start.2) | collective-permute-done | bytes 2336 | tf_op jit(solution)/shard_map/ppermute | solution.py:44
  23.3 4.3 %collective-permute-done.3 = f32[4,8,18,1]{3,2,1,0:T(8,128)S(1)} collective-permute-done((f32[4,8,18,1]{3,2,1,0:T(8,128)}, f32[4,8,18,1]{3,2,1,0:T(8,128)S(1)}, u32[]{:S(2)}, u32[]{:S(2)}) %collective-permute-start.3) | collective-permute-done | bytes 2336 | tf_op jit(solution)/shard_map/ppermute | solution.py:46
  28.9 3.3 %collective-permute-start.4 = (f32[4,8,1,256]{3,2,1,0:T(1,128)S(1)}, f32[4,8,1,256]{3,2,1,0:T(1,128)S(1)}, u32[]{:S(2)}, u32[]{:S(2)}) collective-permute-start(f32[4,8,1,256]{3,2,1,0:T(1,128)S(1)} %get-tuple-element.303), channel_id=1, source_target_pairs={{0,8},{8,16},{16,24},{24,32},{32,40},{40,48},{48,56},{56,64},{64,7... | collective-permute-start | bytes 98312 | tf_op jit(solution)/shard_map/ppermute | solution.py:44
  32.2 2.0 %collective-permute-start.5 = (f32[4,8,1,256]{3,2,1,0:T(1,128)S(1)}, f32[4,8,1,256]{3,2,1,0:T(1,128)S(1)}, u32[]{:S(2)}, u32[]{:S(2)}) collective-permute-start(f32[4,8,1,256]{3,2,1,0:T(1,128)S(1)} %get-tuple-element.304), channel_id=1, source_target_pairs={{8,0},{16,8},{24,16},{32,24},{40,32},{48,40},{56,48},{64,56},{72,6... | collective-permute-start | bytes 98312 | tf_op jit(solution)/shard_map/ppermute | solution.py:46
  34.2 5.1 %collective-permute-done.5 = f32[4,8,1,256]{3,2,1,0:T(1,128)S(1)} collective-permute-done((f32[4,8,1,256]{3,2,1,0:T(1,128)S(1)}, f32[4,8,1,256]{3,2,1,0:T(1,128)S(1)}, u32[]{:S(2)}, u32[]{:S(2)}) %collective-permute-start.5) | collective-permute-done | bytes 32800 | tf_op jit(solution)/shard_map/ppermute | solution.py:46
  39.6 3.0 %collective-permute-start.6 = (f32[4,8,18,1]{3,2,1,0:T(8,128)S(1)}, f32[4,8,18,1]{3,2,1,0:T(8,128)S(1)}, u32[]{:S(2)}, u32[]{:S(2)}) collective-permute-start(f32[4,8,18,1]{3,2,1,0:T(8,128)S(1)} %get-tuple-element.295), channel_id=1, source_target_pairs={{0,1},{1,2},{2,3},{3,4},{4,5},{5,6},{6,7},{8,9},{9,10},{10,11},{11... | collective-permute-start | bytes 6920 | tf_op jit(solution)/shard_map/ppermute | solution.py:44
  42.6 1.9 %collective-permute-start.7 = (f32[4,8,18,1]{3,2,1,0:T(8,128)S(1)}, f32[4,8,18,1]{3,2,1,0:T(8,128)S(1)}, u32[]{:S(2)}, u32[]{:S(2)}) collective-permute-start(f32[4,8,18,1]{3,2,1,0:T(8,128)S(1)} %get-tuple-element.296), channel_id=1, source_target_pairs={{1,0},{2,1},{3,2},{4,3},{5,4},{6,5},{7,6},{9,8},{10,9},{11,10},{12... | collective-permute-start | bytes 6920 | tf_op jit(solution)/shard_map/ppermute | solution.py:46
  44.5 2.8 %collective-permute-done.6 = f32[4,8,18,1]{3,2,1,0:T(8,128)S(1)} collective-permute-done((f32[4,8,18,1]{3,2,1,0:T(8,128)S(1)}, f32[4,8,18,1]{3,2,1,0:T(8,128)S(1)}, u32[]{:S(2)}, u32[]{:S(2)}) %collective-permute-start.6) | collective-permute-done | bytes 2336 | tf_op jit(solution)/shard_map/ppermute | solution.py:44
  47.3 4.4 %collective-permute-done.7 = f32[4,8,18,1]{3,2,1,0:T(8,128)S(1)} collective-permute-done((f32[4,8,18,1]{3,2,1,0:T(8,128)S(1)}, f32[4,8,18,1]{3,2,1,0:T(8,128)S(1)}, u32[]{:S(2)}, u32[]{:S(2)}) %collective-permute-start.7) | collective-permute-done | bytes 2336 | tf_op jit(solution)/shard_map/ppermute | solution.py:46
  52.4 2.0 %conditional.7 = (f32[4,8,16,256]{3,2,1,0:T(8,128)S(1)}, f32[16,256]{1,0:T(8,128)S(1)}) conditional(s32[]{:T(128)} %convert_element_type.259, (f32[4,8,16,256]{3,2,1,0:T(8,128)S(1)}, f32[4,8,18,256]{3,2,1,0:T(8,128)S(1)}, f32[4,8,18,258]{3,2,1,0:T(8,128)S(1)}, f32[8,16,256]{2,1,0:T(8,128)S(1)}, f32[1,16,256]{2,1,0:T(8,128)S(1)}, ...), branch_computations={%region_4.6_spmd, %region_6.8_spmd} | conditional | flops 10059872 | bytes 15909264 | solution.py:248
  54.5 3.8 %collective-permute-start.8 = (f32[4,8,1,256]{3,2,1,0:T(1,128)S(1)}, f32[4,8,1,256]{3,2,1,0:T(1,128)S(1)}, u32[]{:S(2)}, u32[]{:S(2)}) collective-permute-start(f32[4,8,1,256]{3,2,1,0:T(1,128)S(1)} %get-tuple-element.301), channel_id=1, source_target_pairs={{0,8},{8,16},{16,24},{24,32},{32,40},{40,48},{48,56},{56,64},{64,7... | collective-permute-start | bytes 98312 | tf_op jit(solution)/shard_map/ppermute | solution.py:44
  58.3 1.9 %collective-permute-start.9 = (f32[4,8,1,256]{3,2,1,0:T(1,128)S(1)}, f32[4,8,1,256]{3,2,1,0:T(1,128)S(1)}, u32[]{:S(2)}, u32[]{:S(2)}) collective-permute-start(f32[4,8,1,256]{3,2,1,0:T(1,128)S(1)} %get-tuple-element.302), channel_id=1, source_target_pairs={{8,0},{16,8},{24,16},{32,24},{40,32},{48,40},{56,48},{64,56},{72,6... | collective-permute-start | bytes 98312 | tf_op jit(solution)/shard_map/ppermute | solution.py:46
  60.3 3.6 %collective-permute-done.9 = f32[4,8,1,256]{3,2,1,0:T(1,128)S(1)} collective-permute-done((f32[4,8,1,256]{3,2,1,0:T(1,128)S(1)}, f32[4,8,1,256]{3,2,1,0:T(1,128)S(1)}, u32[]{:S(2)}, u32[]{:S(2)}) %collective-permute-start.9) | collective-permute-done | bytes 32800 | tf_op jit(solution)/shard_map/ppermute | solution.py:46
  64.2 3.4 %collective-permute-start.10 = (f32[4,8,18,1]{3,2,1,0:T(8,128)S(1)}, f32[4,8,18,1]{3,2,1,0:T(8,128)S(1)}, u32[]{:S(2)}, u32[]{:S(2)}) collective-permute-start(f32[4,8,18,1]{3,2,1,0:T(8,128)S(1)} %get-tuple-element.293), channel_id=1, source_target_pairs={{0,1},{1,2},{2,3},{3,4},{4,5},{5,6},{6,7},{8,9},{9,10},{10,11},{11... | collective-permute-start | bytes 6920 | tf_op jit(solution)/shard_map/ppermute | solution.py:44
  67.5 1.9 %collective-permute-start.11 = (f32[4,8,18,1]{3,2,1,0:T(8,128)S(1)}, f32[4,8,18,1]{3,2,1,0:T(8,128)S(1)}, u32[]{:S(2)}, u32[]{:S(2)}) collective-permute-start(f32[4,8,18,1]{3,2,1,0:T(8,128)S(1)} %get-tuple-element.294), channel_id=1, source_target_pairs={{1,0},{2,1},{3,2},{4,3},{5,4},{6,5},{7,6},{9,8},{10,9},{11,10},{12... | collective-permute-start | bytes 6920 | tf_op jit(solution)/shard_map/ppermute | solution.py:46
  69.5 1.6 %collective-permute-start.12 = (f32[16,256]{1,0:T(8,128)S(1)}, f32[16,256]{1,0:T(8,128)S(1)}, u32[]{:S(2)}, u32[]{:S(2)}) collective-permute-start(f32[16,256]{1,0:T(8,128)S(1)} %get-tuple-element.188), channel_id=1, source_target_pairs={{0,128},{128,0},{1,129},{129,1},{2,130},{130,2},{3,131},{131,3},{4... | collective-permute-start | bytes 49160 | tf_op jit(solution)/shard_map/ppermute | solution.py:33
  72.2 4.4 %collective-permute-done.11 = f32[4,8,18,1]{3,2,1,0:T(8,128)S(1)} collective-permute-done((f32[4,8,18,1]{3,2,1,0:T(8,128)S(1)}, f32[4,8,18,1]{3,2,1,0:T(8,128)S(1)}, u32[]{:S(2)}, u32[]{:S(2)}) %collective-permute-start.11) | collective-permute-done | bytes 2336 | tf_op jit(solution)/shard_map/ppermute | solution.py:46
  78.0 2.6 %collective-permute-start.13 = (f32[4,8,1,256]{3,2,1,0:T(1,128)S(1)}, f32[4,8,1,256]{3,2,1,0:T(1,128)S(1)}, u32[]{:S(2)}, u32[]{:S(2)}) collective-permute-start(f32[4,8,1,256]{3,2,1,0:T(1,128)S(1)} %get-tuple-element.299), channel_id=1, source_target_pairs={{0,8},{8,16},{16,24},{24,32},{32,40},{40,48},{48,56},{56,64},{64,7... | collective-permute-start | bytes 98312 | tf_op jit(solution)/shard_map/ppermute | solution.py:44
  80.5 2.7 %collective-permute-start.14 = (f32[4,8,1,256]{3,2,1,0:T(1,128)S(1)}, f32[4,8,1,256]{3,2,1,0:T(1,128)S(1)}, u32[]{:S(2)}, u32[]{:S(2)}) collective-permute-start(f32[4,8,1,256]{3,2,1,0:T(1,128)S(1)} %get-tuple-element.300), channel_id=1, source_target_pairs={{8,0},{16,8},{24,16},{32,24},{40,32},{48,40},{56,48},{64,56},{72,6... | collective-permute-start | bytes 98312 | tf_op jit(solution)/shard_map/ppermute | solution.py:46
  83.3 2.8 %collective-permute-done.14 = f32[4,8,1,256]{3,2,1,0:T(1,128)S(1)} collective-permute-done((f32[4,8,1,256]{3,2,1,0:T(1,128)S(1)}, f32[4,8,1,256]{3,2,1,0:T(1,128)S(1)}, u32[]{:S(2)}, u32[]{:S(2)}) %collective-permute-start.14) | collective-permute-done | bytes 32800 | tf_op jit(solution)/shard_map/ppermute | solution.py:46
  86.4 3.3 %collective-permute-start.15 = (f32[4,8,18,1]{3,2,1,0:T(8,128)S(1)}, f32[4,8,18,1]{3,2,1,0:T(8,128)S(1)}, u32[]{:S(2)}, u32[]{:S(2)}) collective-permute-start(f32[4,8,18,1]{3,2,1,0:T(8,128)S(1)} %get-tuple-element.291), channel_id=1, source_target_pairs={{0,1},{1,2},{2,3},{3,4},{4,5},{5,6},{6,7},{8,9},{9,10},{10,11},{11... | collective-permute-start | bytes 6920 | tf_op jit(solution)/shard_map/ppermute | solution.py:44
  89.7 2.2 %collective-permute-start.16 = (f32[4,8,18,1]{3,2,1,0:T(8,128)S(1)}, f32[4,8,18,1]{3,2,1,0:T(8,128)S(1)}, u32[]{:S(2)}, u32[]{:S(2)}) collective-permute-start(f32[4,8,18,1]{3,2,1,0:T(8,128)S(1)} %get-tuple-element.292), channel_id=1, source_target_pairs={{1,0},{2,1},{3,2},{4,3},{5,4},{6,5},{7,6},{9,8},{10,9},{11,10},{12... | collective-permute-start | bytes 6920 | tf_op jit(solution)/shard_map/ppermute | solution.py:46
  91.9 2.4 %collective-permute-done.15 = f32[4,8,18,1]{3,2,1,0:T(8,128)S(1)} collective-permute-done((f32[4,8,18,1]{3,2,1,0:T(8,128)S(1)}, f32[4,8,18,1]{3,2,1,0:T(8,128)S(1)}, u32[]{:S(2)}, u32[]{:S(2)}) %collective-permute-start.15) | collective-permute-done | bytes 2336 | tf_op jit(solution)/shard_map/ppermute | solution.py:44
  94.4 4.5 %collective-permute-done.16 = f32[4,8,18,1]{3,2,1,0:T(8,128)S(1)} collective-permute-done((f32[4,8,18,1]{3,2,1,0:T(8,128)S(1)}, f32[4,8,18,1]{3,2,1,0:T(8,128)S(1)}, u32[]{:S(2)}, u32[]{:S(2)}) %collective-permute-start.16) | collective-permute-done | bytes 2336 | tf_op jit(solution)/shard_map/ppermute | solution.py:46
  99.7 2.0 %conditional.9 = (f32[4,8,16,256]{3,2,1,0:T(8,128)S(1)}, f32[1,16,256]{2,1,0:T(8,128)S(1)}) conditional(s32[]{:T(128)} %convert_element_type.259, (f32[4,8,16,256]{3,2,1,0:T(8,128)S(1)}, f32[4,8,18,256]{3,2,1,0:T(8,128)S(1)}, f32[4,8,18,258]{3,2,1,0:T(8,128)S(1)}, f32[8,16,256]{2,1,0:T(8,128)S(1)}, f32[16,256]{1,0:T(8,128)S(1)}, ...), branch_computations={%region_10.12_spmd, %region_12.14_spmd} | conditional | flops 10059872 | bytes 15909264 | solution.py:248
  (87 shorter events, 14.0 us)
Async XLA Ops:
  1.7 6.2 %collective-permute-start = (f32[4,8,1,256]{3,2,1,0:T(1,128)S(1)}, f32[4,8,1,256]{3,2,1,0:T(1,128)S(1)}, u32[]{:S(2)}, u32[]{:S(2)}) collective-permute-start(f32[4,8,1,256]{3,2,1,0:T(1,128)S(1)} %get-tuple-element.305), channel_id=1, source_target_pairs={{0,8},{8,16},{16,24},{24,32},{32,40},{40,48},{48,56},{56,64},{64,7... | collective-permute-start | bytes 98312 | tf_op jit(solution)/shard_map/ppermute | solution.py:44
  5.2 5.6 %collective-permute-start.1 = (f32[4,8,1,256]{3,2,1,0:T(1,128)S(1)}, f32[4,8,1,256]{3,2,1,0:T(1,128)S(1)}, u32[]{:S(2)}, u32[]{:S(2)}) collective-permute-start(f32[4,8,1,256]{3,2,1,0:T(1,128)S(1)} %get-tuple-element.306), channel_id=1, source_target_pairs={{8,0},{16,8},{24,16},{32,24},{40,32},{48,40},{56,48},{64,56},{72,6... | collective-permute-start | bytes 98312 | tf_op jit(solution)/shard_map/ppermute | solution.py:46
  12.0 8.4 %copy-start.6 = (s32[1,8,16,256]{3,2,1,0:T(8,128)S(1)}, s32[1,8,16,256]{3,2,1,0:T(8,128)}, u32[]{:S(2)}) copy-start(s32[1,8,16,256]{3,2,1,0:T(8,128)} %param.15) | copy-start | bytes 393220
  13.0 14.6 %copy-start = (f32[1,4,8,16,256]{4,3,2,1,0:T(8,128)S(1)}, f32[1,4,8,16,256]{4,3,2,1,0:T(8,128)}, u32[]{:S(2)}) copy-start(f32[1,4,8,16,256]{4,3,2,1,0:T(8,128)} %param.14) | copy-start | bytes 1572868
  13.0 10.3 %collective-permute-start.2 = (f32[4,8,18,1]{3,2,1,0:T(8,128)}, f32[4,8,18,1]{3,2,1,0:T(8,128)S(1)}, u32[]{:S(2)}, u32[]{:S(2)}) collective-permute-start(f32[4,8,18,1]{3,2,1,0:T(8,128)} %get-tuple-element.297), channel_id=1, source_target_pairs={{0,1},{1,2},{2,3},{3,4},{4,5},{5,6},{6,7},{8,9},{9,10},{10,11},{11... | collective-permute-start | bytes 6920 | tf_op jit(solution)/shard_map/ppermute | solution.py:44
  18.3 9.3 %collective-permute-start.3 = (f32[4,8,18,1]{3,2,1,0:T(8,128)}, f32[4,8,18,1]{3,2,1,0:T(8,128)S(1)}, u32[]{:S(2)}, u32[]{:S(2)}) collective-permute-start(f32[4,8,18,1]{3,2,1,0:T(8,128)} %get-tuple-element.298), channel_id=1, source_target_pairs={{1,0},{2,1},{3,2},{4,3},{5,4},{6,5},{7,6},{9,8},{10,9},{11,10},{12... | collective-permute-start | bytes 6920 | tf_op jit(solution)/shard_map/ppermute | solution.py:46
  20.3 57.1 %copy-start.3 = (f32[8,16,256]{2,1,0:T(8,128)}, f32[8,16,256]{2,1,0:T(8,128)S(1)}, u32[]{:S(2)}) copy-start(f32[8,16,256]{2,1,0:T(8,128)S(1)} %and_select_fusion) | copy-start | bytes 393220
  20.6 31.8 %copy-start.1 = (f32[8,16,256]{2,1,0:T(8,128)}, f32[8,16,256]{2,1,0:T(8,128)S(1)}, u32[]{:S(2)}) copy-start(f32[8,16,256]{2,1,0:T(8,128)S(1)} %get-tuple-element.186) | copy-start | bytes 393220
  20.6 7.7 %copy-start.7 = (f32[1,16,256]{2,1,0:T(8,128)S(1)}, f32[1,16,256]{2,1,0:T(8,128)}, u32[]{:S(2)}) copy-start(f32[1,16,256]{2,1,0:T(8,128)} %param.17) | copy-start | bytes 49156
  28.9 5.3 %collective-permute-start.4 = (f32[4,8,1,256]{3,2,1,0:T(1,128)S(1)}, f32[4,8,1,256]{3,2,1,0:T(1,128)S(1)}, u32[]{:S(2)}, u32[]{:S(2)}) collective-permute-start(f32[4,8,1,256]{3,2,1,0:T(1,128)S(1)} %get-tuple-element.303), channel_id=1, source_target_pairs={{0,8},{8,16},{16,24},{24,32},{32,40},{40,48},{48,56},{56,64},{64,7... | collective-permute-start | bytes 98312 | tf_op jit(solution)/shard_map/ppermute | solution.py:44
  32.2 7.0 %collective-permute-start.5 = (f32[4,8,1,256]{3,2,1,0:T(1,128)S(1)}, f32[4,8,1,256]{3,2,1,0:T(1,128)S(1)}, u32[]{:S(2)}, u32[]{:S(2)}) collective-permute-start(f32[4,8,1,256]{3,2,1,0:T(1,128)S(1)} %get-tuple-element.304), channel_id=1, source_target_pairs={{8,0},{16,8},{24,16},{32,24},{40,32},{48,40},{56,48},{64,56},{72,6... | collective-permute-start | bytes 98312 | tf_op jit(solution)/shard_map/ppermute | solution.py:46
  39.6 7.7 %collective-permute-start.6 = (f32[4,8,18,1]{3,2,1,0:T(8,128)S(1)}, f32[4,8,18,1]{3,2,1,0:T(8,128)S(1)}, u32[]{:S(2)}, u32[]{:S(2)}) collective-permute-start(f32[4,8,18,1]{3,2,1,0:T(8,128)S(1)} %get-tuple-element.295), channel_id=1, source_target_pairs={{0,1},{1,2},{2,3},{3,4},{4,5},{5,6},{6,7},{8,9},{9,10},{10,11},{11... | collective-permute-start | bytes 6920 | tf_op jit(solution)/shard_map/ppermute | solution.py:44
  42.6 9.1 %collective-permute-start.7 = (f32[4,8,18,1]{3,2,1,0:T(8,128)S(1)}, f32[4,8,18,1]{3,2,1,0:T(8,128)S(1)}, u32[]{:S(2)}, u32[]{:S(2)}) collective-permute-start(f32[4,8,18,1]{3,2,1,0:T(8,128)S(1)} %get-tuple-element.296), channel_id=1, source_target_pairs={{1,0},{2,1},{3,2},{4,3},{5,4},{6,5},{7,6},{9,8},{10,9},{11,10},{12... | collective-permute-start | bytes 6920 | tf_op jit(solution)/shard_map/ppermute | solution.py:46
  54.5 5.7 %collective-permute-start.8 = (f32[4,8,1,256]{3,2,1,0:T(1,128)S(1)}, f32[4,8,1,256]{3,2,1,0:T(1,128)S(1)}, u32[]{:S(2)}, u32[]{:S(2)}) collective-permute-start(f32[4,8,1,256]{3,2,1,0:T(1,128)S(1)} %get-tuple-element.301), channel_id=1, source_target_pairs={{0,8},{8,16},{16,24},{24,32},{32,40},{40,48},{48,56},{56,64},{64,7... | collective-permute-start | bytes 98312 | tf_op jit(solution)/shard_map/ppermute | solution.py:44
  58.3 5.6 %collective-permute-start.9 = (f32[4,8,1,256]{3,2,1,0:T(1,128)S(1)}, f32[4,8,1,256]{3,2,1,0:T(1,128)S(1)}, u32[]{:S(2)}, u32[]{:S(2)}) collective-permute-start(f32[4,8,1,256]{3,2,1,0:T(1,128)S(1)} %get-tuple-element.302), channel_id=1, source_target_pairs={{8,0},{16,8},{24,16},{32,24},{40,32},{48,40},{56,48},{64,56},{72,6... | collective-permute-start | bytes 98312 | tf_op jit(solution)/shard_map/ppermute | solution.py:46
  64.2 8.1 %collective-permute-start.10 = (f32[4,8,18,1]{3,2,1,0:T(8,128)S(1)}, f32[4,8,18,1]{3,2,1,0:T(8,128)S(1)}, u32[]{:S(2)}, u32[]{:S(2)}) collective-permute-start(f32[4,8,18,1]{3,2,1,0:T(8,128)S(1)} %get-tuple-element.293), channel_id=1, source_target_pairs={{0,1},{1,2},{2,3},{3,4},{4,5},{5,6},{6,7},{8,9},{9,10},{10,11},{11... | collective-permute-start | bytes 6920 | tf_op jit(solution)/shard_map/ppermute | solution.py:44
  67.5 9.1 %collective-permute-start.11 = (f32[4,8,18,1]{3,2,1,0:T(8,128)S(1)}, f32[4,8,18,1]{3,2,1,0:T(8,128)S(1)}, u32[]{:S(2)}, u32[]{:S(2)}) collective-permute-start(f32[4,8,18,1]{3,2,1,0:T(8,128)S(1)} %get-tuple-element.294), channel_id=1, source_target_pairs={{1,0},{2,1},{3,2},{4,3},{5,4},{6,5},{7,6},{9,8},{10,9},{11,10},{12... | collective-permute-start | bytes 6920 | tf_op jit(solution)/shard_map/ppermute | solution.py:46
  69.5 7.8 %collective-permute-start.12 = (f32[16,256]{1,0:T(8,128)S(1)}, f32[16,256]{1,0:T(8,128)S(1)}, u32[]{:S(2)}, u32[]{:S(2)}) collective-permute-start(f32[16,256]{1,0:T(8,128)S(1)} %get-tuple-element.188), channel_id=1, source_target_pairs={{0,128},{128,0},{1,129},{129,1},{2,130},{130,2},{3,131},{131,3},{4... | collective-permute-start | bytes 49160 | tf_op jit(solution)/shard_map/ppermute | solution.py:33
  78.0 5.3 %collective-permute-start.13 = (f32[4,8,1,256]{3,2,1,0:T(1,128)S(1)}, f32[4,8,1,256]{3,2,1,0:T(1,128)S(1)}, u32[]{:S(2)}, u32[]{:S(2)}) collective-permute-start(f32[4,8,1,256]{3,2,1,0:T(1,128)S(1)} %get-tuple-element.299), channel_id=1, source_target_pairs={{0,8},{8,16},{16,24},{24,32},{32,40},{40,48},{48,56},{56,64},{64,7... | collective-permute-start | bytes 98312 | tf_op jit(solution)/shard_map/ppermute | solution.py:44
  80.5 5.6 %collective-permute-start.14 = (f32[4,8,1,256]{3,2,1,0:T(1,128)S(1)}, f32[4,8,1,256]{3,2,1,0:T(1,128)S(1)}, u32[]{:S(2)}, u32[]{:S(2)}) collective-permute-start(f32[4,8,1,256]{3,2,1,0:T(1,128)S(1)} %get-tuple-element.300), channel_id=1, source_target_pairs={{8,0},{16,8},{24,16},{32,24},{40,32},{48,40},{56,48},{64,56},{72,6... | collective-permute-start | bytes 98312 | tf_op jit(solution)/shard_map/ppermute | solution.py:46
  86.4 8.0 %collective-permute-start.15 = (f32[4,8,18,1]{3,2,1,0:T(8,128)S(1)}, f32[4,8,18,1]{3,2,1,0:T(8,128)S(1)}, u32[]{:S(2)}, u32[]{:S(2)}) collective-permute-start(f32[4,8,18,1]{3,2,1,0:T(8,128)S(1)} %get-tuple-element.291), channel_id=1, source_target_pairs={{0,1},{1,2},{2,3},{3,4},{4,5},{5,6},{6,7},{8,9},{9,10},{10,11},{11... | collective-permute-start | bytes 6920 | tf_op jit(solution)/shard_map/ppermute | solution.py:44
  89.7 10.0 %copy-start.2 = (f32[8,16,256]{2,1,0:T(8,128)S(1)}, f32[8,16,256]{2,1,0:T(8,128)}, u32[]{:S(2)}) copy-start(f32[8,16,256]{2,1,0:T(8,128)} %copy-done.1) | copy-start | bytes 393220
  89.7 10.0 %copy-start.4 = (f32[8,16,256]{2,1,0:T(8,128)S(1)}, f32[8,16,256]{2,1,0:T(8,128)}, u32[]{:S(2)}) copy-start(f32[8,16,256]{2,1,0:T(8,128)} %copy-done.3) | copy-start | bytes 393220
  89.7 9.2 %collective-permute-start.16 = (f32[4,8,18,1]{3,2,1,0:T(8,128)S(1)}, f32[4,8,18,1]{3,2,1,0:T(8,128)S(1)}, u32[]{:S(2)}, u32[]{:S(2)}) collective-permute-start(f32[4,8,18,1]{3,2,1,0:T(8,128)S(1)} %get-tuple-element.292), channel_id=1, source_target_pairs={{1,0},{2,1},{3,2},{4,3},{5,4},{6,5},{7,6},{9,8},{10,9},{11,10},{12... | collective-permute-start | bytes 6920 | tf_op jit(solution)/shard_map/ppermute | solution.py:46
  101.7 0.8 copy-start.5
  101.7 0.8 copy-start.8
where the time goes:
time: 103 us
  starting transfers between devices  46.3 us (45%)
  waiting for transfers between devices  41 us (40%)
  other arithmetic  9.83 us (10%)
  local copies, waits for them, and re-layouts  4.04 us (4%)
  between operations  1.04 us (1%)
    ppermute x8, waiting for transfers between devices, with_halo(): lax.ppermute(head, axis, [((i + 1) % count, i) for i in range(ends)])  32 us
    ppermute x8, starting transfers between devices, with_halo(): lax.ppermute(tail, axis, [(i, (i + 1) % count) for i in range(ends)])  28.1 us
    ppermute x8, starting transfers between devices, with_halo(): lax.ppermute(head, axis, [((i + 1) % count, i) for i in range(ends)])  16.5 us
    ppermute x8, waiting for transfers between devices, with_halo(): lax.ppermute(tail, axis, [(i, (i + 1) % count) for i in range(ends)])  8.97 us
    concatenate x8, other arithmetic, with_halo(): jnp.concatenate([lax.ppermute(tail, axis, [(i, (i + 1) % count) for i in...  4.4 us
    slice x8, local copies, waits for them, and re-layouts, with_halo(): lax.slice_in_dim(cells, cells.shape[dim] - width, cells.shape[dim], axis=...  2.72 us
    another operation x6, other arithmetic, semiconductor_pass(): jnp.stack([electrostatic_field, next_elec, next_hole, upcoming_warmth])  2.16 us
  transfers between devices with their start and end apart: 17, of which 12 were waited for; matrix products, arithmetic and copies ran while one was open for 2% of the time, Pallas kernels for 0%

commit v1 on v0

v1 whole, which is shorter than its diff:
```python
import jax
import jax.numpy as jnp
from jax import lax
from jax.experimental import pallas as pl
from jax.experimental.pallas import tpu as pltpu
from jax.sharding import PartitionSpec as P

F32 = jnp.float32
LAYERS = 8
TX = 16
LANES = 128
TILES = 3
HALO = 3
ROWS = TX + 2 * HALO
FIRST = HALO

DOPING = (1.5, -1.5, 0.6, -0.6)
MOB_ELEC = (1.0, 0.35, 0.7, 0.5)
MOB_HOLE = (0.4, 0.8, 0.3, 0.6)
CONDUCT = (1.0, 0.15, 2.5, 0.5)
CAPACITY = (0.6, 1.2, 0.4, 0.9)
INV_ELEC = tuple(1.0 / m for m in MOB_ELEC)
INV_HOLE = tuple(1.0 / m for m in MOB_HOLE)
SPREAD_TOP = tuple(0.9 * k / (5.0 * k + c) for k, c in zip(CONDUCT, CAPACITY))
SPREAD_IN = tuple(0.9 * k / (6.0 * k + c) for k, c in zip(CONDUCT, CAPACITY))
KEEP_TOP = tuple(0.9 * c / (5.0 * k + c) for k, c in zip(CONDUCT, CAPACITY))
KEEP_IN = tuple(0.9 * c / (6.0 * k + c) for k, c in zip(CONDUCT, CAPACITY))
SOURCE_TOP = tuple(0.45 / (5.0 * k + c) for k, c in zip(CONDUCT, CAPACITY))

CODE, SHEET = 4, 5
WIDTH = (3, 2, 2, 2, 2, 2)
SLOT = (0, 3, 5, 7, 9, 11)
LOW = [(f, r) for f in range(6) for r in range(WIDTH[f])]
HIGH = [(f, TX - WIDTH[f] + r) for f in range(6) for r in range(WIDTH[f])]
ITEMS = len(LOW)
VMEM = pl.BlockSpec(memory_space=pltpu.VMEM)
HBM = pl.BlockSpec(memory_space=pltpu.HBM)
SHEET_SHAPE = (24, TILES * LANES)


def call(kernel, outs, ins, specs=None, out_specs=None, scratch=(), aliases=None, flops=0):
    return pl.pallas_call(
        kernel,
        out_shape=[jax.ShapeDtypeStruct(s, F32) for s in outs],
        in_specs=specs or [VMEM] * len(ins),
        out_specs=out_specs or [VMEM] * len(outs),
        scratch_shapes=list(scratch),
        input_output_aliases=aliases or {},
        compiler_params=pltpu.CompilerParams(vmem_limit_bytes=12 << 20),
        cost_estimate=pl.CostEstimate(flops=flops, bytes_accessed=1 << 20, transcendentals=0),
    )(*ins)


def lane_index():
    return lax.broadcasted_iota(jnp.int32, (LAYERS, LANES), 1)


def layer_index(width):
    return lax.broadcasted_iota(jnp.int32, (LAYERS, width), 0)


def pick(code, table):
    low = jnp.where(code < 0.5, table[0], table[1])
    high = jnp.where(code < 2.5, table[2], table[3])
    return jnp.where(code < 1.5, low, high)


def wide(ref, f, i):
    return jnp.concatenate([ref[f, i, t] for t in range(TILES)], axis=1)


def put(ref, f, i, value):
    for t in range(TILES):
        ref[f, i, t] = value[:, t * LANES : (t + 1) * LANES]


def sheet_row(ref, i, sub):
    parts = [ref[SHEET, i, t, sub : sub + 1, :] for t in range(TILES)]
    return jnp.concatenate([jnp.broadcast_to(p, (LAYERS, LANES)) for p in parts], axis=1)


def prev_lane(v):
    return pltpu.roll(v, 1, 1)


def next_lane(v):
    return pltpu.roll(v, v.shape[1] - 1, 1)


def above(v):
    return pltpu.roll(v, 1, 0)


def below(v):
    return pltpu.roll(v, LAYERS - 1, 0)


def on_device():
    return lax.axis_index("half") == 0


def pack_kernel(
    grid, codes, contacts, sheets, field_ref, low_ref, high_ref, raw, raw_code, sem
):
    copies = []
    for t in range(2):
        cols = pl.ds(t * LANES, LANES)
        copies.append(
            pltpu.make_async_copy(grid.at[0, :, :, :, cols], raw.at[t], sem.at[2 * t])
        )
        copies.append(
            pltpu.make_async_copy(codes.at[0, :, :, cols], raw_code.at[t], sem.at[2 * t + 1])
        )
    for c in copies:
        c.start()
    lanes = lane_index()
    sub = layer_index(LANES)
    raw_rows = raw.reshape(2, 4, LAYERS * TX, LANES)
    code_rows = raw_code.reshape(2, LAYERS * TX, LANES)
    for c in copies:
        c.wait()
    for x in range(TX):
        slot = 16 * (x % 8)
        if x % 8 == 0:
            low = jnp.zeros((LAYERS, LANES), F32)
            high = jnp.zeros((LAYERS, LANES), F32)
        for f in range(6):
            vals = []
            for t in range(2):
                if f < 4:
                    v = raw_rows[t, f, pl.ds(x, LAYERS, stride=TX), :]
                elif f == CODE:
                    v = code_rows[t, pl.ds(x, LAYERS, stride=TX), :].astype(F32)
                else:
                    cols = slice(t * LANES, (t + 1) * LANES)
                    con = jnp.broadcast_to(contacts[x : x + 1, cols].astype(F32), (LAYERS, LANES))
                    she = jnp.broadcast_to(sheets[0, x : x + 1, cols], (LAYERS, LANES))
                    v = jnp.where(sub < 2, con, jnp.where(sub < 4, 1.0, she))
                field_ref[f, FIRST + x, t] = v
                vals.append(v)
            w = WIDTH[f]
            at = slot + SLOT[f]
            here = (lanes >= at) & (lanes < at + w)
            low = jnp.where(here, pltpu.roll(vals[0], at, 1) if at else vals[0], low)
            high = jnp.where(here, pltpu.roll(vals[1], (at + w) % LANES, 1), high)
        if x % 8 == 7:
            low_ref[x // 8] = low
            high_ref[x // 8] = high


def y_masks(lanes):
    gy = lax.axis_index("gy")
    has_right = gy < lax.axis_size("gy") - 1
    has_left = gy > 0
    right = {w: (lanes < w) & has_right for w in (2, 3)}
    left = {w: (lanes >= LANES - w) & has_left for w in (2, 3)}
    return left, right


def side_columns(left_ref, right_ref, f, x, masks):
    w = WIDTH[f]
    at = 16 * (x % 8) + SLOT[f]
    left, right = masks
    a = pltpu.roll(right_ref[x // 8], (LANES - at) % LANES, 1)
    b = pltpu.roll(left_ref[x // 8], (2 * LANES - at - w) % LANES, 1)
    return jnp.where(right[w], a, jnp.where(left[w], b, 0.0))


def edge_kernel(field_ref, left_ref, right_ref, low_ref, high_ref):
    lanes = lane_index()
    masks = y_masks(lanes)
    for items, out in ((LOW, low_ref), (HIGH, high_ref)):
        packed = jnp.zeros((LAYERS, LANES), F32)
        for n, (f, x) in enumerate(items):
            for t in range(2):
                out[2 * n + t] = field_ref[f, FIRST + x, t]
            side = side_columns(left_ref, right_ref, f, x, masks)
            here = (lanes >= 8 * n) & (lanes < 8 * n + 8)
            packed = jnp.where(here, pltpu.roll(side, 8 * n + 3, 1), packed)
        out[2 * ITEMS] = packed


def newton_row(src, fields, dst, i):
    width = TILES * LANES
    sub = layer_index(width)
    u, e, h = wide(src, 0, i), wide(fields[1], 1, i), wide(fields[1], 2, i)
    code = wide(fields[0], CODE, i)
    total = wide(src, 0, i - 1) + wide(src, 0, i + 1) + prev_lane(u) + next_lane(u)
    total = total + jnp.where(sub > 0, above(u), 0.0) + jnp.where(sub < LAYERS - 1, below(u), 0.0)
    weight = jnp.where((sub > 0) & (sub < LAYERS - 1), 6.0, 5.0)
    r = total - weight * u + 0.7 * (h - e + pick(code, DOPING))
    diag = weight + 0.7 * (jnp.abs(e) + jnp.abs(h))
    value = u + free_cells(fields[0], i, sub) * (0.8 * r / diag)
    put(dst, 0, i, value)


def free_cells(fields, i, sub):
    contact = sheet_row(fields, i, 0)
    inside = sheet_row(fields, i, 2)
    return jnp.where(sub == 0, inside * (1.0 - contact), inside)


def face(p, n):
    g = 0.5 * jnp.tanh(n[0] - p[0])
    a = (n[1] - p[1]) - (n[1] + p[1]) * g
    c = (n[2] - p[2]) + (n[2] + p[2]) * g
    return a, c, g


def x_face(uref, fref, i):
    p = (wide(uref, 0, i), wide(fref, 1, i), wide(fref, 2, i))
    n = (wide(uref, 0, i + 1), wide(fref, 1, i + 1), wide(fref, 2, i + 1))
    return face(p, n)


def relax_row(uref, fref, fields, i, before):
    width = TILES * LANES
    sub = layer_index(width)
    here = (wide(uref, 0, i), wide(fref, 1, i), wide(fref, 2, i))
    u, e, h = here
    k = wide(fref, 3, i)
    after = face(here, (wide(uref, 0, i + 1), wide(fref, 1, i + 1), wide(fref, 2, i + 1)))
    y_after = face(here, tuple(next_lane(v) for v in here))
    y_before = tuple(prev_lane(v) for v in y_after)
    l_after = face(here, tuple(below(v) for v in here))
    l_after = tuple(jnp.where(sub < LAYERS - 1, v, 0.0) for v in l_after)
    l_before = tuple(above(v) for v in l_after)
    net = [
        (after[n] - before[n]) + (y_after[n] - y_before[n]) + (l_after[n] - l_before[n])
        for n in range(3)
    ]
    square = [
        (after[n] * after[n] + before[n] * before[n])
        + (y_after[n] * y_after[n] + y_before[n] * y_before[n])
        + (l_after[n] * l_after[n] + l_before[n] * l_before[n])
        for n in range(2)
    ]
    weight = jnp.where((sub > 0) & (sub < LAYERS - 1), 6.0, 5.0)
    spread = wide(fref, 3, i - 1) + wide(fref, 3, i + 1) + prev_lane(k) + next_lane(k)
    spread = spread + jnp.where(sub > 0, above(k), 0.0)
    spread = spread + jnp.where(sub < LAYERS - 1, below(k), 0.0) - weight * k
    code = wide(fields, CODE, i)
    mob_e, mob_h = pick(code, MOB_ELEC), pick(code, MOB_HOLE)
    power = 0.05 * (mob_e * mob_e * square[0] + mob_h * mob_h * square[1])
    recombine = 0.3 * (e * h - 1.0) / (e * e + h * h + 2.0)
    step = 0.8 * free_cells(fields, i, sub)
    scale_e = step / (weight + net[2])
    scale_h = step / (weight - net[2])
    fixed = (
        e + scale_e * net[0],
        h + scale_h * net[1],
        k + step * (0.5 * spread - 0.5 * k) / (0.5 * weight + 0.5),
    )
    varying = (
        scale_e * recombine * pick(code, INV_ELEC),
        scale_h * recombine * pick(code, INV_HOLE),
        power,
    )
    return after, fixed, varying, step / (0.5 * weight + 0.5)


def relax_first(uref, fref, fields, dst, sheet_ref, i, before):
    after, fixed, varying, heat_step = relax_row(uref, fref, fields, i, before)
    s = sheet_row(fields, i, 4)
    slow = jnp.exp(-0.3 * s)
    fast = jnp.exp(0.3 * s)
    q = varying[2] * (slow * slow)
    put(dst, 1, i, fixed[0] - varying[0] * fast)
    put(dst, 2, i, fixed[1] - varying[1] * fast)
    put(dst, 3, i, fixed[2] + heat_step * (q + 0.5 * s))
    sheet_ref[pl.ds(i - 2, 1), :] = jnp.sum(q, axis=0, keepdims=True)
    return after


def thermal_row(
    src, anchor, fields, dst, i, halves=(0, 1), source=True, first=False, put_row=put
):
    width = TILES * LANES
    sub = layer_index(width)
    top = sub == 0
    cells = [wide(src, f, i) for f in range(4)]
    code = wide(fields, CODE, i)
    inside = sheet_row(fields, i, 2)
    spread = jnp.where(top, pick(code, SPREAD_TOP), pick(code, SPREAD_IN)) * inside
    held = jnp.where(top, pick(code, KEEP_TOP), pick(code, KEEP_IN)) * inside
    if source:
        heat = jnp.where(top, pick(code, SOURCE_TOP) * sheet_row(fields, i, 4), 0.0) * inside
    out = []
    for s in halves:
        for t in range(2):
            f = 2 * s + t
            v = cells[f]
            if s == 0:
                total = wide(src, 2 + t, i - 1) + cells[2 + t]
            else:
                total = cells[t] + wide(src, t, i + 1)
            other = cells[2 * s + 1 - t]
            total = total + other + (prev_lane(other) if t == 0 else next_lane(other))
            total = total + jnp.where(sub > 0, above(v), 0.0)
            total = total + jnp.where(sub < LAYERS - 1, below(v), 0.0)
            value = spread * total + 0.1 * v
            value = value + held * (v if first else wide(anchor, f, i))
            if source:
                value = value + heat
            out.append(value)
            put_row(dst, f, i, value)
    return out


def top_mean(cells):
    total = (cells[0] + cells[1]) + (cells[2] + cells[3])
    return 0.25 * total[0:1, :]


def inner_kernel(field_in, left_ref, right_ref, field_ref, next_ref, mid_ref, sheet_ref):
    lanes = lane_index()
    masks = y_masks(lanes)
    for x in range(TX):
        for f in range(6):
            field_ref[f, FIRST + x, 2] = side_columns(left_ref, right_ref, f, x, masks)

    @pl.when(on_device())
    def _():
        def newton(i, carry):
            newton_row(field_ref, (field_ref, field_ref), next_ref, i)
            return carry

        lax.fori_loop(FIRST + 1, FIRST + TX - 1, newton, 0)

        def relax(i, carry):
            return relax_first(next_ref, field_ref, field_ref, next_ref, sheet_ref, i, carry)

        lax.fori_loop(
            FIRST + 2, FIRST + TX - 2, relax, x_face(next_ref, field_ref, FIRST + 1)
        )

    @pl.when(jnp.logical_not(on_device()))
    def _():
        def one(i, carry):
            thermal_row(field_ref, field_ref, field_ref, mid_ref, i, first=True)
            return carry

        lax.fori_loop(FIRST + 1, FIRST + TX - 1, one, 0)

        def two(i, carry):
            cells = thermal_row(mid_ref, field_ref, field_ref, next_ref, i)
            sheet_ref[pl.ds(i - FIRST, 1), :] = top_mean(cells)
            return carry

        lax.fori_loop(FIRST + 2, FIRST + TX - 2, two, 0)


def rim_kernel(
    field_in, next_in, mid_in, sheet_in, up_ref, down_ref, field_ref, next_ref, mid_ref, sheet_ref
):
    lanes = lane_index()
    gx = lax.axis_index("gx")
    has_up = gx > 0
    has_down = gx < lax.axis_size("gx") - 1
    edge = {w: (lanes < w) | (lanes >= LANES - w) for w in (2, 3)}
    for items, src, ok, base in (
        (HIGH, up_ref, has_up, FIRST - TX),
        (LOW, down_ref, has_down, FIRST + TX),
    ):
        packed = src[2 * ITEMS]
        for n, (f, x) in enumerate(items):
            for t in range(2):
                field_ref[f, base + x, t] = jnp.where(ok, src[2 * n + t], 0.0)
            side = pltpu.roll(packed, LANES - 8 * n - 3, 1)
            field_ref[f, base + x, 2] = jnp.where(edge[WIDTH[f]] & ok, side, 0.0)

    @pl.when(on_device())
    def _():
        def newton(n, carry):
            newton_row(field_ref, (field_ref, field_ref), next_ref, FIRST - 2 + n)
            newton_row(field_ref, (field_ref, field_ref), next_ref, FIRST + TX - 1 + n)
            return carry

        lax.fori_loop(0, 3, newton, 0)

        def relax(n, carry):
            args = (next_ref, field_ref, field_ref, next_ref, sheet_ref)
            one = relax_first(*args, FIRST - 1 + n, carry[0])
            two = relax_first(*args, FIRST + TX - 2 + n, carry[1])
            return one, two

        start = (
            x_face(next_ref, field_ref, FIRST - 2),
            x_face(next_ref, field_ref, FIRST + TX - 3),
        )
        lax.fori_loop(0, 3, relax, start)

    @pl.when(jnp.logical_not(on_device()))
    def _():
        args = (field_ref, field_ref, field_ref, mid_ref)
        thermal_row(*args, FIRST - 2, halves=(1,), first=True)
        thermal_row(*args, FIRST + TX + 1, halves=(0,), first=True)
        for i in (FIRST - 1, FIRST, FIRST + TX - 1, FIRST + TX):
            thermal_row(*args, i, first=True)
        for n in range(3):
            for i in (FIRST - 1 + n, FIRST + TX - 2 + n):
                cells = thermal_row(mid_ref, field_ref, field_ref, next_ref, i)
                if FIRST <= i < FIRST + TX:
                    sheet_ref[pl.ds(i - FIRST, 1), :] = top_mean(cells)


def second_kernel(field_ref, next_ref, fixed_ref, varying_ref, source_ref, spread_ref, mid_ref):
    fixed_rows = fixed_ref.reshape(2, 4, LAYERS * TX, LANES)
    varying_rows = varying_ref.reshape(2, 3, LAYERS * TX, LANES)

    def native(ref, f, i, value):
        for t in range(2):
            rows = pl.ds(i - FIRST, LAYERS, stride=TX)
            ref[t, f, rows, :] = value[:, t * LANES : (t + 1) * LANES]

    @pl.when(on_device())
    def _():
        def newton(i, carry):
            newton_row(next_ref, (field_ref, next_ref), mid_ref, i)
            return carry

        lax.fori_loop(FIRST - 1, FIRST + TX + 1, newton, 0)

        def relax(i, before):
            after, fixed, varying, _ = relax_row(mid_ref, next_ref, field_ref, i, before)
            native(fixed_rows, 0, i, wide(mid_ref, 0, i))
            for n in range(3):
                native(fixed_rows, n + 1, i, fixed[n])
                native(varying_rows, n, i, varying[n])
            return after

        lax.fori_loop(FIRST, FIRST + TX, relax, x_face(mid_ref, next_ref, FIRST - 1))

    @pl.when(jnp.logical_not(on_device()))
    def _():
        args = (next_ref, next_ref, field_ref, mid_ref)
        thermal_row(*args, FIRST - 1, halves=(1,), source=False, first=True)
        thermal_row(*args, FIRST + TX, halves=(0,), source=False, first=True)

        def three(i, carry):
            thermal_row(*args, i, source=False, first=True)
            return carry

        lax.fori_loop(FIRST, FIRST + TX, three, 0)

        def four(i, carry):
            def keep(ref, f, i, value):
                native(fixed_rows, f, i, value)

            thermal_row(mid_ref, next_ref, field_ref, None, i, source=False, put_row=keep)
            return carry

        lax.fori_loop(FIRST, FIRST + TX, four, 0)

        def top(i, carry):
            code = jnp.concatenate([field_ref[CODE, i, t] for t in range(TILES)], axis=1)
            inside = jnp.concatenate(
                [field_ref[SHEET, i, t, 2:3, :] for t in range(TILES)], axis=1
            )
            source_ref[pl.ds(i - FIRST + 1, 1), :] = pick(code[0:1, :], SOURCE_TOP) * inside
            return carry

        lax.fori_loop(FIRST - 1, FIRST + TX + 1, top, 0)

        def sides(i, carry):
            code = jnp.concatenate([field_ref[CODE, i, t] for t in range(2)], axis=1)
            spread_ref[0, pl.ds(i - FIRST, 1), :] = pick(code[0:1, :], SPREAD_TOP)
            spread_ref[1, pl.ds(i - FIRST, 1), :] = pick(code[1:2, :], SPREAD_IN)
            return carry

        lax.fori_loop(FIRST, FIRST + TX, sides, 0)


def last_kernel(
    sheet_ref, fixed_ref, varying_ref, source_ref, spread_ref, contacts,
    state_out, sheet_out, done, delta, sem,
):
    def send(src, f, t, layers):
        dst = state_out.at[0, f, layers, :, pl.ds(t * LANES, LANES)]
        return pltpu.make_async_copy(src.at[t, f, layers], dst, sem.at[f, t])

    @pl.when(on_device())
    def _():
        every = pl.ds(0, LAYERS)
        copies = [send(fixed_ref, 0, t, every) for t in range(2)]
        for c in copies:
            c.start()
        for t in range(2):
            cols = slice(t * LANES, (t + 1) * LANES)
            s = sheet_ref[0:TX, cols]
            slow = jnp.exp(-0.3 * s)
            slow = slow * slow
            fast = jnp.exp(0.3 * s)
            total = jnp.zeros((TX, LANES), F32)
            for layer in range(LAYERS):
                for f in (1, 2):
                    done[t, f, layer] = (
                        fixed_ref[t, f, layer] - varying_ref[t, f - 1, layer] * fast
                    )
                q = varying_ref[t, 2, layer] * slow
                total = total + q
                step = 0.8 / 3.5 if 0 < layer < LAYERS - 1 else 0.8 / 3.0
                if layer == 0:
                    step = step * (1.0 - contacts[:, cols].astype(F32))
                done[t, 3, layer] = fixed_ref[t, 3, layer] + step * (q + 0.5 * s)
            sheet_out[0, :, cols] = total
            for f in (1, 2, 3):
                copies.append(send(done, f, t, every))
                copies[-1].start()
        for c in copies:
            c.wait()

    @pl.when(jnp.logical_not(on_device()))
    def _():
        rest = pl.ds(2, LAYERS - 2)
        copies = [send(fixed_ref, f, t, rest) for t in range(2) for f in range(4)]
        for c in copies:
            c.start()
        delta[...] = source_ref[...] * sheet_ref[...]
        middle = delta[1 : TX + 1, :]
        by_x = (delta[0:TX, :], delta[2 : TX + 2, :])
        by_y = (prev_lane(middle), next_lane(middle))
        more = []
        for t in range(2):
            cols = slice(t * LANES, (t + 1) * LANES)
            mid = middle[:, cols]
            total = jnp.zeros((TX, LANES), F32)
            for f in range(4):
                around = 2.0 * mid + by_x[f // 2][:, cols] + by_y[f % 2][:, cols]
                value = fixed_ref[t, f, 0] + 1.1 * mid + spread_ref[0, :, cols] * around
                done[t, f, 0] = value
                total = total + value
                done[t, f, 1] = fixed_ref[t, f, 1] + spread_ref[1, :, cols] * mid
                dst = state_out.at[0, f, pl.ds(0, 2), :, pl.ds(t * LANES, LANES)]
                more.append(
                    pltpu.make_async_copy(done.at[t, f, pl.ds(0, 2)], dst, sem.at[4 + f, t])
                )
                more[-1].start()
            sheet_out[0, :, cols] = 0.25 * total
        for c in copies + more:
            c.wait()


def per_device(grid_state, materials, contacts, received_sheets):
    nx, ny = lax.axis_size("gx"), lax.axis_size("gy")

    def shift(block, axis, count, by):
        return lax.ppermute(block, axis, [(i, (i + by) % count) for i in range(count)])

    tile = (LAYERS, LANES)
    field_shape = (6, ROWS, TILES) + tile
    state_shape = (4, ROWS, TILES) + tile
    fields, y_low, y_high = call(
        pack_kernel,
        [field_shape, (2,) + tile, (2,) + tile],
        [grid_state, materials, contacts, received_sheets],
        specs=[HBM, HBM, VMEM, VMEM],
        scratch=[
            pltpu.VMEM((2, 4, LAYERS, TX, LANES), F32),
            pltpu.VMEM((2, LAYERS, TX, LANES), jnp.int32),
            pltpu.SemaphoreType.DMA((4,)),
        ],
    )
    left = shift(y_high, "gy", ny, 1)
    right = shift(y_low, "gy", ny, -1)
    edge_shape = (2 * ITEMS + 1,) + tile
    x_low, x_high = call(edge_kernel, [edge_shape, edge_shape], [fields, left, right])
    up = shift(x_high, "gx", nx, 1)
    down = shift(x_low, "gx", nx, -1)
    fields, following, middle, sheet = call(
        inner_kernel,
        [field_shape, state_shape, state_shape, SHEET_SHAPE],
        [fields, left, right],
        aliases={0: 0},
        flops=1 << 22,
    )
    fields, following, middle, sheet = call(
        rim_kernel,
        [field_shape, state_shape, state_shape, SHEET_SHAPE],
        [fields, following, middle, sheet, up, down],
        aliases={0: 0, 1: 1, 2: 2, 3: 3},
    )
    swapped = lax.ppermute(sheet, "half", [(0, 1), (1, 0)])
    fixed, varying, source, spread = call(
        second_kernel,
        [
            (2, 4, LAYERS, TX, LANES),
            (2, 3, LAYERS, TX, LANES),
            SHEET_SHAPE,
            (2, TX, 2 * LANES),
        ],
        [fields, following],
        scratch=[pltpu.VMEM(state_shape, F32)],
        flops=1 << 22,
    )
    state, outgoing = call(
        last_kernel,
        [(1, 4, LAYERS, TX, 2 * LANES), (1, TX, 2 * LANES)],
        [swapped, fixed, varying, source, spread, contacts],
        out_specs=[HBM, VMEM],
        scratch=[
            pltpu.VMEM((2, 4, LAYERS, TX, LANES), F32),
            pltpu.VMEM(SHEET_SHAPE, F32),
            pltpu.SemaphoreType.DMA((8, 2)),
        ],
    )
    return state, outgoing


def solution(mesh):
    placed = (
        P("half", None, None, "gx", "gy"),
        P("half", None, "gx", "gy"),
        P("gx", "gy"),
        P("half", "gx", "gy"),
    )
    return jax.shard_map(
        per_device,
        mesh=mesh,
        in_specs=placed,
        out_specs=(P("half", None, None, "gx", "gy"), P("half", "gx", "gy")),
        check_vma=False,
    )
```

time: 103 us -> 29.7 us (0.29)
  the two profiles are of different devices: /device:TPU:75 before, /device:TPU:1 now
where the time goes in v1:
time: 29.7 us; the launch traced here: 29.5 us
  starting transfers between devices  11.5 us (39%)
  Pallas kernels  11.4 us (38%)
  local copies, waits for them, and re-layouts  3.38 us (11%)
  waiting for transfers between devices  2.5 us (8%)
  between operations  0.71 us (2%)
    pallas_call x6, Pallas kernels, call(): pl.pallas_call(kernel, out_shape=[jax.ShapeDtypeStruct(s, F32) for s in o...  11.4 us
    ppermute x4, starting transfers between devices, shift(): lax.ppermute(block, axis, [(i, (i + by) % count) for i in range(count)])  9.95 us
    unnamed x10, local copies, waits for them, and re-layouts  3.38 us
    ppermute x4, waiting for transfers between devices, shift(): lax.ppermute(block, axis, [(i, (i + by) % count) for i in range(count)])  2.5 us
    ppermute x1, starting transfers between devices, per_device(): swapped = lax.ppermute(sheet, 'half', [(0, 1), (1, 0)])  1.51 us
  transfers between devices with their start and end apart: 5, of which 2 were waited for; matrix products, arithmetic and copies ran while one was open for 0% of the time, Pallas kernels for 28%

profile of v1, /device:TPU:1, one launch (start us, length us, event | category | flops | bytes accessed | tf_op | source)
XLA Modules:
  0.0 29.5 jit_solution(17084571662358017557)
XLA Ops:
  0.6 0.0 copy-start
  0.6 1.0 %copy-done = f32[1,4,8,16,256]{4,3,2,1,0:T(8,128)S(1)} copy-done((f32[1,4,8,16,256]{4,3,2,1,0:T(8,128)S(1)}, f32[1,4,8,16,256]{4,3,2,1,0:T(8,128)}, u32[]{:S(2)}) %copy-start) | copy-done | bytes 524312
  1.7 0.0 copy-start.1
  1.7 0.9 %copy-done.1 = s32[1,8,16,256]{3,2,1,0:T(8,128)S(1)} copy-done((s32[1,8,16,256]{3,2,1,0:T(8,128)S(1)}, s32[1,8,16,256]{3,2,1,0:T(8,128)}, u32[]{:S(2)}) %copy-start.1) | copy-done | bytes 131096
  2.6 0.0 copy-start.2
  2.6 0.7 %copy-done.2 = s32[16,256]{1,0:T(8,128)S(1)} copy-done((s32[16,256]{1,0:T(8,128)S(1)}, s32[16,256]{1,0:T(8,128)}, u32[]{:S(2)}) %copy-start.2) | copy-done | bytes 16408
  3.3 0.0 copy-start.4
  3.3 0.7 %copy-done.4 = f32[1,16,256]{2,1,0:T(8,128)S(1)} copy-done((f32[1,16,256]{2,1,0:T(8,128)S(1)}, f32[1,16,256]{2,1,0:T(8,128)}, u32[]{:S(2)}) %copy-start.4) | copy-done | bytes 16408
  4.0 0.4 %shard_map.59 = (f32[6,22,3,8,128]{4,3,2,1,0:T(8,128)S(1)}, f32[2,8,128]{2,1,0:T(8,128)S(1)}, f32[2,8,128]{2,1,0:T(8,128)S(1)}) custom-call(f32[1,4,8,16,256]{4,3,2,1,0:T(8,128)S(1)} %copy-done, s32[1,8,16,256]{3,2,1,0:T(8,128)S(1)} %copy-done.1, s32[16,256]{1,0:T(8,128)S(1)} %copy-done.2, f32[1,16,256]{2,1,0:T(8,128)S(1)} %copy-done.4), custom_call_target="tpu_custom_call" | custom-call | bytes 1048576 | tf_op jit(solution)/shard_map/pallas_call | solution.py:42
  4.5 2.7 %collective-permute-start = (f32[2,8,128]{2,1,0:T(8,128)S(1)}, f32[2,8,128]{2,1,0:T(8,128)S(1)}, u32[]{:S(2)}, u32[]{:S(2)}) collective-permute-start(f32[2,8,128]{2,1,0:T(8,128)S(1)} %get-tuple-element.19), channel_id=1, source_target_pairs={{0,1},{1,2},{2,3},{3,4},{4,5},{5,6},{6,7},{7,0},{8,9},{9,10},{10,1... | collective-permute-start | bytes 24584 | tf_op jit(solution)/shard_map/ppermute | solution.py:548
  7.2 0.6 %collective-permute-start.1 = (f32[2,8,128]{2,1,0:T(8,128)S(1)}, f32[2,8,128]{2,1,0:T(8,128)S(1)}, u32[]{:S(2)}, u32[]{:S(2)}) collective-permute-start(f32[2,8,128]{2,1,0:T(8,128)S(1)} %get-tuple-element.20), channel_id=1, source_target_pairs={{0,7},{1,0},{2,1},{3,2},{4,3},{5,4},{6,5},{7,6},{8,15},{9,8},{10,9... | collective-permute-start | bytes 24584 | tf_op jit(solution)/shard_map/ppermute | solution.py:548
  7.7 0.6 %collective-permute-done.left_ref = f32[2,8,128]{2,1,0:T(8,128)S(1)} collective-permute-done((f32[2,8,128]{2,1,0:T(8,128)S(1)}, f32[2,8,128]{2,1,0:T(8,128)S(1)}, u32[]{:S(2)}, u32[]{:S(2)}) %collective-permute-start) | collective-permute-done | bytes 8224 | tf_op jit(solution)/shard_map/ppermute | solution.py:548
  8.4 1.9 %collective-permute-done.1.right_ref = f32[2,8,128]{2,1,0:T(8,128)S(1)} collective-permute-done((f32[2,8,128]{2,1,0:T(8,128)S(1)}, f32[2,8,128]{2,1,0:T(8,128)S(1)}, u32[]{:S(2)}, u32[]{:S(2)}) %collective-permute-start.1) | collective-permute-done | bytes 8224 | tf_op jit(solution)/shard_map/ppermute | solution.py:548
  10.2 0.2 shard_map.61
  10.4 1.3 %collective-permute-start.2 = (f32[27,8,128]{2,1,0:T(8,128)S(1)}, f32[27,8,128]{2,1,0:T(8,128)S(1)}, u32[]{:S(2)}, u32[]{:S(2)}) collective-permute-start(f32[27,8,128]{2,1,0:T(8,128)S(1)} %get-tuple-element.25), channel_id=1, source_target_pairs={{0,8},{8,16},{16,24},{24,32},{32,40},{40,48},{48,56},{56,64},{64,7... | collective-permute-start | bytes 331784 | tf_op jit(solution)/shard_map/ppermute | solution.py:548
  11.7 5.4 %collective-permute-start.3 = (f32[27,8,128]{2,1,0:T(8,128)S(1)}, f32[27,8,128]{2,1,0:T(8,128)S(1)}, u32[]{:S(2)}, u32[]{:S(2)}) collective-permute-start(f32[27,8,128]{2,1,0:T(8,128)S(1)} %get-tuple-element.26), channel_id=1, source_target_pairs={{0,120},{8,0},{16,8},{24,16},{32,24},{40,32},{48,40},{56,48},{64,5... | collective-permute-start | bytes 331784 | tf_op jit(solution)/shard_map/ppermute | solution.py:548
  17.1 3.7 %shard_map.60 = (f32[6,22,3,8,128]{4,3,2,1,0:T(8,128)S(1)}, f32[4,22,3,8,128]{4,3,2,1,0:T(8,128)S(1)}, f32[4,22,3,8,128]{4,3,2,1,0:T(8,128)S(1)}, f32[24,384]{1,0:T(8,128)S(1)}) custom-call(f32[6,22,3,8,128]{4,3,2,1,0:T(8,128)S(1)} %get-tuple-element.18.field_in.field_ref, ...), custom_call_target="tpu_custom_call", output_to_operand_aliasing={{0}: (0, {})} | custom-call | flops 4194304 | bytes 1048576 | tf_op jit(solution)/shard_map/pallas_call | solution.py:42
  20.8 0.0 collective-permute-done.2.up_ref
  20.8 0.0 collective-permute-done.3.down_ref
  20.8 1.1 %shard_map.62 = (f32[6,22,3,8,128]{4,3,2,1,0:T(8,128)S(1)}, f32[4,22,3,8,128]{4,3,2,1,0:T(8,128)S(1)}, f32[4,22,3,8,128]{4,3,2,1,0:T(8,128)S(1)}, f32[24,384]{1,0:T(8,128)S(1)}) custom-call(f32[6,22,3,8,128]{4,3,2,1,0:T(8,128)S(1)} %get-tuple-element.21.field_in, ...), custom_call_target="tpu_custom_call", output_to_operand_aliasing={{0}: (0, {}), {1}: (1, {}), {2}: (2, {}), {3}: (3, {})} | custom-call | bytes 1048576 | tf_op jit(solution)/shard_map/pallas_call | solution.py:42
  21.9 1.5 %collective-permute-start.4 = (f32[24,384]{1,0:T(8,128)S(1)}, f32[24,384]{1,0:T(8,128)S(1)}, u32[]{:S(2)}, u32[]{:S(2)}) collective-permute-start(f32[24,384]{1,0:T(8,128)S(1)} %get-tuple-element.27), channel_id=1, source_target_pairs={{0,128},{128,0},{1,129},{129,1},{2,130},{130,2},{3,131},{131,3},{4... | collective-permute-start | bytes 110600 | tf_op jit(solution)/shard_map/ppermute | solution.py:583
  23.5 0.0 copy-start.3
  23.5 4.4 %shard_map.63 = (f32[2,4,8,16,128]{4,3,2,1,0:T(8,128)S(1)}, f32[2,3,8,16,128]{4,3,2,1,0:T(8,128)S(1)}, f32[24,384]{1,0:T(8,128)S(1)}, f32[2,16,256]{2,1,0:T(8,128)S(1)}) custom-call(f32[6,22,3,8,128]{4,3,2,1,0:T(8,128)S(1)} %get-tuple-element.28.field_ref, f32[4,22,3,8,128]{4,3,2,1,0:T(8,128)S(1)} %get-tuple-element.29.next_ref), custom_call_target="tpu_custom_call" | custom-call | flops 4194304 | bytes 1048576 | tf_op jit(solution)/shard_map/pallas_call | solution.py:42
  27.9 0.0 collective-permute-done.4.sheet_ref
  27.9 0.0 copy-done.3
  27.9 1.5 %shard_map.64 = (f32[1,4,8,16,256]{4,3,2,1,0:T(8,128)}, f32[1,16,256]{2,1,0:T(8,128)}) custom-call(f32[24,384]{1,0:T(8,128)S(1)} %collective-permute-done.4.sheet_ref, f32[2,4,8,16,128]{4,3,2,1,0:T(8,128)S(1)} %get-tuple-element.30.fixed_ref, f32[2,3,8,16,128]{4,3,2,1,0:T(8,128)S(1)} %get-tuple-element.31.varying_ref, ...), custom_call_target="tpu_custom_call" | custom-call | bytes 1048576 | tf_op jit(solution)/shard_map/pallas_call | solution.py:42
Async XLA Ops:
  0.6 1.0 %copy-start = (f32[1,4,8,16,256]{4,3,2,1,0:T(8,128)S(1)}, f32[1,4,8,16,256]{4,3,2,1,0:T(8,128)}, u32[]{:S(2)}) copy-start(f32[1,4,8,16,256]{4,3,2,1,0:T(8,128)} %grid.1) | copy-start | bytes 1572868
  1.7 0.9 %copy-start.1 = (s32[1,8,16,256]{3,2,1,0:T(8,128)S(1)}, s32[1,8,16,256]{3,2,1,0:T(8,128)}, u32[]{:S(2)}) copy-start(s32[1,8,16,256]{3,2,1,0:T(8,128)} %codes.1) | copy-start | bytes 393220
  2.6 0.7 %copy-start.2 = (s32[16,256]{1,0:T(8,128)S(1)}, s32[16,256]{1,0:T(8,128)}, u32[]{:S(2)}) copy-start(s32[16,256]{1,0:T(8,128)} %contacts.3) | copy-start | bytes 49156
  3.3 0.7 %copy-start.4 = (f32[1,16,256]{2,1,0:T(8,128)S(1)}, f32[1,16,256]{2,1,0:T(8,128)}, u32[]{:S(2)}) copy-start(f32[1,16,256]{2,1,0:T(8,128)} %sheets.1) | copy-start | bytes 49156
  4.5 3.9 %collective-permute-start = (f32[2,8,128]{2,1,0:T(8,128)S(1)}, f32[2,8,128]{2,1,0:T(8,128)S(1)}, u32[]{:S(2)}, u32[]{:S(2)}) collective-permute-start(f32[2,8,128]{2,1,0:T(8,128)S(1)} %get-tuple-element.19), channel_id=1, source_target_pairs={{0,1},{1,2},{2,3},{3,4},{4,5},{5,6},{6,7},{7,0},{8,9},{9,10},{10,1... | collective-permute-start | bytes 24584 | tf_op jit(solution)/shard_map/ppermute | solution.py:548
  7.2 3.1 %collective-permute-start.1 = (f32[2,8,128]{2,1,0:T(8,128)S(1)}, f32[2,8,128]{2,1,0:T(8,128)S(1)}, u32[]{:S(2)}, u32[]{:S(2)}) collective-permute-start(f32[2,8,128]{2,1,0:T(8,128)S(1)} %get-tuple-element.20), channel_id=1, source_target_pairs={{0,7},{1,0},{2,1},{3,2},{4,3},{5,4},{6,5},{7,6},{8,15},{9,8},{10,9... | collective-permute-start | bytes 24584 | tf_op jit(solution)/shard_map/ppermute | solution.py:548
  10.4 10.4 %collective-permute-start.2 = (f32[27,8,128]{2,1,0:T(8,128)S(1)}, f32[27,8,128]{2,1,0:T(8,128)S(1)}, u32[]{:S(2)}, u32[]{:S(2)}) collective-permute-start(f32[27,8,128]{2,1,0:T(8,128)S(1)} %get-tuple-element.25), channel_id=1, source_target_pairs={{0,8},{8,16},{16,24},{24,32},{32,40},{40,48},{48,56},{56,64},{64,7... | collective-permute-start | bytes 331784 | tf_op jit(solution)/shard_map/ppermute | solution.py:548
  11.7 9.1 %collective-permute-start.3 = (f32[27,8,128]{2,1,0:T(8,128)S(1)}, f32[27,8,128]{2,1,0:T(8,128)S(1)}, u32[]{:S(2)}, u32[]{:S(2)}) collective-permute-start(f32[27,8,128]{2,1,0:T(8,128)S(1)} %get-tuple-element.26), channel_id=1, source_target_pairs={{0,120},{8,0},{16,8},{24,16},{32,24},{40,32},{48,40},{56,48},{64,5... | collective-permute-start | bytes 331784 | tf_op jit(solution)/shard_map/ppermute | solution.py:548
  21.9 6.0 %collective-permute-start.4 = (f32[24,384]{1,0:T(8,128)S(1)}, f32[24,384]{1,0:T(8,128)S(1)}, u32[]{:S(2)}, u32[]{:S(2)}) collective-permute-start(f32[24,384]{1,0:T(8,128)S(1)} %get-tuple-element.27), channel_id=1, source_target_pairs={{0,128},{128,0},{1,129},{129,1},{2,130},{130,2},{3,131},{131,3},{4... | collective-permute-start | bytes 110600 | tf_op jit(solution)/shard_map/ppermute | solution.py:583
  23.5 4.5 %copy-start.3 = (s32[16,256]{1,0:T(8,128)S(1)}, s32[16,256]{1,0:T(8,128)}, u32[]{:S(2)}) copy-start(s32[16,256]{1,0:T(8,128)} %contacts.3) | copy-start | bytes 49156

commit v2 on v1

v2 whole, which is shorter than its diff:
```python
import jax
import jax.numpy as jnp
from jax import lax
from jax.experimental import pallas as pl
from jax.experimental.pallas import tpu as pltpu
from jax.sharding import PartitionSpec as P

F32 = jnp.float32
LAYERS = 8
TX = 16
LANES = 128
TILES = 3
HALO = 3
ROWS = TX + 2 * HALO
FIRST = HALO

DOPING = (1.5, -1.5, 0.6, -0.6)
MOB_ELEC = (1.0, 0.35, 0.7, 0.5)
MOB_HOLE = (0.4, 0.8, 0.3, 0.6)
CONDUCT = (1.0, 0.15, 2.5, 0.5)
CAPACITY = (0.6, 1.2, 0.4, 0.9)
POWER_ELEC = tuple(0.05 * m * m for m in MOB_ELEC)
POWER_HOLE = tuple(0.05 * m * m for m in MOB_HOLE)
LOSS_ELEC = tuple(0.3 / m for m in MOB_ELEC)
LOSS_HOLE = tuple(0.3 / m for m in MOB_HOLE)
SPREAD_TOP = tuple(0.9 * k / (5.0 * k + c) for k, c in zip(CONDUCT, CAPACITY))
SPREAD_IN = tuple(0.9 * k / (6.0 * k + c) for k, c in zip(CONDUCT, CAPACITY))
SOURCE_TOP = tuple(0.45 / (5.0 * k + c) for k, c in zip(CONDUCT, CAPACITY))

CODE, FREE, SHEET = 4, 5, 6
FIELDS = 7
WIDTH = (3, 2, 2, 2, 2, 2, 2)
SLOT = (0, 3, 5, 7, 9, 11, 13)
LOW = [(f, r) for f in range(FIELDS) for r in range(WIDTH[f])]
HIGH = [(f, TX - WIDTH[f] + r) for f in range(FIELDS) for r in range(WIDTH[f])]
BULK = sum(1 for f, _ in LOW if f < FREE)
SIDE = 2 * BULK + 2
VMEM = pl.BlockSpec(memory_space=pltpu.VMEM)
HBM = pl.BlockSpec(memory_space=pltpu.HBM)
SHEET_SHAPE = (24, TILES * LANES)
INNER = 1 << 23
UNROLL_NEWTON, UNROLL_RELAX, UNROLL_HEAT = 2, 4, 2


def call(kernel, outs, ins, specs=None, out_specs=None, scratch=(), aliases=None, cost=1 << 20):
    return pl.pallas_call(
        kernel,
        out_shape=[
            jax.ShapeDtypeStruct(*(s if isinstance(s[0], tuple) else (s, F32))) for s in outs
        ],
        in_specs=specs or [VMEM] * len(ins),
        out_specs=out_specs or [VMEM] * len(outs),
        scratch_shapes=list(scratch),
        input_output_aliases=aliases or {},
        compiler_params=pltpu.CompilerParams(vmem_limit_bytes=12 << 20),
        cost_estimate=pl.CostEstimate(flops=0, bytes_accessed=cost, transcendentals=0),
    )(*ins)


def lane_index():
    return lax.broadcasted_iota(jnp.int32, (LAYERS, LANES), 1)


def layer_index(width):
    return lax.broadcasted_iota(jnp.int32, (LAYERS, width), 0)


def pick(code, table):
    low = jnp.where(code < 0.5, table[0], table[1])
    high = jnp.where(code < 2.5, table[2], table[3])
    return jnp.where(code < 1.5, low, high)


def wide(ref, f, i):
    return jnp.concatenate([ref[f, i, t] for t in range(TILES)], axis=1)


def put(ref, f, i, value):
    for t in range(TILES):
        ref[f, i, t] = value[:, t * LANES : (t + 1) * LANES]


def cut(v, tiles):
    return v if v.shape[1] == tiles * LANES else v[:, : tiles * LANES]


def recip(v):
    r = pl.reciprocal(v, approx=True)
    return r * (2.0 - v * r)


def prev_lane(v):
    return pltpu.roll(v, 1, 1)


def next_lane(v):
    return pltpu.roll(v, v.shape[1] - 1, 1)


def above(v):
    return pltpu.roll(v, 1, 0)


def below(v):
    return pltpu.roll(v, LAYERS - 1, 0)


def on_device():
    return lax.axis_index("half") == 0


def own_row(raw_rows, code_rows, contact_ref, sheet_ref, device, sub, f, x, t):
    cols = slice(t * LANES, (t + 1) * LANES)
    if f < 4:
        return raw_rows[t, f, pl.ds(x, LAYERS, stride=TX), :]
    if f == CODE:
        return code_rows[t, pl.ds(x, LAYERS, stride=TX), :].astype(F32)
    if f == FREE:
        held = jnp.broadcast_to(contact_ref[x : x + 1, cols], (LAYERS, LANES))
        return jnp.where((held == 1) & (sub == 0) & device, 0.0, 1.0)
    return jnp.broadcast_to(sheet_ref[0, x : x + 1, cols], (LAYERS, LANES))


def pack_kernel(
    grid, codes, contacts, sheets, raw, raw_code, raw_contact, raw_sheet, left_ref, right_ref, sem
):
    copies = [
        pltpu.make_async_copy(contacts, raw_contact, sem.at[4]),
        pltpu.make_async_copy(sheets, raw_sheet, sem.at[5]),
    ]
    for t in range(2):
        cols = pl.ds(t * LANES, LANES)
        copies.append(
            pltpu.make_async_copy(grid.at[0, :, :, :, cols], raw.at[t], sem.at[2 * t])
        )
        copies.append(
            pltpu.make_async_copy(codes.at[0, :, :, cols], raw_code.at[t], sem.at[2 * t + 1])
        )
    for c in copies:
        c.start()
    lanes = lane_index()
    raw_rows = raw.reshape(2, 4, LAYERS * TX, LANES)
    code_rows = raw_code.reshape(2, LAYERS * TX, LANES)
    args = (raw_rows, code_rows, raw_contact, raw_sheet, on_device(), layer_index(LANES))
    for c in copies:
        c.wait()
    for block in range(2):
        left = jnp.zeros((LAYERS, LANES), F32)
        right = jnp.zeros((LAYERS, LANES), F32)
        for row in range(8):
            for f in range(FIELDS):
                w = WIDTH[f]
                at = 16 * row + SLOT[f]
                here = (lanes >= at) & (lanes < at + w)
                low = own_row(*args, f, 8 * block + row, 0)
                high = own_row(*args, f, 8 * block + row, 1)
                left = jnp.where(here, pltpu.roll(low, at, 1) if at else low, left)
                right = jnp.where(here, pltpu.roll(high, (at + w) % LANES, 1), right)
        left_ref[block] = left
        right_ref[block] = right


def rows_kernel(raw, raw_code, raw_contact, raw_sheet, field_ref, low_ref, high_ref):
    sub = layer_index(LANES)
    raw_rows = raw.reshape(2, 4, LAYERS * TX, LANES)
    code_rows = raw_code.reshape(2, LAYERS * TX, LANES)
    args = (raw_rows, code_rows, raw_contact, raw_sheet, on_device(), sub)
    for f in range(FIELDS):
        for x in range(TX):
            for t in range(2):
                v = own_row(*args, f, x, t)
                field_ref[f, FIRST + x, t] = v
                for items, out in ((LOW, low_ref), (HIGH, high_ref)):
                    if f < FREE and (f, x) in items:
                        out[2 * items.index((f, x)) + t] = v
    for out, x in ((low_ref, 0), (high_ref, TX - 2)):
        for t in range(2):
            free = [field_ref[FREE, FIRST + x + n, t] for n in range(2)]
            sheet = [field_ref[SHEET, FIRST + x + n, t] for n in range(2)]
            v = jnp.where(sub == 0, free[0], pltpu.roll(free[1], 1, 0))
            v = jnp.where(sub < 2, v, 1.0)
            v = jnp.where(sub < 4, v, jnp.where(sub < 6, sheet[0], sheet[1]))
            out[2 * BULK + t] = v


def y_masks(lanes):
    gy = lax.axis_index("gy")
    has_right = gy < lax.axis_size("gy") - 1
    has_left = gy > 0
    right = {w: (lanes < w) & has_right for w in (2, 3)}
    left = {w: (lanes >= LANES - w) & has_left for w in (2, 3)}
    return left, right


def side_columns(left_ref, right_ref, f, x, masks):
    w = WIDTH[f]
    at = 16 * (x % 8) + SLOT[f]
    left, right = masks
    a = pltpu.roll(right_ref[x // 8], (LANES - at) % LANES, 1)
    b = pltpu.roll(left_ref[x // 8], (2 * LANES - at - w) % LANES, 1)
    return jnp.where(right[w], a, jnp.where(left[w], b, 0.0))


def corner_kernel(low_in, high_in, left_ref, right_ref, low_ref, high_ref):
    lanes = lane_index()
    masks = y_masks(lanes)
    for items, out in ((LOW, low_ref), (HIGH, high_ref)):
        packed = jnp.zeros((LAYERS, LANES), F32)
        for n, (f, x) in enumerate(items):
            side = side_columns(left_ref, right_ref, f, x, masks)
            here = (lanes >= 8 * n) & (lanes < 8 * n + 8)
            packed = jnp.where(here, pltpu.roll(side, 8 * n + 3, 1), packed)
        out[SIDE] = packed


def newton_row(uref, fref, fields, dst, i):
    width = TILES * LANES
    sub = layer_index(width)
    u, e, h = wide(uref, 0, i), wide(fref, 1, i), wide(fref, 2, i)
    code = wide(fields, CODE, i)
    total = wide(uref, 0, i - 1) + wide(uref, 0, i + 1) + prev_lane(u) + next_lane(u)
    total = total + jnp.where(sub > 0, above(u), 0.0) + jnp.where(sub < LAYERS - 1, below(u), 0.0)
    weight = jnp.where((sub > 0) & (sub < LAYERS - 1), 6.0, 5.0)
    r = total - weight * u + 0.7 * (h - e + pick(code, DOPING))
    diag = weight + 0.7 * (jnp.abs(e) + jnp.abs(h))
    put(dst, 0, i, u + (0.8 * wide(fields, FREE, i)) * (r * recip(diag)))


def face(p, n):
    g = 0.5 * jnp.tanh(n[0] - p[0])
    a = (n[1] - p[1]) - (n[1] + p[1]) * g
    c = (n[2] - p[2]) + (n[2] + p[2]) * g
    return a, c, g


def x_face(uref, fref, i, tiles=TILES):
    p = (wide(uref, 0, i), wide(fref, 1, i), wide(fref, 2, i))
    n = (wide(uref, 0, i + 1), wide(fref, 1, i + 1), wide(fref, 2, i + 1))
    return face([cut(v, tiles) for v in p], [cut(v, tiles) for v in n])


def relax_row(uref, fref, fields, i, before, tiles=TILES):
    sub = layer_index(tiles * LANES)
    here = (wide(uref, 0, i), wide(fref, 1, i), wide(fref, 2, i))
    k = wide(fref, 3, i)
    after = (wide(uref, 0, i + 1), wide(fref, 1, i + 1), wide(fref, 2, i + 1))
    y_after = face(here, tuple(next_lane(v) for v in here))
    y_before = tuple(cut(prev_lane(v), tiles) for v in y_after)
    y_after = tuple(cut(v, tiles) for v in y_after)
    spread = cut(prev_lane(k), tiles) + cut(next_lane(k), tiles)
    here = tuple(cut(v, tiles) for v in here)
    k = cut(k, tiles)
    u, e, h = here
    after = face(here, tuple(cut(v, tiles) for v in after))
    l_after = face(here, tuple(below(v) for v in here))
    l_after = tuple(jnp.where(sub < LAYERS - 1, v, 0.0) for v in l_after)
    l_before = tuple(above(v) for v in l_after)
    net = [
        (after[n] - before[n]) + (y_after[n] - y_before[n]) + (l_after[n] - l_before[n])
        for n in range(3)
    ]
    square = [
        (after[n] * after[n] + before[n] * before[n])
        + (y_after[n] * y_after[n] + y_before[n] * y_before[n])
        + (l_after[n] * l_after[n] + l_before[n] * l_before[n])
        for n in range(2)
    ]
    inner = (sub > 0) & (sub < LAYERS - 1)
    weight = jnp.where(inner, 6.0, 5.0)
    spread = spread + cut(wide(fref, 3, i - 1), tiles) + cut(wide(fref, 3, i + 1), tiles)
    spread = spread + jnp.where(sub > 0, above(k), 0.0)
    spread = spread + jnp.where(sub < LAYERS - 1, below(k), 0.0) - weight * k
    code = cut(wide(fields, CODE, i), tiles)
    free = cut(wide(fields, FREE, i), tiles)
    power = pick(code, POWER_ELEC) * square[0] + pick(code, POWER_HOLE) * square[1]
    recombine = (e * h - 1.0) * recip(e * e + h * h + 2.0)
    step = 0.8 * free
    scale_e = step * recip(weight + net[2])
    scale_h = step * recip(weight - net[2])
    heat_step = free * jnp.where(inner, 0.8 / 3.5, 0.8 / 3.0)
    fixed = (
        e + scale_e * net[0],
        h + scale_h * net[1],
        k + heat_step * (0.5 * spread - 0.5 * k),
    )
    varying = (
        scale_e * recombine * pick(code, LOSS_ELEC),
        scale_h * recombine * pick(code, LOSS_HOLE),
        power,
    )
    return after, fixed, varying, heat_step


def relax_first(uref, fref, fields, dst, sheet_ref, i, before):
    after, fixed, varying, heat_step = relax_row(uref, fref, fields, i, before)
    s = wide(fields, SHEET, i)
    slow = jnp.exp(-0.6 * s)
    fast = jnp.exp(0.3 * s)
    q = varying[2] * slow
    put(dst, 1, i, fixed[0] - varying[0] * fast)
    put(dst, 2, i, fixed[1] - varying[1] * fast)
    put(dst, 3, i, fixed[2] + heat_step * (q + 0.5 * s))
    sheet_ref[pl.ds(i - 2, 1), :] = jnp.sum(q, axis=0, keepdims=True)
    return after


def thermal_row(
    src, anchor, fields, dst, i, halves=(0, 1), source=True, first=False, put_row=put
):
    width = TILES * LANES
    sub = layer_index(width)
    top = sub == 0
    cells = [wide(src, f, i) for f in range(4)]
    code = wide(fields, CODE, i)
    spread = jnp.where(top, pick(code, SPREAD_TOP), pick(code, SPREAD_IN))
    held = 0.9 - jnp.where(top, 5.0, 6.0) * spread
    spread = spread * wide(fields, FREE, i)
    if source:
        heat = jnp.where(top, pick(code, SOURCE_TOP) * wide(fields, SHEET, i), 0.0)
    out = []
    for s in halves:
        for t in range(2):
            f = 2 * s + t
            v = cells[f]
            if s == 0:
                total = wide(src, 2 + t, i - 1) + cells[2 + t]
            else:
                total = cells[t] + wide(src, t, i + 1)
            other = cells[2 * s + 1 - t]
            total = total + other + (prev_lane(other) if t == 0 else next_lane(other))
            total = total + jnp.where(sub > 0, above(v), 0.0)
            total = total + jnp.where(sub < LAYERS - 1, below(v), 0.0)
            value = spread * total + 0.1 * v
            value = value + held * (v if first else wide(anchor, f, i))
            if source:
                value = value + heat
            out.append(value)
            put_row(dst, f, i, value)
    return out


def top_mean(cells):
    total = (cells[0] + cells[1]) + (cells[2] + cells[3])
    return 0.25 * total[0:1, :]


def inner_kernel(field_in, left_ref, right_ref, field_ref, next_ref, mid_ref, sheet_ref):
    lanes = lane_index()
    masks = y_masks(lanes)
    for x in range(TX):
        for f in range(FIELDS):
            field_ref[f, FIRST + x, 2] = side_columns(left_ref, right_ref, f, x, masks)

    @pl.when(on_device())
    def _():
        def newton(i, carry):
            newton_row(field_ref, field_ref, field_ref, mid_ref, i)
            return carry

        lax.fori_loop(FIRST + 1, FIRST + TX - 1, newton, 0, unroll=UNROLL_NEWTON)

        def relax(i, carry):
            return relax_first(mid_ref, field_ref, field_ref, next_ref, sheet_ref, i, carry)

        start = x_face(mid_ref, field_ref, FIRST + 1)
        lax.fori_loop(FIRST + 2, FIRST + TX - 2, relax, start, unroll=UNROLL_RELAX)

    @pl.when(jnp.logical_not(on_device()))
    def _():
        def one(i, carry):
            thermal_row(field_ref, field_ref, field_ref, mid_ref, i, first=True)
            return carry

        lax.fori_loop(FIRST + 1, FIRST + TX - 1, one, 0, unroll=UNROLL_HEAT)

        def two(i, carry):
            cells = thermal_row(mid_ref, field_ref, field_ref, next_ref, i)
            sheet_ref[pl.ds(i - FIRST, 1), :] = top_mean(cells)
            return carry

        lax.fori_loop(FIRST + 2, FIRST + TX - 2, two, 0, unroll=UNROLL_HEAT)


def rim_kernel(
    field_in, next_in, mid_in, sheet_in, up_ref, down_ref,
    field_ref, next_ref, mid_ref, sheet_ref,
):
    lanes = lane_index()
    sub = layer_index(LANES)
    gx = lax.axis_index("gx")
    has_up = gx > 0
    has_down = gx < lax.axis_size("gx") - 1
    edge = {w: (lanes < w) | (lanes >= LANES - w) for w in (2, 3)}
    for items, src, ok, base in (
        (HIGH, up_ref, has_up, FIRST - TX),
        (LOW, down_ref, has_down, FIRST + TX),
    ):
        packed = src[SIDE]
        for n, (f, x) in enumerate(items):
            for t in range(2):
                second = x % 2
                if f < FREE:
                    v = src[2 * n + t]
                elif f == FREE:
                    at = 2 * BULK + t
                    top = jnp.broadcast_to(src[at, second : second + 1, :], (LAYERS, LANES))
                    v = jnp.where(sub == 0, top, 1.0)
                else:
                    row = slice(4 + 2 * second, 5 + 2 * second)
                    v = jnp.broadcast_to(src[2 * BULK + t, row, :], (LAYERS, LANES))
                field_ref[f, base + x, t] = jnp.where(ok, v, 0.0)
            side = pltpu.roll(packed, LANES - 8 * n - 3, 1)
            field_ref[f, base + x, 2] = jnp.where(edge[WIDTH[f]] & ok, side, 0.0)

    @pl.when(on_device())
    def _():
        for n in range(3):
            for i in (FIRST - 2 + n, FIRST + TX - 1 + n):
                newton_row(field_ref, field_ref, field_ref, mid_ref, i)
        args = (mid_ref, field_ref, field_ref, next_ref, sheet_ref)
        one = x_face(mid_ref, field_ref, FIRST - 2)
        two = x_face(mid_ref, field_ref, FIRST + TX - 3)
        for n in range(3):
            one = relax_first(*args, FIRST - 1 + n, one)
            two = relax_first(*args, FIRST + TX - 2 + n, two)

    @pl.when(jnp.logical_not(on_device()))
    def _():
        args = (field_ref, field_ref, field_ref, mid_ref)
        thermal_row(*args, FIRST - 2, halves=(1,), first=True)
        thermal_row(*args, FIRST + TX + 1, halves=(0,), first=True)
        for i in (FIRST - 1, FIRST, FIRST + TX - 1, FIRST + TX):
            thermal_row(*args, i, first=True)
        for n in range(3):
            for i in (FIRST - 1 + n, FIRST + TX - 2 + n):
                cells = thermal_row(mid_ref, field_ref, field_ref, next_ref, i)
                if FIRST <= i < FIRST + TX:
                    sheet_ref[pl.ds(i - FIRST, 1), :] = top_mean(cells)


def second_kernel(
    field_ref, next_ref, first_ref, fixed_ref, varying_ref, source_ref, spread_ref, mid_ref
):
    fixed_rows = fixed_ref.reshape(2, 4, LAYERS * TX, LANES)
    varying_rows = varying_ref.reshape(2, 3, LAYERS * TX, LANES)

    def native(ref, f, i, value):
        for t in range(2):
            rows = pl.ds(i - FIRST, LAYERS, stride=TX)
            ref[t, f, rows, :] = value[:, t * LANES : (t + 1) * LANES]

    @pl.when(on_device())
    def _():
        def newton(i, carry):
            newton_row(first_ref, next_ref, field_ref, mid_ref, i)
            return carry

        lax.fori_loop(FIRST - 1, FIRST + TX + 1, newton, 0, unroll=UNROLL_NEWTON)

        def relax(i, before):
            after, fixed, varying, _ = relax_row(mid_ref, next_ref, field_ref, i, before, 2)
            for t in range(2):
                fixed_rows[t, 0, pl.ds(i - FIRST, LAYERS, stride=TX), :] = mid_ref[0, i, t]
            for n in range(3):
                native(fixed_rows, n + 1, i, fixed[n])
                native(varying_rows, n, i, varying[n])
            return after

        start = x_face(mid_ref, next_ref, FIRST - 1, 2)
        lax.fori_loop(FIRST, FIRST + TX, relax, start, unroll=UNROLL_RELAX)

    @pl.when(jnp.logical_not(on_device()))
    def _():
        args = (next_ref, next_ref, field_ref, mid_ref)
        thermal_row(*args, FIRST - 1, halves=(1,), source=False, first=True)
        thermal_row(*args, FIRST + TX, halves=(0,), source=False, first=True)

        def three(i, carry):
            thermal_row(*args, i, source=False, first=True)
            return carry

        lax.fori_loop(FIRST, FIRST + TX, three, 0, unroll=UNROLL_HEAT)

        def four(i, carry):
            def keep(ref, f, i, value):
                native(fixed_rows, f, i, value)

            thermal_row(mid_ref, next_ref, field_ref, None, i, source=False, put_row=keep)
            return carry

        lax.fori_loop(FIRST, FIRST + TX, four, 0, unroll=UNROLL_HEAT)

        def top(i, carry):
            code = jnp.concatenate([field_ref[CODE, i, t] for t in range(TILES)], axis=1)
            inside = wide(field_ref, FREE, i)[0:1, :]
            source_ref[pl.ds(i - FIRST + 1, 1), :] = pick(code[0:1, :], SOURCE_TOP) * inside
            return carry

        lax.fori_loop(FIRST - 1, FIRST + TX + 1, top, 0, unroll=3)

        def sides(i, carry):
            code = jnp.concatenate([field_ref[CODE, i, t] for t in range(2)], axis=1)
            spread_ref[0, pl.ds(i - FIRST, 1), :] = pick(code[0:1, :], SPREAD_TOP)
            spread_ref[1, pl.ds(i - FIRST, 1), :] = pick(code[1:2, :], SPREAD_IN)
            return carry

        lax.fori_loop(FIRST, FIRST + TX, sides, 0, unroll=4)


def last_kernel(
    sheet_ref, fixed_ref, varying_ref, source_ref, spread_ref, contacts,
    state_out, sheet_out, done, total_ref, delta, sem,
):
    def send(src, f, t, layers):
        dst = state_out.at[0, f, layers, :, pl.ds(t * LANES, LANES)]
        return pltpu.make_async_copy(src.at[t, f, layers], dst, sem.at[f, t])

    @pl.when(on_device())
    def _():
        every = pl.ds(0, LAYERS)
        copies = [send(fixed_ref, 0, t, every) for t in range(2)]
        for c in copies:
            c.start()
        for t in range(2):
            cols = slice(t * LANES, (t + 1) * LANES)
            s = sheet_ref[0:TX, cols]
            slow = jnp.exp(-0.6 * s)
            fast = jnp.exp(0.3 * s)
            total = jnp.zeros((TX, LANES), F32)
            for layer in range(LAYERS):
                for f in (1, 2):
                    done[t, f, layer] = (
                        fixed_ref[t, f, layer] - varying_ref[t, f - 1, layer] * fast
                    )
                q = varying_ref[t, 2, layer] * slow
                total = total + q
                step = 0.8 / 3.5 if 0 < layer < LAYERS - 1 else 0.8 / 3.0
                if layer == 0:
                    step = step * (1.0 - contacts[:, cols].astype(F32))
                done[t, 3, layer] = fixed_ref[t, 3, layer] + step * (q + 0.5 * s)
            total_ref[0, :, cols] = total
            for f in (1, 2, 3):
                copies.append(send(done, f, t, every))
                copies[-1].start()
        copies.append(pltpu.make_async_copy(total_ref, sheet_out, sem.at[8, 0]))
        copies[-1].start()
        for c in copies:
            c.wait()

    @pl.when(jnp.logical_not(on_device()))
    def _():
        rest = pl.ds(2, LAYERS - 2)
        copies = [send(fixed_ref, f, t, rest) for t in range(2) for f in range(4)]
        for c in copies:
            c.start()
        delta[...] = source_ref[...] * sheet_ref[...]
        middle = delta[1 : TX + 1, :]
        by_x = (delta[0:TX, :], delta[2 : TX + 2, :])
        by_y = (prev_lane(middle), next_lane(middle))
        more = []
        for t in range(2):
            cols = slice(t * LANES, (t + 1) * LANES)
            mid = middle[:, cols]
            total = jnp.zeros((TX, LANES), F32)
            for f in range(4):
                around = 2.0 * mid + by_x[f // 2][:, cols] + by_y[f % 2][:, cols]
                value = fixed_ref[t, f, 0] + 1.1 * mid + spread_ref[0, :, cols] * around
                done[t, f, 0] = value
                total = total + value
                done[t, f, 1] = fixed_ref[t, f, 1] + spread_ref[1, :, cols] * mid
                dst = state_out.at[0, f, pl.ds(0, 2), :, pl.ds(t * LANES, LANES)]
                more.append(
                    pltpu.make_async_copy(done.at[t, f, pl.ds(0, 2)], dst, sem.at[4 + f, t])
                )
                more[-1].start()
            total_ref[0, :, cols] = 0.25 * total
        more.append(pltpu.make_async_copy(total_ref, sheet_out, sem.at[8, 0]))
        more[-1].start()
        for c in copies + more:
            c.wait()


def per_device(grid_state, materials, contacts, received_sheets):
    nx, ny = lax.axis_size("gx"), lax.axis_size("gy")

    def shift(block, axis, count, by):
        return lax.ppermute(block, axis, [(i, (i + by) % count) for i in range(count)])

    tile = (LAYERS, LANES)
    field_shape = (FIELDS, ROWS, TILES) + tile
    state_shape = (4, ROWS, TILES) + tile
    y_shape, x_shape = (2,) + tile, (SIDE + 1,) + tile
    inputs = (grid_state, materials, contacts, received_sheets)
    inputs = [pltpu.with_memory_space_constraint(v, pltpu.HBM) for v in inputs]
    raw_shapes = [
        (2, 4, LAYERS, TX, LANES),
        ((2, LAYERS, TX, LANES), jnp.int32),
        ((TX, 2 * LANES), jnp.int32),
        (1, TX, 2 * LANES),
    ]
    *raw, y_low, y_high = call(
        pack_kernel,
        raw_shapes + [y_shape, y_shape],
        inputs,
        specs=[HBM] * 4,
        scratch=[pltpu.SemaphoreType.DMA((6,))],
    )
    fields, x_low, x_high = call(rows_kernel, [field_shape, x_shape, x_shape], raw)
    left = shift(y_high, "gy", ny, 1)
    right = shift(y_low, "gy", ny, -1)
    x_low, x_high = call(
        corner_kernel, [x_shape, x_shape], [x_low, x_high, left, right], aliases={0: 0, 1: 1}
    )
    up = shift(x_high, "gx", nx, 1)
    down = shift(x_low, "gx", nx, -1)
    fields, following, middle, sheet = call(
        inner_kernel,
        [field_shape, state_shape, state_shape, SHEET_SHAPE],
        [fields, left, right],
        aliases={0: 0},
        cost=INNER,
    )
    fields, following, middle, sheet = call(
        rim_kernel,
        [field_shape, state_shape, state_shape, SHEET_SHAPE],
        [fields, following, middle, sheet, up, down],
        aliases={0: 0, 1: 1, 2: 2, 3: 3},
    )
    swapped = lax.ppermute(sheet, "half", [(0, 1), (1, 0)])
    fixed, varying, source, spread = call(
        second_kernel,
        [
            (2, 4, LAYERS, TX, LANES),
            (2, 3, LAYERS, TX, LANES),
            SHEET_SHAPE,
            (2, TX, 2 * LANES),
        ],
        [fields, following, middle],
        scratch=[pltpu.VMEM(state_shape, F32)],
        cost=1 << 23,
    )
    state, outgoing = call(
        last_kernel,
        [(1, 4, LAYERS, TX, 2 * LANES), (1, TX, 2 * LANES)],
        [swapped, fixed, varying, source, spread, contacts],
        out_specs=[HBM, HBM],
        scratch=[
            pltpu.VMEM((2, 4, LAYERS, TX, LANES), F32),
            pltpu.VMEM((1, TX, 2 * LANES), F32),
            pltpu.VMEM(SHEET_SHAPE, F32),
            pltpu.SemaphoreType.DMA((9, 2)),
        ],
    )
    return state, outgoing


def solution(mesh):
    placed = (
        P("half", None, None, "gx", "gy"),
        P("half", None, "gx", "gy"),
        P("gx", "gy"),
        P("half", "gx", "gy"),
    )
    return jax.shard_map(
        per_device,
        mesh=mesh,
        in_specs=placed,
        out_specs=(P("half", None, None, "gx", "gy"), P("half", "gx", "gy")),
        check_vma=False,
    )
```

time: 29.7 us -> 24.4 us (0.82)
  the two profiles are of different devices: /device:TPU:1 before, /device:TPU:102 now
where the time goes in v2:
time: 24.4 us; the launch traced here: 24.2 us
  waiting for transfers between devices  8.55 us (35%)
  starting transfers between devices  7.84 us (32%)
  Pallas kernels  7.13 us (29%)
  between operations  0.68 us (3%)
    pallas_call x7, Pallas kernels, call(): pl.pallas_call(kernel, out_shape=[jax.ShapeDtypeStruct(*(s if isinstance(...  7.13 us
    ppermute x4, waiting for transfers between devices, shift(): lax.ppermute(block, axis, [(i, (i + by) % count) for i in range(count)])  6.45 us
    ppermute x4, starting transfers between devices, shift(): lax.ppermute(block, axis, [(i, (i + by) % count) for i in range(count)])  6.43 us
    ppermute x1, waiting for transfers between devices, per_device(): swapped = lax.ppermute(sheet, 'half', [(0, 1), (1, 0)])  2.11 us
    ppermute x1, starting transfers between devices, per_device(): swapped = lax.ppermute(sheet, 'half', [(0, 1), (1, 0)])  1.4 us
  transfers between devices with their start and end apart: 5, of which 4 were waited for; matrix products, arithmetic and copies ran while one was open for 0% of the time, Pallas kernels for 17%

profile of v2, /device:TPU:102, one launch (start us, length us, event | category | flops | bytes accessed | tf_op | source)
XLA Modules:
  0.0 24.2 jit_solution(8634681976389348543)
XLA Ops:
  0.6 1.5 %shard_map.59 = (f32[2,4,8,16,128]{4,3,2,1,0:T(8,128)S(1)}, s32[2,8,16,128]{3,2,1,0:T(8,128)S(1)}, s32[16,256]{1,0:T(8,128)S(1)}, f32[1,16,256]{2,1,0:T(8,128)S(...) custom-call(f32[1,4,8,16,256]{4,3,2,1,0:T(8,128)} %grid.1, s32[1,8,16,256]{3,2,1,0:T(8,128)} %codes.1, ...), custom_call_target="tpu_custom_call" | custom-call | bytes 1048576 | tf_op jit(solution)/shard_map/pallas_call | solution.py:46
  2.1 0.0 collective-permute-start
  2.2 2.9 %collective-permute-start.1 = (f32[2,8,128]{2,1,0:T(8,128)S(1)}, f32[2,8,128]{2,1,0:T(8,128)S(1)}, u32[]{:S(2)}, u32[]{:S(2)}) collective-permute-start(f32[2,8,128]{2,1,0:T(8,128)S(1)} %get-tuple-element.31), channel_id=1, source_target_pairs={{0,7},{1,0},{2,1},{3,2},{4,3},{5,4},{6,5},{7,6},{8,15},{9,8},{10,9... | collective-permute-start | bytes 24584 | tf_op jit(solution)/shard_map/ppermute | solution.py:587
  5.1 0.2 shard_map.60
  5.3 1.1 %collective-permute-done.left_ref = f32[2,8,128]{2,1,0:T(8,128)S(1)} collective-permute-done((f32[2,8,128]{2,1,0:T(8,128)S(1)}, f32[2,8,128]{2,1,0:T(8,128)S(1)}, u32[]{:S(2)}, u32[]{:S(2)}) %collective-permute-start) | collective-permute-done | bytes 8224 | tf_op jit(solution)/shard_map/ppermute | solution.py:587
  6.4 0.0 collective-permute-done.1.right_ref
  6.5 0.2 shard_map.62
  6.7 3.5 %collective-permute-start.2 = (f32[25,8,128]{2,1,0:T(8,128)S(1)}, f32[25,8,128]{2,1,0:T(8,128)S(1)}, u32[]{:S(2)}, u32[]{:S(2)}) collective-permute-start(f32[25,8,128]{2,1,0:T(8,128)S(1)} %get-tuple-element.38), channel_id=1, source_target_pairs={{0,8},{8,16},{16,24},{24,32},{32,40},{40,48},{48,56},{56,64},{64,7... | collective-permute-start | bytes 307208 | tf_op jit(solution)/shard_map/ppermute | solution.py:587
  10.1 0.0 collective-permute-start.3
  10.1 1.7 %shard_map.61 = (f32[7,22,3,8,128]{4,3,2,1,0:T(8,128)S(1)}, f32[4,22,3,8,128]{4,3,2,1,0:T(8,128)S(1)}, f32[4,22,3,8,128]{4,3,2,1,0:T(8,128)S(1)}, f32[24,384]{1,0:T(8,128)S(1)}) custom-call(f32[7,22,3,8,128]{4,3,2,1,0:T(8,128)S(1)} %get-tuple-element.29.field_in, f32[2,8,128]{2,1,0:T(8,128)S(1)} %collective-permute-done.left_ref, ...), custom_call_target="tpu_custom_call", output_to_operand_aliasing={{0}: (0, {})} | custom-call | bytes 8388608 | tf_op jit(solution)/shard_map/pallas_call | solution.py:46
  11.9 1.0 %collective-permute-done.2.up_ref = f32[25,8,128]{2,1,0:T(8,128)S(1)} collective-permute-done((f32[25,8,128]{2,1,0:T(8,128)S(1)}, f32[25,8,128]{2,1,0:T(8,128)S(1)}, u32[]{:S(2)}, u32[]{:S(2)}) %collective-permute-start.2) | collective-permute-done | bytes 102432 | tf_op jit(solution)/shard_map/ppermute | solution.py:587
  12.9 4.3 %collective-permute-done.3.down_ref = f32[25,8,128]{2,1,0:T(8,128)S(1)} collective-permute-done((f32[25,8,128]{2,1,0:T(8,128)S(1)}, f32[25,8,128]{2,1,0:T(8,128)S(1)}, u32[]{:S(2)}, u32[]{:S(2)}) %collective-permute-start.3) | collective-permute-done | bytes 102432 | tf_op jit(solution)/shard_map/ppermute | solution.py:587
  17.2 0.5 %shard_map.63 = (f32[7,22,3,8,128]{4,3,2,1,0:T(8,128)S(1)}, f32[4,22,3,8,128]{4,3,2,1,0:T(8,128)S(1)}, f32[4,22,3,8,128]{4,3,2,1,0:T(8,128)S(1)}, f32[24,384]{1,0:T(8,128)S(1)}) custom-call(f32[7,22,3,8,128]{4,3,2,1,0:T(8,128)S(1)} %get-tuple-element.32.field_in, ...), custom_call_target="tpu_custom_call", output_to_operand_aliasing={{0}: (0, {}), {1}: (1, {}), {2}: (2, {}), {3}: (3, {})} | custom-call | bytes 1048576 | tf_op jit(solution)/shard_map/pallas_call | solution.py:46
  17.7 1.4 %collective-permute-start.4 = (f32[24,384]{1,0:T(8,128)S(1)}, f32[24,384]{1,0:T(8,128)S(1)}, u32[]{:S(2)}, u32[]{:S(2)}) collective-permute-start(f32[24,384]{1,0:T(8,128)S(1)} %get-tuple-element.40), channel_id=1, source_target_pairs={{0,128},{128,0},{1,129},{129,1},{2,130},{130,2},{3,131},{131,3},{4... | collective-permute-start | bytes 110600 | tf_op jit(solution)/shard_map/ppermute | solution.py:629
  19.1 0.0 copy-start
  19.1 2.0 %shard_map.64 = (f32[2,4,8,16,128]{4,3,2,1,0:T(8,128)S(1)}, f32[2,3,8,16,128]{4,3,2,1,0:T(8,128)S(1)}, f32[24,384]{1,0:T(8,128)S(1)}, f32[2,16,256]{2,1,0:T(8,128)S(1)}) custom-call(f32[7,22,3,8,128]{4,3,2,1,0:T(8,128)S(1)} %get-tuple-element.41.field_ref, f32[4,22,3,8,128]{4,3,2,1,0:T(8,128)S(1)} %get-tuple-element.42.next_ref, ...), custom_call_target="tpu_custom_call" | custom-call | bytes 8388608 | tf_op jit(solution)/shard_map/pallas_call | solution.py:46
  21.1 2.1 %collective-permute-done.4.sheet_ref = f32[24,384]{1,0:T(8,128)S(1)} collective-permute-done((f32[24,384]{1,0:T(8,128)S(1)}, f32[24,384]{1,0:T(8,128)S(1)}, u32[]{:S(2)}, u32[]{:S(2)}) %collective-permute-start.4) | collective-permute-done | bytes 36896 | tf_op jit(solution)/shard_map/ppermute | solution.py:629
  23.3 0.0 copy-done
  23.3 0.9 %shard_map.65 = (f32[1,4,8,16,256]{4,3,2,1,0:T(8,128)}, f32[1,16,256]{2,1,0:T(8,128)}) custom-call(f32[24,384]{1,0:T(8,128)S(1)} %collective-permute-done.4.sheet_ref, f32[2,4,8,16,128]{4,3,2,1,0:T(8,128)S(1)} %get-tuple-element.44.fixed_ref, f32[2,3,8,16,128]{4,3,2,1,0:T(8,128)S(1)} %get-tuple-element.45.varying_ref, ...), custom_call_target="tpu_custom_call" | custom-call | bytes 1048576 | tf_op jit(solution)/shard_map/pallas_call | solution.py:46
Async XLA Ops:
  2.1 4.3 %collective-permute-start = (f32[2,8,128]{2,1,0:T(8,128)S(1)}, f32[2,8,128]{2,1,0:T(8,128)S(1)}, u32[]{:S(2)}, u32[]{:S(2)}) collective-permute-start(f32[2,8,128]{2,1,0:T(8,128)S(1)} %get-tuple-element.30), channel_id=1, source_target_pairs={{0,1},{1,2},{2,3},{3,4},{4,5},{5,6},{6,7},{7,0},{8,9},{9,10},{10,1... | collective-permute-start | bytes 24584 | tf_op jit(solution)/shard_map/ppermute | solution.py:587
  2.2 4.3 %collective-permute-start.1 = (f32[2,8,128]{2,1,0:T(8,128)S(1)}, f32[2,8,128]{2,1,0:T(8,128)S(1)}, u32[]{:S(2)}, u32[]{:S(2)}) collective-permute-start(f32[2,8,128]{2,1,0:T(8,128)S(1)} %get-tuple-element.31), channel_id=1, source_target_pairs={{0,7},{1,0},{2,1},{3,2},{4,3},{5,4},{6,5},{7,6},{8,15},{9,8},{10,9... | collective-permute-start | bytes 24584 | tf_op jit(solution)/shard_map/ppermute | solution.py:587
  6.7 6.2 %collective-permute-start.2 = (f32[25,8,128]{2,1,0:T(8,128)S(1)}, f32[25,8,128]{2,1,0:T(8,128)S(1)}, u32[]{:S(2)}, u32[]{:S(2)}) collective-permute-start(f32[25,8,128]{2,1,0:T(8,128)S(1)} %get-tuple-element.38), channel_id=1, source_target_pairs={{0,8},{8,16},{16,24},{24,32},{32,40},{40,48},{48,56},{56,64},{64,7... | collective-permute-start | bytes 307208 | tf_op jit(solution)/shard_map/ppermute | solution.py:587
  10.1 7.1 %collective-permute-start.3 = (f32[25,8,128]{2,1,0:T(8,128)S(1)}, f32[25,8,128]{2,1,0:T(8,128)S(1)}, u32[]{:S(2)}, u32[]{:S(2)}) collective-permute-start(f32[25,8,128]{2,1,0:T(8,128)S(1)} %get-tuple-element.39), channel_id=1, source_target_pairs={{0,120},{8,0},{16,8},{24,16},{32,24},{40,32},{48,40},{56,48},{64,5... | collective-permute-start | bytes 307208 | tf_op jit(solution)/shard_map/ppermute | solution.py:587
  17.7 5.5 %collective-permute-start.4 = (f32[24,384]{1,0:T(8,128)S(1)}, f32[24,384]{1,0:T(8,128)S(1)}, u32[]{:S(2)}, u32[]{:S(2)}) collective-permute-start(f32[24,384]{1,0:T(8,128)S(1)} %get-tuple-element.40), channel_id=1, source_target_pairs={{0,128},{128,0},{1,129},{129,1},{2,130},{130,2},{3,131},{131,3},{4... | collective-permute-start | bytes 110600 | tf_op jit(solution)/shard_map/ppermute | solution.py:629
  19.1 4.2 %copy-start = (s32[16,256]{1,0:T(8,128)S(1)}, s32[16,256]{1,0:T(8,128)}, u32[]{:S(2)}) copy-start(s32[16,256]{1,0:T(8,128)} %contacts.3) | copy-start | bytes 49156

commit v3 on v2

--- a/solution.py
+++ b/solution.py
@@ -109,6 +109,10 @@
     return lax.axis_index("half") == 0
 
 
+def is_even(axis):
+    return lax.axis_index(axis) % 2 == 0
+
+
 def own_row(raw_rows, code_rows, contact_ref, sheet_ref, device, sub, f, x, t):
     cols = slice(t * LANES, (t + 1) * LANES)
     if f < 4:
@@ -122,7 +126,7 @@
 
 
 def pack_kernel(
-    grid, codes, contacts, sheets, raw, raw_code, raw_contact, raw_sheet, left_ref, right_ref, sem
+    grid, codes, contacts, sheets, raw, raw_code, raw_contact, raw_sheet, first_ref, second_ref, sem
 ):
     copies = [
         pltpu.make_async_copy(contacts, raw_contact, sem.at[4]),
@@ -139,6 +143,7 @@
     for c in copies:
         c.start()
     lanes = lane_index()
+    even = is_even("gy")
     raw_rows = raw.reshape(2, 4, LAYERS * TX, LANES)
     code_rows = raw_code.reshape(2, LAYERS * TX, LANES)
     args = (raw_rows, code_rows, raw_contact, raw_sheet, on_device(), layer_index(LANES))
@@ -156,31 +161,38 @@
                 high = own_row(*args, f, 8 * block + row, 1)
                 left = jnp.where(here, pltpu.roll(low, at, 1) if at else low, left)
                 right = jnp.where(here, pltpu.roll(high, (at + w) % LANES, 1), right)
-        left_ref[block] = left
-        right_ref[block] = right
-
-
-def rows_kernel(raw, raw_code, raw_contact, raw_sheet, field_ref, low_ref, high_ref):
+        first_ref[block] = jnp.where(even, right, left)
+        second_ref[block] = jnp.where(even, left, right)
+
+
+def rows_kernel(raw, raw_code, raw_contact, raw_sheet, field_ref, first_ref, second_ref):
     sub = layer_index(LANES)
+    even = is_even("gx")
     raw_rows = raw.reshape(2, 4, LAYERS * TX, LANES)
     code_rows = raw_code.reshape(2, LAYERS * TX, LANES)
     args = (raw_rows, code_rows, raw_contact, raw_sheet, on_device(), sub)
     for f in range(FIELDS):
         for x in range(TX):
             for t in range(2):
-                v = own_row(*args, f, x, t)
-                field_ref[f, FIRST + x, t] = v
-                for items, out in ((LOW, low_ref), (HIGH, high_ref)):
-                    if f < FREE and (f, x) in items:
-                        out[2 * items.index((f, x)) + t] = v
-    for out, x in ((low_ref, 0), (high_ref, TX - 2)):
+                field_ref[f, FIRST + x, t] = own_row(*args, f, x, t)
+
+    def both(x, t):
+        free = [field_ref[FREE, FIRST + x + n, t] for n in range(2)]
+        sheet = [field_ref[SHEET, FIRST + x + n, t] for n in range(2)]
+        v = jnp.where(sub == 0, free[0], pltpu.roll(free[1], 1, 0))
+        v = jnp.where(sub < 2, v, 1.0)
+        return jnp.where(sub < 4, v, jnp.where(sub < 6, sheet[0], sheet[1]))
+
+    for n in range(BULK + 1):
         for t in range(2):
-            free = [field_ref[FREE, FIRST + x + n, t] for n in range(2)]
-            sheet = [field_ref[SHEET, FIRST + x + n, t] for n in range(2)]
-            v = jnp.where(sub == 0, free[0], pltpu.roll(free[1], 1, 0))
-            v = jnp.where(sub < 2, v, 1.0)
-            v = jnp.where(sub < 4, v, jnp.where(sub < 6, sheet[0], sheet[1]))
-            out[2 * BULK + t] = v
+            if n < BULK:
+                f, x = LOW[n]
+                low = field_ref[f, FIRST + x, t]
+                high = field_ref[f, FIRST + HIGH[n][1], t]
+            else:
+                low, high = both(0, t), both(TX - 2, t)
+            first_ref[2 * n + t] = jnp.where(even, high, low)
+            second_ref[2 * n + t] = jnp.where(even, low, high)
 
 
 def y_masks(lanes):
@@ -192,25 +204,36 @@
     return left, right
 
 
-def side_columns(left_ref, right_ref, f, x, masks):
+def sides(first_ref, second_ref, axis):
+    even = is_even(axis)
+    first, second = first_ref[...], second_ref[...]
+    return jnp.where(even, second, first), jnp.where(even, first, second)
+
+
+def side_columns(before, after, f, x, masks):
     w = WIDTH[f]
     at = 16 * (x % 8) + SLOT[f]
     left, right = masks
-    a = pltpu.roll(right_ref[x // 8], (LANES - at) % LANES, 1)
-    b = pltpu.roll(left_ref[x // 8], (2 * LANES - at - w) % LANES, 1)
+    a = pltpu.roll(after[x // 8], (LANES - at) % LANES, 1)
+    b = pltpu.roll(before[x // 8], (2 * LANES - at - w) % LANES, 1)
     return jnp.where(right[w], a, jnp.where(left[w], b, 0.0))
 
 
-def corner_kernel(low_in, high_in, left_ref, right_ref, low_ref, high_ref):
+def corner_kernel(first_in, second_in, y_first, y_second, first_ref, second_ref):
     lanes = lane_index()
     masks = y_masks(lanes)
-    for items, out in ((LOW, low_ref), (HIGH, high_ref)):
-        packed = jnp.zeros((LAYERS, LANES), F32)
+    before, after = sides(y_first, y_second, "gy")
+    even = is_even("gx")
+    packed = []
+    for items in (LOW, HIGH):
+        both = jnp.zeros((LAYERS, LANES), F32)
         for n, (f, x) in enumerate(items):
-            side = side_columns(left_ref, right_ref, f, x, masks)
+            side = side_columns(before, after, f, x, masks)
             here = (lanes >= 8 * n) & (lanes < 8 * n + 8)
-            packed = jnp.where(here, pltpu.roll(side, 8 * n + 3, 1), packed)
-        out[SIDE] = packed
+            both = jnp.where(here, pltpu.roll(side, 8 * n + 3, 1), both)
+        packed.append(both)
+    first_ref[SIDE] = jnp.where(even, packed[1], packed[0])
+    second_ref[SIDE] = jnp.where(even, packed[0], packed[1])
 
 
 def newton_row(uref, fref, fields, dst, i):
@@ -344,12 +367,13 @@
     return 0.25 * total[0:1, :]
 
 
-def inner_kernel(field_in, left_ref, right_ref, field_ref, next_ref, mid_ref, sheet_ref):
+def inner_kernel(field_in, y_first, y_second, field_ref, next_ref, mid_ref, sheet_ref):
     lanes = lane_index()
     masks = y_masks(lanes)
+    before, after = sides(y_first, y_second, "gy")
     for x in range(TX):
         for f in range(FIELDS):
-            field_ref[f, FIRST + x, 2] = side_columns(left_ref, right_ref, f, x, masks)
+            field_ref[f, FIRST + x, 2] = side_columns(before, after, f, x, masks)
 
     @pl.when(on_device())
     def _():
@@ -382,7 +406,7 @@
 
 
 def rim_kernel(
-    field_in, next_in, mid_in, sheet_in, up_ref, down_ref,
+    field_in, next_in, mid_in, sheet_in, x_first, x_second,
     field_ref, next_ref, mid_ref, sheet_ref,
 ):
     lanes = lane_index()
@@ -391,9 +415,10 @@
     has_up = gx > 0
     has_down = gx < lax.axis_size("gx") - 1
     edge = {w: (lanes < w) | (lanes >= LANES - w) for w in (2, 3)}
+    up, down = sides(x_first, x_second, "gx")
     for items, src, ok, base in (
-        (HIGH, up_ref, has_up, FIRST - TX),
-        (LOW, down_ref, has_down, FIRST + TX),
+        (HIGH, up, has_up, FIRST - TX),
+        (LOW, down, has_down, FIRST + TX),
     ):
         packed = src[SIDE]
         for n, (f, x) in enumerate(items):
@@ -402,12 +427,11 @@
                 if f < FREE:
                     v = src[2 * n + t]
                 elif f == FREE:
-                    at = 2 * BULK + t
-                    top = jnp.broadcast_to(src[at, second : second + 1, :], (LAYERS, LANES))
-                    v = jnp.where(sub == 0, top, 1.0)
+                    top = src[2 * BULK + t][second : second + 1, :]
+                    v = jnp.where(sub == 0, jnp.broadcast_to(top, (LAYERS, LANES)), 1.0)
                 else:
-                    row = slice(4 + 2 * second, 5 + 2 * second)
-                    v = jnp.broadcast_to(src[2 * BULK + t, row, :], (LAYERS, LANES))
+                    row = src[2 * BULK + t][4 + 2 * second : 5 + 2 * second, :]
+                    v = jnp.broadcast_to(row, (LAYERS, LANES))
                 field_ref[f, base + x, t] = jnp.where(ok, v, 0.0)
             side = pltpu.roll(packed, LANES - 8 * n - 3, 1)
             field_ref[f, base + x, 2] = jnp.where(edge[WIDTH[f]] & ok, side, 0.0)
@@ -583,8 +607,18 @@
 def per_device(grid_state, materials, contacts, received_sheets):
     nx, ny = lax.axis_size("gx"), lax.axis_size("gy")
 
-    def shift(block, axis, count, by):
-        return lax.ppermute(block, axis, [(i, (i + by) % count) for i in range(count)])
+    def swap(block, axis, parity):
+        route = []
+        for i in range(nx):
+            for j in range(ny):
+                at, count = (i, nx) if axis == "gx" else (j, ny)
+                to = ((at - parity) ^ 1) + parity
+                if axis == "gx":
+                    p = (to, j) if 0 <= to < count else (i, j ^ 1)
+                else:
+                    p = (i, to) if 0 <= to < count else (i ^ 1, j)
+                route.append((i * ny + j, p[0] * ny + p[1]))
+        return lax.ppermute(block, ("gx", "gy"), route)
 
     tile = (LAYERS, LANES)
     field_shape = (FIELDS, ROWS, TILES) + tile
@@ -598,32 +632,35 @@
         ((TX, 2 * LANES), jnp.int32),
         (1, TX, 2 * LANES),
     ]
-    *raw, y_low, y_high = call(
+    *raw, y_first, y_second = call(
         pack_kernel,
         raw_shapes + [y_shape, y_shape],
         inputs,
         specs=[HBM] * 4,
         scratch=[pltpu.SemaphoreType.DMA((6,))],
     )
-    fields, x_low, x_high = call(rows_kernel, [field_shape, x_shape, x_shape], raw)
-    left = shift(y_high, "gy", ny, 1)
-    right = shift(y_low, "gy", ny, -1)
-    x_low, x_high = call(
-        corner_kernel, [x_shape, x_shape], [x_low, x_high, left, right], aliases={0: 0, 1: 1}
-    )
-    up = shift(x_high, "gx", nx, 1)
-    down = shift(x_low, "gx", nx, -1)
+    fields, x_first, x_second = call(rows_kernel, [field_shape, x_shape, x_shape], raw)
+    y_second = swap(y_second, "gy", 1)
+    y_first = swap(y_first, "gy", 0)
+    x_first, x_second = call(
+        corner_kernel,
+        [x_shape, x_shape],
+        [x_first, x_second, y_first, y_second],
+        aliases={0: 0, 1: 1},
+    )
+    x_second = swap(x_second, "gx", 1)
+    x_first = swap(x_first, "gx", 0)
     fields, following, middle, sheet = call(
         inner_kernel,
         [field_shape, state_shape, state_shape, SHEET_SHAPE],
-        [fields, left, right],
+        [fields, y_first, y_second],
         aliases={0: 0},
         cost=INNER,
     )
     fields, following, middle, sheet = call(
         rim_kernel,
         [field_shape, state_shape, state_shape, SHEET_SHAPE],
-        [fields, following, middle, sheet, up, down],
+        [fields, following, middle, sheet, x_first, x_second],
         aliases={0: 0, 1: 1, 2: 2, 3: 3},
     )
     swapped = lax.ppermute(sheet, "half", [(0, 1), (1, 0)])

time: 24.4 us -> 21.9 us (0.90)
  the two profiles are of different devices: /device:TPU:102 before, /device:TPU:128 now
where the time goes in v3:
time: 21.9 us; the launch traced here: 21.7 us
  Pallas kernels  7.79 us (36%)
  waiting for transfers between devices  7.33 us (33%)
  starting transfers between devices  5.94 us (27%)
  between operations  0.69 us (3%)
    pallas_call x7, Pallas kernels, call(): pl.pallas_call(kernel, out_shape=[jax.ShapeDtypeStruct(*(s if isinstance(...  7.79 us
    ppermute x4, waiting for transfers between devices, swap(): return lax.ppermute(block, ('gx', 'gy'), route)  6.49 us
    ppermute x4, starting transfers between devices, swap(): return lax.ppermute(block, ('gx', 'gy'), route)  3.32 us
    ppermute x1, starting transfers between devices, per_device(): swapped = lax.ppermute(sheet, 'half', [(0, 1), (1, 0)])  2.61 us
    ppermute x1, waiting for transfers between devices, per_device(): swapped = lax.ppermute(sheet, 'half', [(0, 1), (1, 0)])  0.84 us
  transfers between devices with their start and end apart: 5, of which 4 were waited for; matrix products, arithmetic and copies ran while one was open for 0% of the time, Pallas kernels for 20%

profile of v3, /device:TPU:128, one launch (start us, length us, event | category | flops | bytes accessed | tf_op | source)
XLA Modules:
  0.0 21.7 jit_solution(12465362933114100367)
XLA Ops:
  0.6 1.5 %shard_map.59 = (f32[2,4,8,16,128]{4,3,2,1,0:T(8,128)S(1)}, s32[2,8,16,128]{3,2,1,0:T(8,128)S(1)}, s32[16,256]{1,0:T(8,128)S(1)}, f32[1,16,256]{2,1,0:T(8,128)S(...) custom-call(f32[1,4,8,16,256]{4,3,2,1,0:T(8,128)} %grid.1, s32[1,8,16,256]{3,2,1,0:T(8,128)} %codes.1, ...), custom_call_target="tpu_custom_call" | custom-call | bytes 1048576 | tf_op jit(solution)/shard_map/pallas_call | solution.py:46
  2.1 0.1 collective-permute-start
  2.2 1.6 %collective-permute-start.1 = (f32[2,8,128]{2,1,0:T(8,128)S(1)}, f32[2,8,128]{2,1,0:T(8,128)S(1)}, u32[]{:S(2)}, u32[]{:S(2)}) collective-permute-start(f32[2,8,128]{2,1,0:T(8,128)S(1)} %get-tuple-element.31), channel_id=1, source_target_pairs={{0,8},{1,2},{2,1},{3,4},{4,3},{5,6},{6,5},{7,15},{8,0},{9,10},{10,... | collective-permute-start | bytes 24584 | tf_op jit(solution)/shard_map/ppermute | solution.py:621
  3.8 0.2 %shard_map.60 = (f32[7,22,3,8,128]{4,3,2,1,0:T(8,128)S(1)}, f32[25,8,128]{2,1,0:T(8,128)S(1)}, f32[25,8,128]{2,1,0:T(8,128)S(1)}) custom-call(f32[2,4,8,16,128]{4,3,2,1,0:T(8,128)S(1)} %get-tuple-element.25.raw, s32[2,8,16,128]{3,2,1,0:T(8,128)S(1)} %get-tuple-element.26.raw_code, s32[16,256]{1,0:T(8,128)S(1)} %get-tuple-element.27.raw_contact, ...), custom_call_target="tpu_custom_call" | custom-call | bytes 1048576 | tf_op jit(solution)/shard_map/pallas_call | solution.py:46
  4.1 0.0 collective-permute-done.y_first
  4.1 1.9 %collective-permute-done.1.y_second = f32[2,8,128]{2,1,0:T(8,128)S(1)} collective-permute-done((f32[2,8,128]{2,1,0:T(8,128)S(1)}, f32[2,8,128]{2,1,0:T(8,128)S(1)}, u32[]{:S(2)}, u32[]{:S(2)}) %collective-permute-start.1) | collective-permute-done | bytes 8224 | tf_op jit(solution)/shard_map/ppermute | solution.py:621
  6.0 0.2 shard_map.62
  6.2 1.6 %collective-permute-start.2 = (f32[25,8,128]{2,1,0:T(8,128)S(1)}, f32[25,8,128]{2,1,0:T(8,128)S(1)}, u32[]{:S(2)}, u32[]{:S(2)}) collective-permute-start(f32[25,8,128]{2,1,0:T(8,128)S(1)} %get-tuple-element.38), channel_id=1, source_target_pairs={{0,8},{1,9},{2,10},{3,11},{4,12},{5,13},{6,14},{7,15},{8,0},{9,1},... | collective-permute-start | bytes 307208 | tf_op jit(solution)/shard_map/ppermute | solution.py:621
  7.8 0.1 collective-permute-start.3
  7.8 2.1 %shard_map.61 = (f32[7,22,3,8,128]{4,3,2,1,0:T(8,128)S(1)}, f32[4,22,3,8,128]{4,3,2,1,0:T(8,128)S(1)}, f32[4,22,3,8,128]{4,3,2,1,0:T(8,128)S(1)}, f32[24,384]{1,0:T(8,128)S(1)}) custom-call(f32[7,22,3,8,128]{4,3,2,1,0:T(8,128)S(1)} %get-tuple-element.29.field_in, f32[2,8,128]{2,1,0:T(8,128)S(1)} %collective-permute-done.y_first, ...), custom_call_target="tpu_custom_call", output_to_operand_aliasing={{0}: (0, {})} | custom-call | bytes 8388608 | tf_op jit(solution)/shard_map/pallas_call | solution.py:46
  9.9 2.4 %collective-permute-done.2.x_first = f32[25,8,128]{2,1,0:T(8,128)S(1)} collective-permute-done((f32[25,8,128]{2,1,0:T(8,128)S(1)}, f32[25,8,128]{2,1,0:T(8,128)S(1)}, u32[]{:S(2)}, u32[]{:S(2)}) %collective-permute-start.2) | collective-permute-done | bytes 102432 | tf_op jit(solution)/shard_map/ppermute | solution.py:621
  12.4 2.2 %collective-permute-done.3.x_second = f32[25,8,128]{2,1,0:T(8,128)S(1)} collective-permute-done((f32[25,8,128]{2,1,0:T(8,128)S(1)}, f32[25,8,128]{2,1,0:T(8,128)S(1)}, u32[]{:S(2)}, u32[]{:S(2)}) %collective-permute-start.3) | collective-permute-done | bytes 102432 | tf_op jit(solution)/shard_map/ppermute | solution.py:621
  14.5 0.7 %shard_map.63 = (f32[7,22,3,8,128]{4,3,2,1,0:T(8,128)S(1)}, f32[4,22,3,8,128]{4,3,2,1,0:T(8,128)S(1)}, f32[4,22,3,8,128]{4,3,2,1,0:T(8,128)S(1)}, f32[24,384]{1,0:T(8,128)S(1)}) custom-call(f32[7,22,3,8,128]{4,3,2,1,0:T(8,128)S(1)} %get-tuple-element.32.field_in, ...), custom_call_target="tpu_custom_call", output_to_operand_aliasing={{0}: (0, {}), {1}: (1, {}), {2}: (2, {}), {3}: (3, {})} | custom-call | bytes 1048576 | tf_op jit(solution)/shard_map/pallas_call | solution.py:46
  15.2 2.6 %collective-permute-start.4 = (f32[24,384]{1,0:T(8,128)S(1)}, f32[24,384]{1,0:T(8,128)S(1)}, u32[]{:S(2)}, u32[]{:S(2)}) collective-permute-start(f32[24,384]{1,0:T(8,128)S(1)} %get-tuple-element.40), channel_id=1, source_target_pairs={{0,128},{128,0},{1,129},{129,1},{2,130},{130,2},{3,131},{131,3},{4... | collective-permute-start | bytes 110600 | tf_op jit(solution)/shard_map/ppermute | solution.py:666
  17.9 0.0 copy-start
  17.9 2.1 %shard_map.64 = (f32[2,4,8,16,128]{4,3,2,1,0:T(8,128)S(1)}, f32[2,3,8,16,128]{4,3,2,1,0:T(8,128)S(1)}, f32[24,384]{1,0:T(8,128)S(1)}, f32[2,16,256]{2,1,0:T(8,128)S(1)}) custom-call(f32[7,22,3,8,128]{4,3,2,1,0:T(8,128)S(1)} %get-tuple-element.41.field_ref, f32[4,22,3,8,128]{4,3,2,1,0:T(8,128)S(1)} %get-tuple-element.42.next_ref, ...), custom_call_target="tpu_custom_call" | custom-call | bytes 8388608 | tf_op jit(solution)/shard_map/pallas_call | solution.py:46
  20.0 0.8 %collective-permute-done.4.sheet_ref = f32[24,384]{1,0:T(8,128)S(1)} collective-permute-done((f32[24,384]{1,0:T(8,128)S(1)}, f32[24,384]{1,0:T(8,128)S(1)}, u32[]{:S(2)}, u32[]{:S(2)}) %collective-permute-start.4) | collective-permute-done | bytes 36896 | tf_op jit(solution)/shard_map/ppermute | solution.py:666
  20.8 0.0 copy-done
  20.8 0.9 %shard_map.65 = (f32[1,4,8,16,256]{4,3,2,1,0:T(8,128)}, f32[1,16,256]{2,1,0:T(8,128)}) custom-call(f32[24,384]{1,0:T(8,128)S(1)} %collective-permute-done.4.sheet_ref, f32[2,4,8,16,128]{4,3,2,1,0:T(8,128)S(1)} %get-tuple-element.44.fixed_ref, f32[2,3,8,16,128]{4,3,2,1,0:T(8,128)S(1)} %get-tuple-element.45.varying_ref, ...), custom_call_target="tpu_custom_call" | custom-call | bytes 1048576 | tf_op jit(solution)/shard_map/pallas_call | solution.py:46
Async XLA Ops:
  2.1 1.9 %collective-permute-start = (f32[2,8,128]{2,1,0:T(8,128)S(1)}, f32[2,8,128]{2,1,0:T(8,128)S(1)}, u32[]{:S(2)}, u32[]{:S(2)}) collective-permute-start(f32[2,8,128]{2,1,0:T(8,128)S(1)} %get-tuple-element.30), channel_id=1, source_target_pairs={{0,1},{1,0},{2,3},{3,2},{4,5},{5,4},{6,7},{7,6},{8,9},{9,8},{10,11... | collective-permute-start | bytes 24584 | tf_op jit(solution)/shard_map/ppermute | solution.py:621
  2.2 3.7 %collective-permute-start.1 = (f32[2,8,128]{2,1,0:T(8,128)S(1)}, f32[2,8,128]{2,1,0:T(8,128)S(1)}, u32[]{:S(2)}, u32[]{:S(2)}) collective-permute-start(f32[2,8,128]{2,1,0:T(8,128)S(1)} %get-tuple-element.31), channel_id=1, source_target_pairs={{0,8},{1,2},{2,1},{3,4},{4,3},{5,6},{6,5},{7,15},{8,0},{9,10},{10,... | collective-permute-start | bytes 24584 | tf_op jit(solution)/shard_map/ppermute | solution.py:621
  6.2 6.2 %collective-permute-start.2 = (f32[25,8,128]{2,1,0:T(8,128)S(1)}, f32[25,8,128]{2,1,0:T(8,128)S(1)}, u32[]{:S(2)}, u32[]{:S(2)}) collective-permute-start(f32[25,8,128]{2,1,0:T(8,128)S(1)} %get-tuple-element.38), channel_id=1, source_target_pairs={{0,8},{1,9},{2,10},{3,11},{4,12},{5,13},{6,14},{7,15},{8,0},{9,1},... | collective-permute-start | bytes 307208 | tf_op jit(solution)/shard_map/ppermute | solution.py:621
  7.8 6.8 %collective-permute-start.3 = (f32[25,8,128]{2,1,0:T(8,128)S(1)}, f32[25,8,128]{2,1,0:T(8,128)S(1)}, u32[]{:S(2)}, u32[]{:S(2)}) collective-permute-start(f32[25,8,128]{2,1,0:T(8,128)S(1)} %get-tuple-element.39), channel_id=1, source_target_pairs={{0,1},{1,0},{2,3},{3,2},{4,5},{5,4},{6,7},{7,6},{8,16},{9,17},{10,... | collective-permute-start | bytes 307208 | tf_op jit(solution)/shard_map/ppermute | solution.py:621
  15.2 5.5 %collective-permute-start.4 = (f32[24,384]{1,0:T(8,128)S(1)}, f32[24,384]{1,0:T(8,128)S(1)}, u32[]{:S(2)}, u32[]{:S(2)}) collective-permute-start(f32[24,384]{1,0:T(8,128)S(1)} %get-tuple-element.40), channel_id=1, source_target_pairs={{0,128},{128,0},{1,129},{129,1},{2,130},{130,2},{3,131},{131,3},{4... | collective-permute-start | bytes 110600 | tf_op jit(solution)/shard_map/ppermute | solution.py:666
  17.9 2.9 %copy-start = (s32[16,256]{1,0:T(8,128)S(1)}, s32[16,256]{1,0:T(8,128)}, u32[]{:S(2)}) copy-start(s32[16,256]{1,0:T(8,128)} %contacts.3) | copy-start | bytes 49156

commit v4 on v3

--- a/solution.py
+++ b/solution.py
@@ -38,7 +38,7 @@
 VMEM = pl.BlockSpec(memory_space=pltpu.VMEM)
 HBM = pl.BlockSpec(memory_space=pltpu.HBM)
 SHEET_SHAPE = (24, TILES * LANES)
-INNER = 1 << 23
+INNER = 10**10
 UNROLL_NEWTON, UNROLL_RELAX, UNROLL_HEAT = 2, 4, 2
 
 
@@ -53,7 +53,7 @@
         scratch_shapes=list(scratch),
         input_output_aliases=aliases or {},
         compiler_params=pltpu.CompilerParams(vmem_limit_bytes=12 << 20),
-        cost_estimate=pl.CostEstimate(flops=0, bytes_accessed=cost, transcendentals=0),
+        cost_estimate=pl.CostEstimate(flops=cost, bytes_accessed=1 << 20, transcendentals=0),
     )(*ins)
 
 
@@ -128,39 +128,48 @@
 def pack_kernel(
     grid, codes, contacts, sheets, raw, raw_code, raw_contact, raw_sheet, first_ref, second_ref, sem
 ):
-    copies = [
-        pltpu.make_async_copy(contacts, raw_contact, sem.at[4]),
-        pltpu.make_async_copy(sheets, raw_sheet, sem.at[5]),
+    small = [
+        pltpu.make_async_copy(contacts, raw_contact, sem.at[10]),
+        pltpu.make_async_copy(sheets, raw_sheet, sem.at[11]),
     ]
+    copies = []
     for t in range(2):
         cols = pl.ds(t * LANES, LANES)
         copies.append(
-            pltpu.make_async_copy(grid.at[0, :, :, :, cols], raw.at[t], sem.at[2 * t])
+            [
+                pltpu.make_async_copy(grid.at[0, f, :, :, cols], raw.at[t, f], sem.at[5 * t + f])
+                for f in range(4)
+            ]
         )
-        copies.append(
-            pltpu.make_async_copy(codes.at[0, :, :, cols], raw_code.at[t], sem.at[2 * t + 1])
+        copies[t].append(
+            pltpu.make_async_copy(codes.at[0, :, :, cols], raw_code.at[t], sem.at[5 * t + 4])
         )
-    for c in copies:
+    for c in copies[0] + small + copies[1]:
         c.start()
     lanes = lane_index()
     even = is_even("gy")
     raw_rows = raw.reshape(2, 4, LAYERS * TX, LANES)
     code_rows = raw_code.reshape(2, LAYERS * TX, LANES)
     args = (raw_rows, code_rows, raw_contact, raw_sheet, on_device(), layer_index(LANES))
-    for c in copies:
+    for c in small:
         c.wait()
+    packed = []
+    for t in range(2):
+        for c in copies[t]:
+            c.wait()
+        for block in range(2):
+            side = jnp.zeros((LAYERS, LANES), F32)
+            for row in range(8):
+                for f in range(FIELDS):
+                    w = WIDTH[f]
+                    at = 16 * row + SLOT[f]
+                    here = (lanes >= at) & (lanes < at + w)
+                    v = own_row(*args, f, 8 * block + row, t)
+                    by = (at + t * w) % LANES
+                    side = jnp.where(here, pltpu.roll(v, by, 1) if by else v, side)
+            packed.append(side)
     for block in range(2):
-        left = jnp.zeros((LAYERS, LANES), F32)
-        right = jnp.zeros((LAYERS, LANES), F32)
-        for row in range(8):
-            for f in range(FIELDS):
-                w = WIDTH[f]
-                at = 16 * row + SLOT[f]
-                here = (lanes >= at) & (lanes < at + w)
-                low = own_row(*args, f, 8 * block + row, 0)
-                high = own_row(*args, f, 8 * block + row, 1)
-                left = jnp.where(here, pltpu.roll(low, at, 1) if at else low, left)
-                right = jnp.where(here, pltpu.roll(high, (at + w) % LANES, 1), right)
+        left, right = packed[block], packed[2 + block]
         first_ref[block] = jnp.where(even, right, left)
         second_ref[block] = jnp.where(even, left, right)
 
@@ -219,21 +228,28 @@
     return jnp.where(right[w], a, jnp.where(left[w], b, 0.0))
 
 
-def corner_kernel(first_in, second_in, y_first, y_second, first_ref, second_ref):
+def corner_kernel(first_in, y_first, y_second, first_ref, second_ref):
     lanes = lane_index()
-    masks = y_masks(lanes)
+    gy = lax.axis_index("gy")
     before, after = sides(y_first, y_second, "gy")
+    before = jnp.where(gy > 0, before, 0.0)
+    after = jnp.where(gy < lax.axis_size("gy") - 1, after, 0.0)
     even = is_even("gx")
     packed = []
     for items in (LOW, HIGH):
         both = jnp.zeros((LAYERS, LANES), F32)
         for n, (f, x) in enumerate(items):
-            side = side_columns(before, after, f, x, masks)
-            here = (lanes >= 8 * n) & (lanes < 8 * n + 8)
-            both = jnp.where(here, pltpu.roll(side, 8 * n + 3, 1), both)
+            w = WIDTH[f]
+            at = 16 * (x % 8) + SLOT[f]
+            middle = 8 * n + 3
+            for src, start in ((before, middle - w), (after, middle)):
+                here = (lanes >= start) & (lanes < start + w)
+                by = (start - at) % LANES
+                v = src[x // 8]
+                both = jnp.where(here, pltpu.roll(v, by, 1) if by else v, both)
         packed.append(both)
     first_ref[SIDE] = jnp.where(even, packed[1], packed[0])
-    second_ref[SIDE] = jnp.where(even, packed[0], packed[1])
+    second_ref[...] = jnp.where(even, packed[0], packed[1])
 
 
 def newton_row(uref, fref, fields, dst, i):
@@ -406,7 +422,7 @@
 
 
 def rim_kernel(
-    field_in, next_in, mid_in, sheet_in, x_first, x_second,
+    field_in, next_in, mid_in, sheet_in, x_first, x_second, side_second,
     field_ref, next_ref, mid_ref, sheet_ref,
 ):
     lanes = lane_index()
@@ -415,12 +431,12 @@
     has_up = gx > 0
     has_down = gx < lax.axis_size("gx") - 1
     edge = {w: (lanes < w) | (lanes >= LANES - w) for w in (2, 3)}
-    up, down = sides(x_first, x_second, "gx")
-    for items, src, ok, base in (
-        (HIGH, up, has_up, FIRST - TX),
-        (LOW, down, has_down, FIRST + TX),
+    up, down = sides(x_first.at[0:SIDE], x_second, "gx")
+    up_side, down_side = sides(x_first.at[SIDE], side_second, "gx")
+    for items, src, packed, ok, base in (
+        (HIGH, up, up_side, has_up, FIRST - TX),
+        (LOW, down, down_side, has_down, FIRST + TX),
     ):
-        packed = src[SIDE]
         for n, (f, x) in enumerate(items):
             for t in range(2):
                 second = x % 2
@@ -623,7 +639,7 @@
     tile = (LAYERS, LANES)
     field_shape = (FIELDS, ROWS, TILES) + tile
     state_shape = (4, ROWS, TILES) + tile
-    y_shape, x_shape = (2,) + tile, (SIDE + 1,) + tile
+    y_shape = (2,) + tile
     inputs = (grid_state, materials, contacts, received_sheets)
     inputs = [pltpu.with_memory_space_constraint(v, pltpu.HBM) for v in inputs]
     raw_shapes = [
@@ -637,18 +653,19 @@
         raw_shapes + [y_shape, y_shape],
         inputs,
         specs=[HBM] * 4,
-        scratch=[pltpu.SemaphoreType.DMA((6,))],
-    )
-    fields, x_first, x_second = call(rows_kernel, [field_shape, x_shape, x_shape], raw)
+        scratch=[pltpu.SemaphoreType.DMA((12,))],
+    )
+    fields, x_first, x_second = call(rows_kernel, [field_shape, (SIDE + 1,) + tile, (SIDE,) + tile], raw)
     y_second = swap(y_second, "gy", 1)
     y_first = swap(y_first, "gy", 0)
-    x_first, x_second = call(
+    x_second = swap(x_second, "gx", 1)
+    x_first, side_second = call(
         corner_kernel,
-        [x_shape, x_shape],
-        [x_first, x_second, y_first, y_second],
-        aliases={0: 0, 1: 1},
-    )
-    x_second = swap(x_second, "gx", 1)
+        [(SIDE + 1,) + tile, tile],
+        [x_first, y_first, y_second],
+        aliases={0: 0},
+    )
+    side_second = swap(side_second, "gx", 1)
     x_first = swap(x_first, "gx", 0)
     fields, following, middle, sheet = call(
         inner_kernel,
@@ -660,7 +677,7 @@
     fields, following, middle, sheet = call(
         rim_kernel,
         [field_shape, state_shape, state_shape, SHEET_SHAPE],
-        [fields, following, middle, sheet, x_first, x_second],
+        [fields, following, middle, sheet, x_first, x_second, side_second],
         aliases={0: 0, 1: 1, 2: 2, 3: 3},
     )
     swapped = lax.ppermute(sheet, "half", [(0, 1), (1, 0)])

time: 21.9 us -> 21.4 us (0.977)
  the two profiles are of different devices: /device:TPU:128 before, /device:TPU:102 now
where the time goes in v4:
time: 21.4 us; the launch traced here: 21.3 us
  starting transfers between devices  8.46 us (40%)
  Pallas kernels  7.06 us (33%)
  waiting for transfers between devices  5.07 us (24%)
  between operations  0.68 us (3%)
    pallas_call x7, Pallas kernels, call(): pl.pallas_call(kernel, out_shape=[jax.ShapeDtypeStruct(*(s if isinstance(...  7.06 us
    ppermute x5, starting transfers between devices, swap(): return lax.ppermute(block, ('gx', 'gy'), route)  7.06 us
    ppermute x5, waiting for transfers between devices, swap(): return lax.ppermute(block, ('gx', 'gy'), route)  2.96 us
    ppermute x1, waiting for transfers between devices, per_device(): swapped = lax.ppermute(sheet, 'half', [(0, 1), (1, 0)])  2.11 us
    ppermute x1, starting transfers between devices, per_device(): swapped = lax.ppermute(sheet, 'half', [(0, 1), (1, 0)])  1.4 us
  transfers between devices with their start and end apart: 6, of which 3 were waited for; matrix products, arithmetic and copies ran while one was open for 0% of the time, Pallas kernels for 19%

profile of v4, /device:TPU:102, one launch (start us, length us, event | category | flops | bytes accessed | tf_op | source)
XLA Modules:
  0.0 21.3 jit_solution(14913355976244725773)
XLA Ops:
  0.6 1.5 %shard_map.59 = (f32[2,4,8,16,128]{4,3,2,1,0:T(8,128)S(1)}, s32[2,8,16,128]{3,2,1,0:T(8,128)S(1)}, s32[16,256]{1,0:T(8,128)S(1)}, f32[1,16,256]{2,1,0:T(8,128)S(...) custom-call(f32[1,4,8,16,256]{4,3,2,1,0:T(8,128)} %grid.1, s32[1,8,16,256]{3,2,1,0:T(8,128)} %codes.1, ...), custom_call_target="tpu_custom_call" | custom-call | flops 1048576 | bytes 1048576 | tf_op jit(solution)/shard_map/pallas_call | solution.py:46
  2.1 0.1 collective-permute-start
  2.2 0.9 %collective-permute-start.1 = (f32[2,8,128]{2,1,0:T(8,128)S(1)}, f32[2,8,128]{2,1,0:T(8,128)S(1)}, u32[]{:S(2)}, u32[]{:S(2)}) collective-permute-start(f32[2,8,128]{2,1,0:T(8,128)S(1)} %get-tuple-element.31), channel_id=1, source_target_pairs={{0,8},{1,2},{2,1},{3,4},{4,3},{5,6},{6,5},{7,15},{8,0},{9,10},{10,... | collective-permute-start | bytes 24584 | tf_op jit(solution)/shard_map/ppermute | solution.py:637
  3.1 0.2 %shard_map.60 = (f32[7,22,3,8,128]{4,3,2,1,0:T(8,128)S(1)}, f32[25,8,128]{2,1,0:T(8,128)S(1)}, f32[24,8,128]{2,1,0:T(8,128)S(1)}) custom-call(f32[2,4,8,16,128]{4,3,2,1,0:T(8,128)S(1)} %get-tuple-element.25.raw, s32[2,8,16,128]{3,2,1,0:T(8,128)S(1)} %get-tuple-element.26.raw_code, s32[16,256]{1,0:T(8,128)S(1)} %get-tuple-element.27.raw_contact, ...), custom_call_target="tpu_custom_call" | custom-call | flops 1048576 | bytes 1048576 | tf_op jit(solution)/shard_map/pallas_call | solution.py:46
  3.4 3.9 %collective-permute-start.3 = (f32[24,8,128]{2,1,0:T(8,128)S(1)}, f32[24,8,128]{2,1,0:T(8,128)S(1)}, u32[]{:S(2)}, u32[]{:S(2)}) collective-permute-start(f32[24,8,128]{2,1,0:T(8,128)S(1)} %get-tuple-element.38), channel_id=1, source_target_pairs={{0,1},{1,0},{2,3},{3,2},{4,5},{5,4},{6,7},{7,6},{8,16},{9,17},{10,... | collective-permute-start | bytes 294920 | tf_op jit(solution)/shard_map/ppermute | solution.py:637
  7.2 0.0 collective-permute-done.y_first
  7.2 0.0 collective-permute-done.1.y_second
  7.2 0.1 shard_map.62
  7.3 2.2 %collective-permute-start.4 = (f32[8,128]{1,0:T(8,128)S(1)}, f32[8,128]{1,0:T(8,128)S(1)}, u32[]{:S(2)}, u32[]{:S(2)}) collective-permute-start(f32[8,128]{1,0:T(8,128)S(1)} %get-tuple-element.39), channel_id=1, source_target_pairs={{0,1},{1,0},{2,3},{3,2},{4,5},{5,4},{6,7},{7,6},{8,16},{9,17},{10,... | collective-permute-start | bytes 12296 | tf_op jit(solution)/shard_map/ppermute | solution.py:637
  9.6 0.0 collective-permute-start.2
  9.6 1.7 %shard_map.61 = (f32[7,22,3,8,128]{4,3,2,1,0:T(8,128)S(1)}, f32[4,22,3,8,128]{4,3,2,1,0:T(8,128)S(1)}, f32[4,22,3,8,128]{4,3,2,1,0:T(8,128)S(1)}, f32[24,384]{1,0:T(8,128)S(1)}) custom-call(f32[7,22,3,8,128]{4,3,2,1,0:T(8,128)S(1)} %get-tuple-element.29.field_in, f32[2,8,128]{2,1,0:T(8,128)S(1)} %collective-permute-done.y_first, ...), custom_call_target="tpu_custom_call", output_to_operand_aliasing={{0}: (0, {})} | custom-call | flops 10000000000 | bytes 1048576 | tf_op jit(solution)/shard_map/pallas_call | solution.py:46
  11.3 1.9 %collective-permute-done.4.side_second = f32[8,128]{1,0:T(8,128)S(1)} collective-permute-done((f32[8,128]{1,0:T(8,128)S(1)}, f32[8,128]{1,0:T(8,128)S(1)}, u32[]{:S(2)}, u32[]{:S(2)}) %collective-permute-start.4) | collective-permute-done | bytes 4128 | tf_op jit(solution)/shard_map/ppermute | solution.py:637
  13.2 0.0 collective-permute-done.3.x_second
  13.2 1.1 %collective-permute-done.2.x_first = f32[25,8,128]{2,1,0:T(8,128)S(1)} collective-permute-done((f32[25,8,128]{2,1,0:T(8,128)S(1)}, f32[25,8,128]{2,1,0:T(8,128)S(1)}, u32[]{:S(2)}, u32[]{:S(2)}) %collective-permute-start.2) | collective-permute-done | bytes 102432 | tf_op jit(solution)/shard_map/ppermute | solution.py:637
  14.3 0.5 %shard_map.63 = (f32[7,22,3,8,128]{4,3,2,1,0:T(8,128)S(1)}, f32[4,22,3,8,128]{4,3,2,1,0:T(8,128)S(1)}, f32[4,22,3,8,128]{4,3,2,1,0:T(8,128)S(1)}, f32[24,384]{1,0:T(8,128)S(1)}) custom-call(f32[7,22,3,8,128]{4,3,2,1,0:T(8,128)S(1)} %get-tuple-element.32.field_in, ...), custom_call_target="tpu_custom_call", output_to_operand_aliasing={{0}: (0, {}), {1}: (1, {}), {2}: (2, {}), {3}: (3, {})} | custom-call | flops 1048576 | bytes 1048576 | tf_op jit(solution)/shard_map/pallas_call | solution.py:46
  14.8 1.4 %collective-permute-start.5 = (f32[24,384]{1,0:T(8,128)S(1)}, f32[24,384]{1,0:T(8,128)S(1)}, u32[]{:S(2)}, u32[]{:S(2)}) collective-permute-start(f32[24,384]{1,0:T(8,128)S(1)} %get-tuple-element.40), channel_id=1, source_target_pairs={{0,128},{128,0},{1,129},{129,1},{2,130},{130,2},{3,131},{131,3},{4... | collective-permute-start | bytes 110600 | tf_op jit(solution)/shard_map/ppermute | solution.py:683
  16.2 0.0 copy-start
  16.2 2.0 %shard_map.64 = (f32[2,4,8,16,128]{4,3,2,1,0:T(8,128)S(1)}, f32[2,3,8,16,128]{4,3,2,1,0:T(8,128)S(1)}, f32[24,384]{1,0:T(8,128)S(1)}, f32[2,16,256]{2,1,0:T(8,128)S(1)}) custom-call(f32[7,22,3,8,128]{4,3,2,1,0:T(8,128)S(1)} %get-tuple-element.41.field_ref, f32[4,22,3,8,128]{4,3,2,1,0:T(8,128)S(1)} %get-tuple-element.42.next_ref, ...), custom_call_target="tpu_custom_call" | custom-call | flops 8388608 | bytes 1048576 | tf_op jit(solution)/shard_map/pallas_call | solution.py:46
  18.2 2.1 %collective-permute-done.5.sheet_ref = f32[24,384]{1,0:T(8,128)S(1)} collective-permute-done((f32[24,384]{1,0:T(8,128)S(1)}, f32[24,384]{1,0:T(8,128)S(1)}, u32[]{:S(2)}, u32[]{:S(2)}) %collective-permute-start.5) | collective-permute-done | bytes 36896 | tf_op jit(solution)/shard_map/ppermute | solution.py:683
  20.3 0.0 copy-done
  20.3 0.9 %shard_map.65 = (f32[1,4,8,16,256]{4,3,2,1,0:T(8,128)}, f32[1,16,256]{2,1,0:T(8,128)}) custom-call(f32[24,384]{1,0:T(8,128)S(1)} %collective-permute-done.5.sheet_ref, f32[2,4,8,16,128]{4,3,2,1,0:T(8,128)S(1)} %get-tuple-element.44.fixed_ref, f32[2,3,8,16,128]{4,3,2,1,0:T(8,128)S(1)} %get-tuple-element.45.varying_ref, ...), custom_call_target="tpu_custom_call" | custom-call | flops 1048576 | bytes 1048576 | tf_op jit(solution)/shard_map/pallas_call | solution.py:46
Async XLA Ops:
  2.1 5.1 %collective-permute-start = (f32[2,8,128]{2,1,0:T(8,128)S(1)}, f32[2,8,128]{2,1,0:T(8,128)S(1)}, u32[]{:S(2)}, u32[]{:S(2)}) collective-permute-start(f32[2,8,128]{2,1,0:T(8,128)S(1)} %get-tuple-element.30), channel_id=1, source_target_pairs={{0,1},{1,0},{2,3},{3,2},{4,5},{5,4},{6,7},{7,6},{8,9},{9,8},{10,11... | collective-permute-start | bytes 24584 | tf_op jit(solution)/shard_map/ppermute | solution.py:637
  2.2 5.0 %collective-permute-start.1 = (f32[2,8,128]{2,1,0:T(8,128)S(1)}, f32[2,8,128]{2,1,0:T(8,128)S(1)}, u32[]{:S(2)}, u32[]{:S(2)}) collective-permute-start(f32[2,8,128]{2,1,0:T(8,128)S(1)} %get-tuple-element.31), channel_id=1, source_target_pairs={{0,8},{1,2},{2,1},{3,4},{4,3},{5,6},{6,5},{7,15},{8,0},{9,10},{10,... | collective-permute-start | bytes 24584 | tf_op jit(solution)/shard_map/ppermute | solution.py:637
  3.4 9.8 %collective-permute-start.3 = (f32[24,8,128]{2,1,0:T(8,128)S(1)}, f32[24,8,128]{2,1,0:T(8,128)S(1)}, u32[]{:S(2)}, u32[]{:S(2)}) collective-permute-start(f32[24,8,128]{2,1,0:T(8,128)S(1)} %get-tuple-element.38), channel_id=1, source_target_pairs={{0,1},{1,0},{2,3},{3,2},{4,5},{5,4},{6,7},{7,6},{8,16},{9,17},{10,... | collective-permute-start | bytes 294920 | tf_op jit(solution)/shard_map/ppermute | solution.py:637
  7.3 5.8 %collective-permute-start.4 = (f32[8,128]{1,0:T(8,128)S(1)}, f32[8,128]{1,0:T(8,128)S(1)}, u32[]{:S(2)}, u32[]{:S(2)}) collective-permute-start(f32[8,128]{1,0:T(8,128)S(1)} %get-tuple-element.39), channel_id=1, source_target_pairs={{0,1},{1,0},{2,3},{3,2},{4,5},{5,4},{6,7},{7,6},{8,16},{9,17},{10,... | collective-permute-start | bytes 12296 | tf_op jit(solution)/shard_map/ppermute | solution.py:637
  9.6 4.7 %collective-permute-start.2 = (f32[25,8,128]{2,1,0:T(8,128)S(1)}, f32[25,8,128]{2,1,0:T(8,128)S(1)}, u32[]{:S(2)}, u32[]{:S(2)}) collective-permute-start(f32[25,8,128]{2,1,0:T(8,128)S(1)} %get-tuple-element.37), channel_id=1, source_target_pairs={{0,8},{1,9},{2,10},{3,11},{4,12},{5,13},{6,14},{7,15},{8,0},{9,1},... | collective-permute-start | bytes 307208 | tf_op jit(solution)/shard_map/ppermute | solution.py:637
  14.8 5.5 %collective-permute-start.5 = (f32[24,384]{1,0:T(8,128)S(1)}, f32[24,384]{1,0:T(8,128)S(1)}, u32[]{:S(2)}, u32[]{:S(2)}) collective-permute-start(f32[24,384]{1,0:T(8,128)S(1)} %get-tuple-element.40), channel_id=1, source_target_pairs={{0,128},{128,0},{1,129},{129,1},{2,130},{130,2},{3,131},{131,3},{4... | collective-permute-start | bytes 110600 | tf_op jit(solution)/shard_map/ppermute | solution.py:683
  16.2 4.2 %copy-start = (s32[16,256]{1,0:T(8,128)S(1)}, s32[16,256]{1,0:T(8,128)}, u32[]{:S(2)}) copy-start(s32[16,256]{1,0:T(8,128)} %contacts.3) | copy-start | bytes 49156

commit v5 on v4

--- a/solution.py
+++ b/solution.py
@@ -34,7 +34,6 @@
 LOW = [(f, r) for f in range(FIELDS) for r in range(WIDTH[f])]
 HIGH = [(f, TX - WIDTH[f] + r) for f in range(FIELDS) for r in range(WIDTH[f])]
 BULK = sum(1 for f, _ in LOW if f < FREE)
-SIDE = 2 * BULK + 2
 VMEM = pl.BlockSpec(memory_space=pltpu.VMEM)
 HBM = pl.BlockSpec(memory_space=pltpu.HBM)
 SHEET_SHAPE = (24, TILES * LANES)
@@ -228,7 +227,7 @@
     return jnp.where(right[w], a, jnp.where(left[w], b, 0.0))
 
 
-def corner_kernel(first_in, y_first, y_second, first_ref, second_ref):
+def corner_kernel(y_first, y_second, first_ref, second_ref):
     lanes = lane_index()
     gy = lax.axis_index("gy")
     before, after = sides(y_first, y_second, "gy")
@@ -248,7 +247,7 @@
                 v = src[x // 8]
                 both = jnp.where(here, pltpu.roll(v, by, 1) if by else v, both)
         packed.append(both)
-    first_ref[SIDE] = jnp.where(even, packed[1], packed[0])
+    first_ref[...] = jnp.where(even, packed[1], packed[0])
     second_ref[...] = jnp.where(even, packed[0], packed[1])
 
 
@@ -422,7 +421,7 @@
 
 
 def rim_kernel(
-    field_in, next_in, mid_in, sheet_in, x_first, x_second, side_second,
+    field_in, next_in, mid_in, sheet_in, x_first, x_second, side_second, side_first,
     field_ref, next_ref, mid_ref, sheet_ref,
 ):
     lanes = lane_index()
@@ -431,8 +430,8 @@
     has_up = gx > 0
     has_down = gx < lax.axis_size("gx") - 1
     edge = {w: (lanes < w) | (lanes >= LANES - w) for w in (2, 3)}
-    up, down = sides(x_first.at[0:SIDE], x_second, "gx")
-    up_side, down_side = sides(x_first.at[SIDE], side_second, "gx")
+    up, down = sides(x_first, x_second, "gx")
+    up_side, down_side = sides(side_first, side_second, "gx")
     for items, src, packed, ok, base in (
         (HIGH, up, up_side, has_up, FIRST - TX),
         (LOW, down, down_side, has_down, FIRST + TX),
@@ -639,7 +638,7 @@
     tile = (LAYERS, LANES)
     field_shape = (FIELDS, ROWS, TILES) + tile
     state_shape = (4, ROWS, TILES) + tile
-    y_shape = (2,) + tile
+    y_shape, x_shape = (2,) + tile, (2 * BULK + 2,) + tile
     inputs = (grid_state, materials, contacts, received_sheets)
     inputs = [pltpu.with_memory_space_constraint(v, pltpu.HBM) for v in inputs]
     raw_shapes = [
@@ -655,18 +654,14 @@
         specs=[HBM] * 4,
         scratch=[pltpu.SemaphoreType.DMA((12,))],
     )
-    fields, x_first, x_second = call(rows_kernel, [field_shape, (SIDE + 1,) + tile, (SIDE,) + tile], raw)
+    fields, x_first, x_second = call(rows_kernel, [field_shape, x_shape, x_shape], raw)
     y_second = swap(y_second, "gy", 1)
     y_first = swap(y_first, "gy", 0)
     x_second = swap(x_second, "gx", 1)
-    x_first, side_second = call(
-        corner_kernel,
-        [(SIDE + 1,) + tile, tile],
-        [x_first, y_first, y_second],
-        aliases={0: 0},
-    )
+    x_first = swap(x_first, "gx", 0)
+    side_first, side_second = call(corner_kernel, [tile, tile], [y_first, y_second])
     side_second = swap(side_second, "gx", 1)
-    x_first = swap(x_first, "gx", 0)
+    side_first = swap(side_first, "gx", 0)
     fields, following, middle, sheet = call(
         inner_kernel,
         [field_shape, state_shape, state_shape, SHEET_SHAPE],
@@ -677,7 +672,7 @@
     fields, following, middle, sheet = call(
         rim_kernel,
         [field_shape, state_shape, state_shape, SHEET_SHAPE],
-        [fields, following, middle, sheet, x_first, x_second, side_second],
+        [fields, following, middle, sheet, x_first, x_second, side_second, side_first],
         aliases={0: 0, 1: 1, 2: 2, 3: 3},
     )
     swapped = lax.ppermute(sheet, "half", [(0, 1), (1, 0)])

time: 21.4 us -> 21.3 us (level)
  waiting for transfers between devices: 5.07 us -> 4.79 us
    ppermute x5 -> x6, waiting for transfers between devices: 2.96 us -> 2.69 us  [swap(): return lax.ppermute(block, ('gx', 'gy'), route)]
    ppermute x5 -> x6, starting transfers between devices: 7.06 us -> 7.06 us  [swap(): return lax.ppermute(block, ('gx', 'gy'), route)]
  transfers between devices with their start and end apart: 6 -> 7, of which waited for: 3 -> 2; matrix products, arithmetic and copies ran while one was open for 0% -> 0% of each run, Pallas kernels for 19% -> 20%
where the time goes in v5:
time: 21.3 us; the launch traced here: 21 us
  starting transfers between devices  8.47 us (40%)
  Pallas kernels  7.07 us (33%)
  waiting for transfers between devices  4.79 us (22%)
  between operations  0.68 us (3%)
    pallas_call x7, Pallas kernels, call(): pl.pallas_call(kernel, out_shape=[jax.ShapeDtypeStruct(*(s if isinstance(...  7.07 us
    ppermute x6, starting transfers between devices, swap(): return lax.ppermute(block, ('gx', 'gy'), route)  7.06 us
    ppermute x6, waiting for transfers between devices, swap(): return lax.ppermute(block, ('gx', 'gy'), route)  2.69 us
    ppermute x1, waiting for transfers between devices, per_device(): swapped = lax.ppermute(sheet, 'half', [(0, 1), (1, 0)])  2.1 us
    ppermute x1, starting transfers between devices, per_device(): swapped = lax.ppermute(sheet, 'half', [(0, 1), (1, 0)])  1.4 us
  transfers between devices with their start and end apart: 7, of which 2 were waited for; matrix products, arithmetic and copies ran while one was open for 0% of the time, Pallas kernels for 20%

profile of v5, /device:TPU:102, one launch (start us, length us, event | category | flops | bytes accessed | tf_op | source)
XLA Modules:
  0.0 21.0 jit_solution(13276401603178920537)
XLA Ops:
  0.6 1.5 %shard_map.59 = (f32[2,4,8,16,128]{4,3,2,1,0:T(8,128)S(1)}, s32[2,8,16,128]{3,2,1,0:T(8,128)S(1)}, s32[16,256]{1,0:T(8,128)S(1)}, f32[1,16,256]{2,1,0:T(8,128)S(...) custom-call(f32[1,4,8,16,256]{4,3,2,1,0:T(8,128)} %grid.1, s32[1,8,16,256]{3,2,1,0:T(8,128)} %codes.1, ...), custom_call_target="tpu_custom_call" | custom-call | flops 1048576 | bytes 1048576 | tf_op jit(solution)/shard_map/pallas_call | solution.py:45
  2.1 0.1 collective-permute-start
  2.2 0.9 %collective-permute-start.1 = (f32[2,8,128]{2,1,0:T(8,128)S(1)}, f32[2,8,128]{2,1,0:T(8,128)S(1)}, u32[]{:S(2)}, u32[]{:S(2)}) collective-permute-start(f32[2,8,128]{2,1,0:T(8,128)S(1)} %get-tuple-element.31), channel_id=1, source_target_pairs={{0,8},{1,2},{2,1},{3,4},{4,3},{5,6},{6,5},{7,15},{8,0},{9,10},{10,... | collective-permute-start | bytes 24584 | tf_op jit(solution)/shard_map/ppermute | solution.py:636
  3.1 0.2 %shard_map.60 = (f32[7,22,3,8,128]{4,3,2,1,0:T(8,128)S(1)}, f32[24,8,128]{2,1,0:T(8,128)S(1)}, f32[24,8,128]{2,1,0:T(8,128)S(1)}) custom-call(f32[2,4,8,16,128]{4,3,2,1,0:T(8,128)S(1)} %get-tuple-element.25.raw, s32[2,8,16,128]{3,2,1,0:T(8,128)S(1)} %get-tuple-element.26.raw_code, s32[16,256]{1,0:T(8,128)S(1)} %get-tuple-element.27.raw_contact, ...), custom_call_target="tpu_custom_call" | custom-call | flops 1048576 | bytes 1048576 | tf_op jit(solution)/shard_map/pallas_call | solution.py:45
  3.4 1.3 %collective-permute-start.2 = (f32[24,8,128]{2,1,0:T(8,128)S(1)}, f32[24,8,128]{2,1,0:T(8,128)S(1)}, u32[]{:S(2)}, u32[]{:S(2)}) collective-permute-start(f32[24,8,128]{2,1,0:T(8,128)S(1)} %get-tuple-element.36), channel_id=1, source_target_pairs={{0,8},{1,9},{2,10},{3,11},{4,12},{5,13},{6,14},{7,15},{8,0},{9,1},... | collective-permute-start | bytes 294920 | tf_op jit(solution)/shard_map/ppermute | solution.py:636
  4.6 3.4 %collective-permute-start.3 = (f32[24,8,128]{2,1,0:T(8,128)S(1)}, f32[24,8,128]{2,1,0:T(8,128)S(1)}, u32[]{:S(2)}, u32[]{:S(2)}) collective-permute-start(f32[24,8,128]{2,1,0:T(8,128)S(1)} %get-tuple-element.37), channel_id=1, source_target_pairs={{0,1},{1,0},{2,3},{3,2},{4,5},{5,4},{6,7},{7,6},{8,16},{9,17},{10,... | collective-permute-start | bytes 294920 | tf_op jit(solution)/shard_map/ppermute | solution.py:636
  8.0 0.0 collective-permute-done.y_first
  8.0 0.0 collective-permute-done.1.y_second
  8.0 0.1 shard_map.62
  8.2 1.4 %collective-permute-start.4 = (f32[8,128]{1,0:T(8,128)S(1)}, f32[8,128]{1,0:T(8,128)S(1)}, u32[]{:S(2)}, u32[]{:S(2)}) collective-permute-start(f32[8,128]{1,0:T(8,128)S(1)} %get-tuple-element.38), channel_id=1, source_target_pairs={{0,1},{1,0},{2,3},{3,2},{4,5},{5,4},{6,7},{7,6},{8,16},{9,17},{10,... | collective-permute-start | bytes 12296 | tf_op jit(solution)/shard_map/ppermute | solution.py:636
  9.6 0.0 collective-permute-start.5
  9.6 1.7 %shard_map.61 = (f32[7,22,3,8,128]{4,3,2,1,0:T(8,128)S(1)}, f32[4,22,3,8,128]{4,3,2,1,0:T(8,128)S(1)}, f32[4,22,3,8,128]{4,3,2,1,0:T(8,128)S(1)}, f32[24,384]{1,0:T(8,128)S(1)}) custom-call(f32[7,22,3,8,128]{4,3,2,1,0:T(8,128)S(1)} %get-tuple-element.29.field_in, f32[2,8,128]{2,1,0:T(8,128)S(1)} %collective-permute-done.y_first, ...), custom_call_target="tpu_custom_call", output_to_operand_aliasing={{0}: (0, {})} | custom-call | flops 10000000000 | bytes 1048576 | tf_op jit(solution)/shard_map/pallas_call | solution.py:45
  11.3 2.7 %collective-permute-done.4.side_second = f32[8,128]{1,0:T(8,128)S(1)} collective-permute-done((f32[8,128]{1,0:T(8,128)S(1)}, f32[8,128]{1,0:T(8,128)S(1)}, u32[]{:S(2)}, u32[]{:S(2)}) %collective-permute-start.4) | collective-permute-done | bytes 4128 | tf_op jit(solution)/shard_map/ppermute | solution.py:636
  14.0 0.0 collective-permute-done.5.side_first
  14.0 0.0 collective-permute-done.2.x_first
  14.0 0.0 collective-permute-done.3.x_second
  14.0 0.5 %shard_map.63 = (f32[7,22,3,8,128]{4,3,2,1,0:T(8,128)S(1)}, f32[4,22,3,8,128]{4,3,2,1,0:T(8,128)S(1)}, f32[4,22,3,8,128]{4,3,2,1,0:T(8,128)S(1)}, f32[24,384]{1,0:T(8,128)S(1)}) custom-call(f32[7,22,3,8,128]{4,3,2,1,0:T(8,128)S(1)} %get-tuple-element.32.field_in, ...), custom_call_target="tpu_custom_call", output_to_operand_aliasing={{0}: (0, {}), {1}: (1, {}), {2}: (2, {}), {3}: (3, {})} | custom-call | flops 1048576 | bytes 1048576 | tf_op jit(solution)/shard_map/pallas_call | solution.py:45
  14.5 1.4 %collective-permute-start.6 = (f32[24,384]{1,0:T(8,128)S(1)}, f32[24,384]{1,0:T(8,128)S(1)}, u32[]{:S(2)}, u32[]{:S(2)}) collective-permute-start(f32[24,384]{1,0:T(8,128)S(1)} %get-tuple-element.40), channel_id=1, source_target_pairs={{0,128},{128,0},{1,129},{129,1},{2,130},{130,2},{3,131},{131,3},{4... | collective-permute-start | bytes 110600 | tf_op jit(solution)/shard_map/ppermute | solution.py:678
  15.9 0.0 copy-start
  15.9 2.0 %shard_map.64 = (f32[2,4,8,16,128]{4,3,2,1,0:T(8,128)S(1)}, f32[2,3,8,16,128]{4,3,2,1,0:T(8,128)S(1)}, f32[24,384]{1,0:T(8,128)S(1)}, f32[2,16,256]{2,1,0:T(8,128)S(1)}) custom-call(f32[7,22,3,8,128]{4,3,2,1,0:T(8,128)S(1)} %get-tuple-element.41.field_ref, f32[4,22,3,8,128]{4,3,2,1,0:T(8,128)S(1)} %get-tuple-element.42.next_ref, ...), custom_call_target="tpu_custom_call" | custom-call | flops 8388608 | bytes 1048576 | tf_op jit(solution)/shard_map/pallas_call | solution.py:45
  18.0 2.1 %collective-permute-done.6.sheet_ref = f32[24,384]{1,0:T(8,128)S(1)} collective-permute-done((f32[24,384]{1,0:T(8,128)S(1)}, f32[24,384]{1,0:T(8,128)S(1)}, u32[]{:S(2)}, u32[]{:S(2)}) %collective-permute-start.6) | collective-permute-done | bytes 36896 | tf_op jit(solution)/shard_map/ppermute | solution.py:678
  20.1 0.0 copy-done
  20.1 0.9 %shard_map.65 = (f32[1,4,8,16,256]{4,3,2,1,0:T(8,128)}, f32[1,16,256]{2,1,0:T(8,128)}) custom-call(f32[24,384]{1,0:T(8,128)S(1)} %collective-permute-done.6.sheet_ref, f32[2,4,8,16,128]{4,3,2,1,0:T(8,128)S(1)} %get-tuple-element.44.fixed_ref, f32[2,3,8,16,128]{4,3,2,1,0:T(8,128)S(1)} %get-tuple-element.45.varying_ref, ...), custom_call_target="tpu_custom_call" | custom-call | flops 1048576 | bytes 1048576 | tf_op jit(solution)/shard_map/pallas_call | solution.py:45
Async XLA Ops:
  2.1 5.9 %collective-permute-start = (f32[2,8,128]{2,1,0:T(8,128)S(1)}, f32[2,8,128]{2,1,0:T(8,128)S(1)}, u32[]{:S(2)}, u32[]{:S(2)}) collective-permute-start(f32[2,8,128]{2,1,0:T(8,128)S(1)} %get-tuple-element.30), channel_id=1, source_target_pairs={{0,1},{1,0},{2,3},{3,2},{4,5},{5,4},{6,7},{7,6},{8,9},{9,8},{10,11... | collective-permute-start | bytes 24584 | tf_op jit(solution)/shard_map/ppermute | solution.py:636
  2.2 5.8 %collective-permute-start.1 = (f32[2,8,128]{2,1,0:T(8,128)S(1)}, f32[2,8,128]{2,1,0:T(8,128)S(1)}, u32[]{:S(2)}, u32[]{:S(2)}) collective-permute-start(f32[2,8,128]{2,1,0:T(8,128)S(1)} %get-tuple-element.31), channel_id=1, source_target_pairs={{0,8},{1,2},{2,1},{3,4},{4,3},{5,6},{6,5},{7,15},{8,0},{9,10},{10,... | collective-permute-start | bytes 24584 | tf_op jit(solution)/shard_map/ppermute | solution.py:636
  3.4 10.6 %collective-permute-start.2 = (f32[24,8,128]{2,1,0:T(8,128)S(1)}, f32[24,8,128]{2,1,0:T(8,128)S(1)}, u32[]{:S(2)}, u32[]{:S(2)}) collective-permute-start(f32[24,8,128]{2,1,0:T(8,128)S(1)} %get-tuple-element.36), channel_id=1, source_target_pairs={{0,8},{1,9},{2,10},{3,11},{4,12},{5,13},{6,14},{7,15},{8,0},{9,1},... | collective-permute-start | bytes 294920 | tf_op jit(solution)/shard_map/ppermute | solution.py:636
  4.6 9.4 %collective-permute-start.3 = (f32[24,8,128]{2,1,0:T(8,128)S(1)}, f32[24,8,128]{2,1,0:T(8,128)S(1)}, u32[]{:S(2)}, u32[]{:S(2)}) collective-permute-start(f32[24,8,128]{2,1,0:T(8,128)S(1)} %get-tuple-element.37), channel_id=1, source_target_pairs={{0,1},{1,0},{2,3},{3,2},{4,5},{5,4},{6,7},{7,6},{8,16},{9,17},{10,... | collective-permute-start | bytes 294920 | tf_op jit(solution)/shard_map/ppermute | solution.py:636
  8.2 5.8 %collective-permute-start.4 = (f32[8,128]{1,0:T(8,128)S(1)}, f32[8,128]{1,0:T(8,128)S(1)}, u32[]{:S(2)}, u32[]{:S(2)}) collective-permute-start(f32[8,128]{1,0:T(8,128)S(1)} %get-tuple-element.38), channel_id=1, source_target_pairs={{0,1},{1,0},{2,3},{3,2},{4,5},{5,4},{6,7},{7,6},{8,16},{9,17},{10,... | collective-permute-start | bytes 12296 | tf_op jit(solution)/shard_map/ppermute | solution.py:636
  9.6 4.4 %collective-permute-start.5 = (f32[8,128]{1,0:T(8,128)S(1)}, f32[8,128]{1,0:T(8,128)S(1)}, u32[]{:S(2)}, u32[]{:S(2)}) collective-permute-start(f32[8,128]{1,0:T(8,128)S(1)} %get-tuple-element.39), channel_id=1, source_target_pairs={{0,8},{1,9},{2,10},{3,11},{4,12},{5,13},{6,14},{7,15},{8,0},{9,1},... | collective-permute-start | bytes 12296 | tf_op jit(solution)/shard_map/ppermute | solution.py:636
  14.5 5.5 %collective-permute-start.6 = (f32[24,384]{1,0:T(8,128)S(1)}, f32[24,384]{1,0:T(8,128)S(1)}, u32[]{:S(2)}, u32[]{:S(2)}) collective-permute-start(f32[24,384]{1,0:T(8,128)S(1)} %get-tuple-element.40), channel_id=1, source_target_pairs={{0,128},{128,0},{1,129},{129,1},{2,130},{130,2},{3,131},{131,3},{4... | collective-permute-start | bytes 110600 | tf_op jit(solution)/shard_map/ppermute | solution.py:678
  15.9 4.1 %copy-start = (s32[16,256]{1,0:T(8,128)S(1)}, s32[16,256]{1,0:T(8,128)}, u32[]{:S(2)}) copy-start(s32[16,256]{1,0:T(8,128)} %contacts.3) | copy-start | bytes 49156

commit v6 on v5

--- a/solution.py
+++ b/solution.py
@@ -430,7 +430,14 @@
     has_up = gx > 0
     has_down = gx < lax.axis_size("gx") - 1
     edge = {w: (lanes < w) | (lanes >= LANES - w) for w in (2, 3)}
-    up, down = sides(x_first, x_second, "gx")
+    even = is_even("gx")
+
+    def up(n):
+        return jnp.where(even, x_second[n], x_first[n])
+
+    def down(n):
+        return jnp.where(even, x_first[n], x_second[n])
+
     up_side, down_side = sides(side_first, side_second, "gx")
     for items, src, packed, ok, base in (
         (HIGH, up, up_side, has_up, FIRST - TX),
@@ -440,12 +447,12 @@
             for t in range(2):
                 second = x % 2
                 if f < FREE:
-                    v = src[2 * n + t]
+                    v = src(2 * n + t)
                 elif f == FREE:
-                    top = src[2 * BULK + t][second : second + 1, :]
+                    top = src(2 * BULK + t)[second : second + 1, :]
                     v = jnp.where(sub == 0, jnp.broadcast_to(top, (LAYERS, LANES)), 1.0)
                 else:
-                    row = src[2 * BULK + t][4 + 2 * second : 5 + 2 * second, :]
+                    row = src(2 * BULK + t)[4 + 2 * second : 5 + 2 * second, :]
                     v = jnp.broadcast_to(row, (LAYERS, LANES))
                 field_ref[f, base + x, t] = jnp.where(ok, v, 0.0)
             side = pltpu.roll(packed, LANES - 8 * n - 3, 1)
@@ -560,27 +567,28 @@
         copies = [send(fixed_ref, 0, t, every) for t in range(2)]
         for c in copies:
             c.start()
-        for t in range(2):
-            cols = slice(t * LANES, (t + 1) * LANES)
-            s = sheet_ref[0:TX, cols]
-            slow = jnp.exp(-0.6 * s)
-            fast = jnp.exp(0.3 * s)
-            total = jnp.zeros((TX, LANES), F32)
-            for layer in range(LAYERS):
-                for f in (1, 2):
-                    done[t, f, layer] = (
-                        fixed_ref[t, f, layer] - varying_ref[t, f - 1, layer] * fast
-                    )
-                q = varying_ref[t, 2, layer] * slow
-                total = total + q
-                step = 0.8 / 3.5 if 0 < layer < LAYERS - 1 else 0.8 / 3.0
-                if layer == 0:
-                    step = step * (1.0 - contacts[:, cols].astype(F32))
-                done[t, 3, layer] = fixed_ref[t, 3, layer] + step * (q + 0.5 * s)
-            total_ref[0, :, cols] = total
-            for f in (1, 2, 3):
-                copies.append(send(done, f, t, every))
-                copies[-1].start()
+        s = sheet_ref[0:TX, 0 : 2 * LANES]
+        slow = jnp.exp(-0.6 * s)
+        fast = jnp.exp(0.3 * s)
+        for f in (1, 2, 3):
+            for t in range(2):
+                cols = slice(t * LANES, (t + 1) * LANES)
+                total = jnp.zeros((TX, LANES), F32)
+                for layer in range(LAYERS):
+                    fixed, varying = fixed_ref[t, f, layer], varying_ref[t, f - 1, layer]
+                    if f < 3:
+                        done[f, layer, :, cols] = fixed - varying * fast[:, cols]
+                        continue
+                    q = varying * slow[:, cols]
+                    total = total + q
+                    step = 0.8 / 3.5 if 0 < layer < LAYERS - 1 else 0.8 / 3.0
+                    if layer == 0:
+                        step = step * (1.0 - contacts[:, cols].astype(F32))
+                    done[f, layer, :, cols] = fixed + step * (q + 0.5 * s[:, cols])
+                if f == 3:
+                    total_ref[0, :, cols] = total
+            copies.append(pltpu.make_async_copy(done.at[f], state_out.at[0, f], sem.at[f, 0]))
+            copies[-1].start()
         copies.append(pltpu.make_async_copy(total_ref, sheet_out, sem.at[8, 0]))
         copies[-1].start()
         for c in copies:
@@ -597,22 +605,23 @@
         by_x = (delta[0:TX, :], delta[2 : TX + 2, :])
         by_y = (prev_lane(middle), next_lane(middle))
         more = []
-        for t in range(2):
-            cols = slice(t * LANES, (t + 1) * LANES)
-            mid = middle[:, cols]
-            total = jnp.zeros((TX, LANES), F32)
-            for f in range(4):
+        totals = [jnp.zeros((TX, LANES), F32)] * 2
+        for f in range(4):
+            for t in range(2):
+                cols = slice(t * LANES, (t + 1) * LANES)
+                mid = middle[:, cols]
                 around = 2.0 * mid + by_x[f // 2][:, cols] + by_y[f % 2][:, cols]
                 value = fixed_ref[t, f, 0] + 1.1 * mid + spread_ref[0, :, cols] * around
-                done[t, f, 0] = value
-                total = total + value
-                done[t, f, 1] = fixed_ref[t, f, 1] + spread_ref[1, :, cols] * mid
-                dst = state_out.at[0, f, pl.ds(0, 2), :, pl.ds(t * LANES, LANES)]
-                more.append(
-                    pltpu.make_async_copy(done.at[t, f, pl.ds(0, 2)], dst, sem.at[4 + f, t])
-                )
-                more[-1].start()
-            total_ref[0, :, cols] = 0.25 * total
+                done[f, 0, :, cols] = value
+                totals[t] = totals[t] + value
+                done[f, 1, :, cols] = fixed_ref[t, f, 1] + spread_ref[1, :, cols] * mid
+            two = pl.ds(0, 2)
+            more.append(
+                pltpu.make_async_copy(done.at[f, two], state_out.at[0, f, two], sem.at[4 + f, 0])
+            )
+            more[-1].start()
+        for t in range(2):
+            total_ref[0, :, t * LANES : (t + 1) * LANES] = 0.25 * totals[t]
         more.append(pltpu.make_async_copy(total_ref, sheet_out, sem.at[8, 0]))
         more[-1].start()
         for c in copies + more:
@@ -694,7 +703,7 @@
         [swapped, fixed, varying, source, spread, contacts],
         out_specs=[HBM, HBM],
         scratch=[
-            pltpu.VMEM((2, 4, LAYERS, TX, LANES), F32),
+            pltpu.VMEM((4, LAYERS, TX, 2 * LANES), F32),
             pltpu.VMEM((1, TX, 2 * LANES), F32),
             pltpu.VMEM(SHEET_SHAPE, F32),
             pltpu.SemaphoreType.DMA((9, 2)),

time: 21.3 us -> 21.3 us (level)
  no operation moved by 1% of the time
where the time goes in v6:
time: 21.3 us; the launch traced here: 21 us
  starting transfers between devices  8.46 us (40%)
  Pallas kernels  7.07 us (33%)
  waiting for transfers between devices  4.8 us (23%)
  between operations  0.68 us (3%)
    pallas_call x7, Pallas kernels, call(): pl.pallas_call(kernel, out_shape=[jax.ShapeDtypeStruct(*(s if isinstance(...  7.07 us
    ppermute x6, starting transfers between devices, swap(): return lax.ppermute(block, ('gx', 'gy'), route)  7.06 us
    ppermute x6, waiting for transfers between devices, swap(): return lax.ppermute(block, ('gx', 'gy'), route)  2.69 us
    ppermute x1, waiting for transfers between devices, per_device(): swapped = lax.ppermute(sheet, 'half', [(0, 1), (1, 0)])  2.11 us
    ppermute x1, starting transfers between devices, per_device(): swapped = lax.ppermute(sheet, 'half', [(0, 1), (1, 0)])  1.4 us
  transfers between devices with their start and end apart: 7, of which 2 were waited for; matrix products, arithmetic and copies ran while one was open for 0% of the time, Pallas kernels for 20%

profile of v6, /device:TPU:102, one launch (start us, length us, event | category | flops | bytes accessed | tf_op | source)
XLA Modules:
  0.0 21.0 jit_solution(4699206317450295162)
XLA Ops:
  0.6 1.5 %shard_map.59 = (f32[2,4,8,16,128]{4,3,2,1,0:T(8,128)S(1)}, s32[2,8,16,128]{3,2,1,0:T(8,128)S(1)}, s32[16,256]{1,0:T(8,128)S(1)}, f32[1,16,256]{2,1,0:T(8,128)S(...) custom-call(f32[1,4,8,16,256]{4,3,2,1,0:T(8,128)} %grid.1, s32[1,8,16,256]{3,2,1,0:T(8,128)} %codes.1, ...), custom_call_target="tpu_custom_call" | custom-call | flops 1048576 | bytes 1048576 | tf_op jit(solution)/shard_map/pallas_call | solution.py:45
  2.1 0.1 collective-permute-start
  2.2 0.9 %collective-permute-start.1 = (f32[2,8,128]{2,1,0:T(8,128)S(1)}, f32[2,8,128]{2,1,0:T(8,128)S(1)}, u32[]{:S(2)}, u32[]{:S(2)}) collective-permute-start(f32[2,8,128]{2,1,0:T(8,128)S(1)} %get-tuple-element.31), channel_id=1, source_target_pairs={{0,8},{1,2},{2,1},{3,4},{4,3},{5,6},{6,5},{7,15},{8,0},{9,10},{10,... | collective-permute-start | bytes 24584 | tf_op jit(solution)/shard_map/ppermute | solution.py:645
  3.1 0.2 %shard_map.60 = (f32[7,22,3,8,128]{4,3,2,1,0:T(8,128)S(1)}, f32[24,8,128]{2,1,0:T(8,128)S(1)}, f32[24,8,128]{2,1,0:T(8,128)S(1)}) custom-call(f32[2,4,8,16,128]{4,3,2,1,0:T(8,128)S(1)} %get-tuple-element.25.raw, s32[2,8,16,128]{3,2,1,0:T(8,128)S(1)} %get-tuple-element.26.raw_code, s32[16,256]{1,0:T(8,128)S(1)} %get-tuple-element.27.raw_contact, ...), custom_call_target="tpu_custom_call" | custom-call | flops 1048576 | bytes 1048576 | tf_op jit(solution)/shard_map/pallas_call | solution.py:45
  3.4 1.3 %collective-permute-start.2 = (f32[24,8,128]{2,1,0:T(8,128)S(1)}, f32[24,8,128]{2,1,0:T(8,128)S(1)}, u32[]{:S(2)}, u32[]{:S(2)}) collective-permute-start(f32[24,8,128]{2,1,0:T(8,128)S(1)} %get-tuple-element.36), channel_id=1, source_target_pairs={{0,8},{1,9},{2,10},{3,11},{4,12},{5,13},{6,14},{7,15},{8,0},{9,1},... | collective-permute-start | bytes 294920 | tf_op jit(solution)/shard_map/ppermute | solution.py:645
  4.6 3.4 %collective-permute-start.3 = (f32[24,8,128]{2,1,0:T(8,128)S(1)}, f32[24,8,128]{2,1,0:T(8,128)S(1)}, u32[]{:S(2)}, u32[]{:S(2)}) collective-permute-start(f32[24,8,128]{2,1,0:T(8,128)S(1)} %get-tuple-element.37), channel_id=1, source_target_pairs={{0,1},{1,0},{2,3},{3,2},{4,5},{5,4},{6,7},{7,6},{8,16},{9,17},{10,... | collective-permute-start | bytes 294920 | tf_op jit(solution)/shard_map/ppermute | solution.py:645
  8.0 0.0 collective-permute-done.y_first
  8.0 0.0 collective-permute-done.1.y_second
  8.0 0.1 shard_map.62
  8.2 1.4 %collective-permute-start.4 = (f32[8,128]{1,0:T(8,128)S(1)}, f32[8,128]{1,0:T(8,128)S(1)}, u32[]{:S(2)}, u32[]{:S(2)}) collective-permute-start(f32[8,128]{1,0:T(8,128)S(1)} %get-tuple-element.38), channel_id=1, source_target_pairs={{0,1},{1,0},{2,3},{3,2},{4,5},{5,4},{6,7},{7,6},{8,16},{9,17},{10,... | collective-permute-start | bytes 12296 | tf_op jit(solution)/shard_map/ppermute | solution.py:645
  9.6 0.0 collective-permute-start.5
  9.6 1.7 %shard_map.61 = (f32[7,22,3,8,128]{4,3,2,1,0:T(8,128)S(1)}, f32[4,22,3,8,128]{4,3,2,1,0:T(8,128)S(1)}, f32[4,22,3,8,128]{4,3,2,1,0:T(8,128)S(1)}, f32[24,384]{1,0:T(8,128)S(1)}) custom-call(f32[7,22,3,8,128]{4,3,2,1,0:T(8,128)S(1)} %get-tuple-element.29.field_in, f32[2,8,128]{2,1,0:T(8,128)S(1)} %collective-permute-done.y_first, ...), custom_call_target="tpu_custom_call", output_to_operand_aliasing={{0}: (0, {})} | custom-call | flops 10000000000 | bytes 1048576 | tf_op jit(solution)/shard_map/pallas_call | solution.py:45
  11.3 2.7 %collective-permute-done.4.side_second = f32[8,128]{1,0:T(8,128)S(1)} collective-permute-done((f32[8,128]{1,0:T(8,128)S(1)}, f32[8,128]{1,0:T(8,128)S(1)}, u32[]{:S(2)}, u32[]{:S(2)}) %collective-permute-start.4) | collective-permute-done | bytes 4128 | tf_op jit(solution)/shard_map/ppermute | solution.py:645
  14.0 0.0 collective-permute-done.5.side_first
  14.0 0.0 collective-permute-done.2.x_first
  14.0 0.0 collective-permute-done.3.x_second
  14.0 0.5 %shard_map.63 = (f32[7,22,3,8,128]{4,3,2,1,0:T(8,128)S(1)}, f32[4,22,3,8,128]{4,3,2,1,0:T(8,128)S(1)}, f32[4,22,3,8,128]{4,3,2,1,0:T(8,128)S(1)}, f32[24,384]{1,0:T(8,128)S(1)}) custom-call(f32[7,22,3,8,128]{4,3,2,1,0:T(8,128)S(1)} %get-tuple-element.32.field_in, ...), custom_call_target="tpu_custom_call", output_to_operand_aliasing={{0}: (0, {}), {1}: (1, {}), {2}: (2, {}), {3}: (3, {})} | custom-call | flops 1048576 | bytes 1048576 | tf_op jit(solution)/shard_map/pallas_call | solution.py:45
  14.5 1.4 %collective-permute-start.6 = (f32[24,384]{1,0:T(8,128)S(1)}, f32[24,384]{1,0:T(8,128)S(1)}, u32[]{:S(2)}, u32[]{:S(2)}) collective-permute-start(f32[24,384]{1,0:T(8,128)S(1)} %get-tuple-element.40), channel_id=1, source_target_pairs={{0,128},{128,0},{1,129},{129,1},{2,130},{130,2},{3,131},{131,3},{4... | collective-permute-start | bytes 110600 | tf_op jit(solution)/shard_map/ppermute | solution.py:687
  15.9 0.0 copy-start
  15.9 2.0 %shard_map.64 = (f32[2,4,8,16,128]{4,3,2,1,0:T(8,128)S(1)}, f32[2,3,8,16,128]{4,3,2,1,0:T(8,128)S(1)}, f32[24,384]{1,0:T(8,128)S(1)}, f32[2,16,256]{2,1,0:T(8,128)S(1)}) custom-call(f32[7,22,3,8,128]{4,3,2,1,0:T(8,128)S(1)} %get-tuple-element.41.field_ref, f32[4,22,3,8,128]{4,3,2,1,0:T(8,128)S(1)} %get-tuple-element.42.next_ref, ...), custom_call_target="tpu_custom_call" | custom-call | flops 8388608 | bytes 1048576 | tf_op jit(solution)/shard_map/pallas_call | solution.py:45
  18.0 2.1 %collective-permute-done.6.sheet_ref = f32[24,384]{1,0:T(8,128)S(1)} collective-permute-done((f32[24,384]{1,0:T(8,128)S(1)}, f32[24,384]{1,0:T(8,128)S(1)}, u32[]{:S(2)}, u32[]{:S(2)}) %collective-permute-start.6) | collective-permute-done | bytes 36896 | tf_op jit(solution)/shard_map/ppermute | solution.py:687
  20.1 0.0 copy-done
  20.1 0.9 %shard_map.65 = (f32[1,4,8,16,256]{4,3,2,1,0:T(8,128)}, f32[1,16,256]{2,1,0:T(8,128)}) custom-call(f32[24,384]{1,0:T(8,128)S(1)} %collective-permute-done.6.sheet_ref, f32[2,4,8,16,128]{4,3,2,1,0:T(8,128)S(1)} %get-tuple-element.44.fixed_ref, f32[2,3,8,16,128]{4,3,2,1,0:T(8,128)S(1)} %get-tuple-element.45.varying_ref, ...), custom_call_target="tpu_custom_call" | custom-call | flops 1048576 | bytes 1048576 | tf_op jit(solution)/shard_map/pallas_call | solution.py:45
Async XLA Ops:
  2.1 5.9 %collective-permute-start = (f32[2,8,128]{2,1,0:T(8,128)S(1)}, f32[2,8,128]{2,1,0:T(8,128)S(1)}, u32[]{:S(2)}, u32[]{:S(2)}) collective-permute-start(f32[2,8,128]{2,1,0:T(8,128)S(1)} %get-tuple-element.30), channel_id=1, source_target_pairs={{0,1},{1,0},{2,3},{3,2},{4,5},{5,4},{6,7},{7,6},{8,9},{9,8},{10,11... | collective-permute-start | bytes 24584 | tf_op jit(solution)/shard_map/ppermute | solution.py:645
  2.2 5.8 %collective-permute-start.1 = (f32[2,8,128]{2,1,0:T(8,128)S(1)}, f32[2,8,128]{2,1,0:T(8,128)S(1)}, u32[]{:S(2)}, u32[]{:S(2)}) collective-permute-start(f32[2,8,128]{2,1,0:T(8,128)S(1)} %get-tuple-element.31), channel_id=1, source_target_pairs={{0,8},{1,2},{2,1},{3,4},{4,3},{5,6},{6,5},{7,15},{8,0},{9,10},{10,... | collective-permute-start | bytes 24584 | tf_op jit(solution)/shard_map/ppermute | solution.py:645
  3.4 10.6 %collective-permute-start.2 = (f32[24,8,128]{2,1,0:T(8,128)S(1)}, f32[24,8,128]{2,1,0:T(8,128)S(1)}, u32[]{:S(2)}, u32[]{:S(2)}) collective-permute-start(f32[24,8,128]{2,1,0:T(8,128)S(1)} %get-tuple-element.36), channel_id=1, source_target_pairs={{0,8},{1,9},{2,10},{3,11},{4,12},{5,13},{6,14},{7,15},{8,0},{9,1},... | collective-permute-start | bytes 294920 | tf_op jit(solution)/shard_map/ppermute | solution.py:645
  4.6 9.4 %collective-permute-start.3 = (f32[24,8,128]{2,1,0:T(8,128)S(1)}, f32[24,8,128]{2,1,0:T(8,128)S(1)}, u32[]{:S(2)}, u32[]{:S(2)}) collective-permute-start(f32[24,8,128]{2,1,0:T(8,128)S(1)} %get-tuple-element.37), channel_id=1, source_target_pairs={{0,1},{1,0},{2,3},{3,2},{4,5},{5,4},{6,7},{7,6},{8,16},{9,17},{10,... | collective-permute-start | bytes 294920 | tf_op jit(solution)/shard_map/ppermute | solution.py:645
  8.2 5.8 %collective-permute-start.4 = (f32[8,128]{1,0:T(8,128)S(1)}, f32[8,128]{1,0:T(8,128)S(1)}, u32[]{:S(2)}, u32[]{:S(2)}) collective-permute-start(f32[8,128]{1,0:T(8,128)S(1)} %get-tuple-element.38), channel_id=1, source_target_pairs={{0,1},{1,0},{2,3},{3,2},{4,5},{5,4},{6,7},{7,6},{8,16},{9,17},{10,... | collective-permute-start | bytes 12296 | tf_op jit(solution)/shard_map/ppermute | solution.py:645
  9.6 4.4 %collective-permute-start.5 = (f32[8,128]{1,0:T(8,128)S(1)}, f32[8,128]{1,0:T(8,128)S(1)}, u32[]{:S(2)}, u32[]{:S(2)}) collective-permute-start(f32[8,128]{1,0:T(8,128)S(1)} %get-tuple-element.39), channel_id=1, source_target_pairs={{0,8},{1,9},{2,10},{3,11},{4,12},{5,13},{6,14},{7,15},{8,0},{9,1},... | collective-permute-start | bytes 12296 | tf_op jit(solution)/shard_map/ppermute | solution.py:645
  14.5 5.5 %collective-permute-start.6 = (f32[24,384]{1,0:T(8,128)S(1)}, f32[24,384]{1,0:T(8,128)S(1)}, u32[]{:S(2)}, u32[]{:S(2)}) collective-permute-start(f32[24,384]{1,0:T(8,128)S(1)} %get-tuple-element.40), channel_id=1, source_target_pairs={{0,128},{128,0},{1,129},{129,1},{2,130},{130,2},{3,131},{131,3},{4... | collective-permute-start | bytes 110600 | tf_op jit(solution)/shard_map/ppermute | solution.py:687
  15.9 4.2 %copy-start = (s32[16,256]{1,0:T(8,128)S(1)}, s32[16,256]{1,0:T(8,128)}, u32[]{:S(2)}) copy-start(s32[16,256]{1,0:T(8,128)} %contacts.3) | copy-start | bytes 49156

commit v7 on v5

--- a/solution.py
+++ b/solution.py
@@ -227,7 +227,7 @@
     return jnp.where(right[w], a, jnp.where(left[w], b, 0.0))
 
 
-def corner_kernel(y_first, y_second, first_ref, second_ref):
+def corner_kernel(y_second, y_first, first_ref, second_ref):
     lanes = lane_index()
     gy = lax.axis_index("gy")
     before, after = sides(y_first, y_second, "gy")
@@ -382,7 +382,7 @@
     return 0.25 * total[0:1, :]
 
 
-def inner_kernel(field_in, y_first, y_second, field_ref, next_ref, mid_ref, sheet_ref):
+def inner_kernel(field_in, y_second, y_first, field_ref, next_ref, mid_ref, sheet_ref):
     lanes = lane_index()
     masks = y_masks(lanes)
     before, after = sides(y_first, y_second, "gy")
@@ -659,13 +659,13 @@
     y_first = swap(y_first, "gy", 0)
     x_second = swap(x_second, "gx", 1)
     x_first = swap(x_first, "gx", 0)
-    side_first, side_second = call(corner_kernel, [tile, tile], [y_first, y_second])
+    side_first, side_second = call(corner_kernel, [tile, tile], [y_second, y_first])
     side_second = swap(side_second, "gx", 1)
     side_first = swap(side_first, "gx", 0)
     fields, following, middle, sheet = call(
         inner_kernel,
         [field_shape, state_shape, state_shape, SHEET_SHAPE],
-        [fields, y_first, y_second],
+        [fields, y_second, y_first],
         aliases={0: 0},
         cost=INNER,
     )

time: 21.3 us -> 22.1 us (1.038)
  waiting for transfers between devices: 4.79 us -> 5.57 us
    ppermute x6, waiting for transfers between devices: 2.69 us -> 3.66 us  [swap(): return lax.ppermute(block, ('gx', 'gy'), route)]
  transfers between devices with their start and end apart: 7 -> 7, of which waited for: 2 -> 2; matrix products, arithmetic and copies ran while one was open for 0% -> 0% of each run, Pallas kernels for 20% -> 19%
where the time goes in v7:
time: 22.1 us; the launch traced here: 21.9 us
  starting transfers between devices  8.57 us (39%)
  Pallas kernels  7.07 us (32%)
  waiting for transfers between devices  5.57 us (25%)
  between operations  0.67 us (3%)
    pallas_call x7, Pallas kernels, call(): pl.pallas_call(kernel, out_shape=[jax.ShapeDtypeStruct(*(s if isinstance(...  7.07 us
    ppermute x6, starting transfers between devices, swap(): return lax.ppermute(block, ('gx', 'gy'), route)  6.97 us
    ppermute x6, waiting for transfers between devices, swap(): return lax.ppermute(block, ('gx', 'gy'), route)  3.66 us
    ppermute x1, waiting for transfers between devices, per_device(): swapped = lax.ppermute(sheet, 'half', [(0, 1), (1, 0)])  1.91 us
    ppermute x1, starting transfers between devices, per_device(): swapped = lax.ppermute(sheet, 'half', [(0, 1), (1, 0)])  1.59 us
  transfers between devices with their start and end apart: 7, of which 2 were waited for; matrix products, arithmetic and copies ran while one was open for 0% of the time, Pallas kernels for 19%

profile of v7, /device:TPU:102, one launch (start us, length us, event | category | flops | bytes accessed | tf_op | source)
XLA Modules:
  0.0 21.9 jit_solution(6653061076931941726)
XLA Ops:
  0.6 1.5 %shard_map.59 = (f32[2,4,8,16,128]{4,3,2,1,0:T(8,128)S(1)}, s32[2,8,16,128]{3,2,1,0:T(8,128)S(1)}, s32[16,256]{1,0:T(8,128)S(1)}, f32[1,16,256]{2,1,0:T(8,128)S(...) custom-call(f32[1,4,8,16,256]{4,3,2,1,0:T(8,128)} %grid.1, s32[1,8,16,256]{3,2,1,0:T(8,128)} %codes.1, ...), custom_call_target="tpu_custom_call" | custom-call | flops 1048576 | bytes 1048576 | tf_op jit(solution)/shard_map/pallas_call | solution.py:45
  2.1 0.9 %collective-permute-start = (f32[2,8,128]{2,1,0:T(8,128)S(1)}, f32[2,8,128]{2,1,0:T(8,128)S(1)}, u32[]{:S(2)}, u32[]{:S(2)}) collective-permute-start(f32[2,8,128]{2,1,0:T(8,128)S(1)} %get-tuple-element.30), channel_id=1, source_target_pairs={{0,8},{1,2},{2,1},{3,4},{4,3},{5,6},{6,5},{7,15},{8,0},{9,10},{10,... | collective-permute-start | bytes 24584 | tf_op jit(solution)/shard_map/ppermute | solution.py:636
  3.0 0.9 %collective-permute-start.1 = (f32[2,8,128]{2,1,0:T(8,128)S(1)}, f32[2,8,128]{2,1,0:T(8,128)S(1)}, u32[]{:S(2)}, u32[]{:S(2)}) collective-permute-start(f32[2,8,128]{2,1,0:T(8,128)S(1)} %get-tuple-element.31), channel_id=1, source_target_pairs={{0,1},{1,0},{2,3},{3,2},{4,5},{5,4},{6,7},{7,6},{8,9},{9,8},{10,11... | collective-permute-start | bytes 24584 | tf_op jit(solution)/shard_map/ppermute | solution.py:636
  3.9 0.2 %shard_map.60 = (f32[7,22,3,8,128]{4,3,2,1,0:T(8,128)S(1)}, f32[24,8,128]{2,1,0:T(8,128)S(1)}, f32[24,8,128]{2,1,0:T(8,128)S(1)}) custom-call(f32[2,4,8,16,128]{4,3,2,1,0:T(8,128)S(1)} %get-tuple-element.25.raw, s32[2,8,16,128]{3,2,1,0:T(8,128)S(1)} %get-tuple-element.26.raw_code, s32[16,256]{1,0:T(8,128)S(1)} %get-tuple-element.27.raw_contact, ...), custom_call_target="tpu_custom_call" | custom-call | flops 1048576 | bytes 1048576 | tf_op jit(solution)/shard_map/pallas_call | solution.py:45
  4.1 0.9 %collective-permute-start.2 = (f32[24,8,128]{2,1,0:T(8,128)S(1)}, f32[24,8,128]{2,1,0:T(8,128)S(1)}, u32[]{:S(2)}, u32[]{:S(2)}) collective-permute-start(f32[24,8,128]{2,1,0:T(8,128)S(1)} %get-tuple-element.36), channel_id=1, source_target_pairs={{0,8},{1,9},{2,10},{3,11},{4,12},{5,13},{6,14},{7,15},{8,0},{9,1},... | collective-permute-start | bytes 294920 | tf_op jit(solution)/shard_map/ppermute | solution.py:636
  5.0 3.8 %collective-permute-start.3 = (f32[24,8,128]{2,1,0:T(8,128)S(1)}, f32[24,8,128]{2,1,0:T(8,128)S(1)}, u32[]{:S(2)}, u32[]{:S(2)}) collective-permute-start(f32[24,8,128]{2,1,0:T(8,128)S(1)} %get-tuple-element.37), channel_id=1, source_target_pairs={{0,1},{1,0},{2,3},{3,2},{4,5},{5,4},{6,7},{7,6},{8,16},{9,17},{10,... | collective-permute-start | bytes 294920 | tf_op jit(solution)/shard_map/ppermute | solution.py:636
  8.8 0.0 collective-permute-done.y_second
  8.8 0.0 collective-permute-done.1.y_first
  8.8 0.1 shard_map.62
  8.9 0.5 %collective-permute-start.4 = (f32[8,128]{1,0:T(8,128)S(1)}, f32[8,128]{1,0:T(8,128)S(1)}, u32[]{:S(2)}, u32[]{:S(2)}) collective-permute-start(f32[8,128]{1,0:T(8,128)S(1)} %get-tuple-element.38), channel_id=1, source_target_pairs={{0,1},{1,0},{2,3},{3,2},{4,5},{5,4},{6,7},{7,6},{8,16},{9,17},{10,... | collective-permute-start | bytes 12296 | tf_op jit(solution)/shard_map/ppermute | solution.py:636
  9.5 0.0 collective-permute-start.5
  9.5 1.7 %shard_map.61 = (f32[7,22,3,8,128]{4,3,2,1,0:T(8,128)S(1)}, f32[4,22,3,8,128]{4,3,2,1,0:T(8,128)S(1)}, f32[4,22,3,8,128]{4,3,2,1,0:T(8,128)S(1)}, f32[24,384]{1,0:T(8,128)S(1)}) custom-call(f32[7,22,3,8,128]{4,3,2,1,0:T(8,128)S(1)} %get-tuple-element.29.field_in, f32[2,8,128]{2,1,0:T(8,128)S(1)} %collective-permute-done.y_second, ...), custom_call_target="tpu_custom_call", output_to_operand_aliasing={{0}: (0, {})} | custom-call | flops 10000000000 | bytes 1048576 | tf_op jit(solution)/shard_map/pallas_call | solution.py:45
  11.2 3.6 %collective-permute-done.4.side_second = f32[8,128]{1,0:T(8,128)S(1)} collective-permute-done((f32[8,128]{1,0:T(8,128)S(1)}, f32[8,128]{1,0:T(8,128)S(1)}, u32[]{:S(2)}, u32[]{:S(2)}) %collective-permute-start.4) | collective-permute-done | bytes 4128 | tf_op jit(solution)/shard_map/ppermute | solution.py:636
  14.8 0.0 collective-permute-done.5.side_first
  14.9 0.0 collective-permute-done.2.x_first
  14.9 0.0 collective-permute-done.3.x_second
  14.9 0.5 %shard_map.63 = (f32[7,22,3,8,128]{4,3,2,1,0:T(8,128)S(1)}, f32[4,22,3,8,128]{4,3,2,1,0:T(8,128)S(1)}, f32[4,22,3,8,128]{4,3,2,1,0:T(8,128)S(1)}, f32[24,384]{1,0:T(8,128)S(1)}) custom-call(f32[7,22,3,8,128]{4,3,2,1,0:T(8,128)S(1)} %get-tuple-element.32.field_in, ...), custom_call_target="tpu_custom_call", output_to_operand_aliasing={{0}: (0, {}), {1}: (1, {}), {2}: (2, {}), {3}: (3, {})} | custom-call | flops 1048576 | bytes 1048576 | tf_op jit(solution)/shard_map/pallas_call | solution.py:45
  15.4 1.6 %collective-permute-start.6 = (f32[24,384]{1,0:T(8,128)S(1)}, f32[24,384]{1,0:T(8,128)S(1)}, u32[]{:S(2)}, u32[]{:S(2)}) collective-permute-start(f32[24,384]{1,0:T(8,128)S(1)} %get-tuple-element.40), channel_id=1, source_target_pairs={{0,128},{128,0},{1,129},{129,1},{2,130},{130,2},{3,131},{131,3},{4... | collective-permute-start | bytes 110600 | tf_op jit(solution)/shard_map/ppermute | solution.py:678
  17.0 0.0 copy-start
  17.0 2.0 %shard_map.64 = (f32[2,4,8,16,128]{4,3,2,1,0:T(8,128)S(1)}, f32[2,3,8,16,128]{4,3,2,1,0:T(8,128)S(1)}, f32[24,384]{1,0:T(8,128)S(1)}, f32[2,16,256]{2,1,0:T(8,128)S(1)}) custom-call(f32[7,22,3,8,128]{4,3,2,1,0:T(8,128)S(1)} %get-tuple-element.41.field_ref, f32[4,22,3,8,128]{4,3,2,1,0:T(8,128)S(1)} %get-tuple-element.42.next_ref, ...), custom_call_target="tpu_custom_call" | custom-call | flops 8388608 | bytes 1048576 | tf_op jit(solution)/shard_map/pallas_call | solution.py:45
  19.0 1.9 %collective-permute-done.6.sheet_ref = f32[24,384]{1,0:T(8,128)S(1)} collective-permute-done((f32[24,384]{1,0:T(8,128)S(1)}, f32[24,384]{1,0:T(8,128)S(1)}, u32[]{:S(2)}, u32[]{:S(2)}) %collective-permute-start.6) | collective-permute-done | bytes 36896 | tf_op jit(solution)/shard_map/ppermute | solution.py:678
  20.9 0.0 copy-done
  20.9 0.9 %shard_map.65 = (f32[1,4,8,16,256]{4,3,2,1,0:T(8,128)}, f32[1,16,256]{2,1,0:T(8,128)}) custom-call(f32[24,384]{1,0:T(8,128)S(1)} %collective-permute-done.6.sheet_ref, f32[2,4,8,16,128]{4,3,2,1,0:T(8,128)S(1)} %get-tuple-element.44.fixed_ref, f32[2,3,8,16,128]{4,3,2,1,0:T(8,128)S(1)} %get-tuple-element.45.varying_ref, ...), custom_call_target="tpu_custom_call" | custom-call | flops 1048576 | bytes 1048576 | tf_op jit(solution)/shard_map/pallas_call | solution.py:45
Async XLA Ops:
  2.1 6.7 %collective-permute-start = (f32[2,8,128]{2,1,0:T(8,128)S(1)}, f32[2,8,128]{2,1,0:T(8,128)S(1)}, u32[]{:S(2)}, u32[]{:S(2)}) collective-permute-start(f32[2,8,128]{2,1,0:T(8,128)S(1)} %get-tuple-element.30), channel_id=1, source_target_pairs={{0,8},{1,2},{2,1},{3,4},{4,3},{5,6},{6,5},{7,15},{8,0},{9,10},{10,... | collective-permute-start | bytes 24584 | tf_op jit(solution)/shard_map/ppermute | solution.py:636
  3.0 5.8 %collective-permute-start.1 = (f32[2,8,128]{2,1,0:T(8,128)S(1)}, f32[2,8,128]{2,1,0:T(8,128)S(1)}, u32[]{:S(2)}, u32[]{:S(2)}) collective-permute-start(f32[2,8,128]{2,1,0:T(8,128)S(1)} %get-tuple-element.31), channel_id=1, source_target_pairs={{0,1},{1,0},{2,3},{3,2},{4,5},{5,4},{6,7},{7,6},{8,9},{9,8},{10,11... | collective-permute-start | bytes 24584 | tf_op jit(solution)/shard_map/ppermute | solution.py:636
  4.1 10.7 %collective-permute-start.2 = (f32[24,8,128]{2,1,0:T(8,128)S(1)}, f32[24,8,128]{2,1,0:T(8,128)S(1)}, u32[]{:S(2)}, u32[]{:S(2)}) collective-permute-start(f32[24,8,128]{2,1,0:T(8,128)S(1)} %get-tuple-element.36), channel_id=1, source_target_pairs={{0,8},{1,9},{2,10},{3,11},{4,12},{5,13},{6,14},{7,15},{8,0},{9,1},... | collective-permute-start | bytes 294920 | tf_op jit(solution)/shard_map/ppermute | solution.py:636
  5.0 9.8 %collective-permute-start.3 = (f32[24,8,128]{2,1,0:T(8,128)S(1)}, f32[24,8,128]{2,1,0:T(8,128)S(1)}, u32[]{:S(2)}, u32[]{:S(2)}) collective-permute-start(f32[24,8,128]{2,1,0:T(8,128)S(1)} %get-tuple-element.37), channel_id=1, source_target_pairs={{0,1},{1,0},{2,3},{3,2},{4,5},{5,4},{6,7},{7,6},{8,16},{9,17},{10,... | collective-permute-start | bytes 294920 | tf_op jit(solution)/shard_map/ppermute | solution.py:636
  8.9 5.9 %collective-permute-start.4 = (f32[8,128]{1,0:T(8,128)S(1)}, f32[8,128]{1,0:T(8,128)S(1)}, u32[]{:S(2)}, u32[]{:S(2)}) collective-permute-start(f32[8,128]{1,0:T(8,128)S(1)} %get-tuple-element.38), channel_id=1, source_target_pairs={{0,1},{1,0},{2,3},{3,2},{4,5},{5,4},{6,7},{7,6},{8,16},{9,17},{10,... | collective-permute-start | bytes 12296 | tf_op jit(solution)/shard_map/ppermute | solution.py:636
  9.5 5.4 %collective-permute-start.5 = (f32[8,128]{1,0:T(8,128)S(1)}, f32[8,128]{1,0:T(8,128)S(1)}, u32[]{:S(2)}, u32[]{:S(2)}) collective-permute-start(f32[8,128]{1,0:T(8,128)S(1)} %get-tuple-element.39), channel_id=1, source_target_pairs={{0,8},{1,9},{2,10},{3,11},{4,12},{5,13},{6,14},{7,15},{8,0},{9,1},... | collective-permute-start | bytes 12296 | tf_op jit(solution)/shard_map/ppermute | solution.py:636
  15.4 5.5 %collective-permute-start.6 = (f32[24,384]{1,0:T(8,128)S(1)}, f32[24,384]{1,0:T(8,128)S(1)}, u32[]{:S(2)}, u32[]{:S(2)}) collective-permute-start(f32[24,384]{1,0:T(8,128)S(1)} %get-tuple-element.40), channel_id=1, source_target_pairs={{0,128},{128,0},{1,129},{129,1},{2,130},{130,2},{3,131},{131,3},{4... | collective-permute-start | bytes 110600 | tf_op jit(solution)/shard_map/ppermute | solution.py:678
  17.0 4.0 %copy-start = (s32[16,256]{1,0:T(8,128)S(1)}, s32[16,256]{1,0:T(8,128)}, u32[]{:S(2)}) copy-start(s32[16,256]{1,0:T(8,128)} %contacts.3) | copy-start | bytes 49156
